TPU v7x, 32 devices: a whole 2x2x4 slice. The times are simulated.
32 devices in a mesh: group: 2 (over x), chan: 16 (over z, y, core).
Axes of the slice: x: 2, y: 2, z: 4, core: 2. Of those that a mesh axis runs over, the one named last changes fastest.
Arguments:
- records: bfloat16 [4, 4096, 2048], P(None, ('group', 'chan')), parts along dimension 1, may hold values from -6 to 6
- dead: int32 [4096], P(('group', 'chan')), parts along dimension 0, may hold values 0 or 1
- glitch: int32 [4, 4096], P(None, ('group', 'chan')), parts along dimension 1, may hold values 0 or 1
- pairs: int32 [512, 2], P(('group', 'chan')), parts along dimension 0, may hold values from -1 to 15, as said below
Outputs:
- stacks: float32 [512, 128, 512], P(('group', 'chan')), parts along dimension 0
There are 2 independent parts, one for each index of `group`. A program takes and returns all parts, laid end to end along the dimension named above; each array names one. Nothing has to cross between parts.
Inputs may be any that keep to these rules, and one draw needn't show every extreme that they name: `pairs`: per row both entries are -1 or both are blocks of the fibre within 4 blocks of the row's owner block; each owner's first slot is filled, and distance 4 is reached.
All inputs are finite; a program needn't handle non-finite values. No bound on the sum of `dead` or of `glitch` on one device may be relied on, other than what follows from the above.
Results may differ from a plain program's by a relative error of at most 0.0042.
Values may be sent and summed in bfloat16 or wider, within the bound.
No kernel may reach another device: no remote copies, remote signals or barrier semaphores. Data moves between devices by JAX's collectives and lax.ppermute only.
A program may use at most 128 MiB of HBM per device.

v0:
```python
import math

import jax
import jax.numpy as jnp
from jax import lax
from jax.sharding import PartitionSpec as P

LAGS = 512
REACH = 4


def passed_along(value, axis, steps):
    count = lax.axis_size(axis)
    leading, last = (max(0, -steps), min(count, count - steps))
    return lax.ppermute(value, axis, [(source, source + steps) for source in range(leading, last)])


def make_basis(width, bins):
    rows = jnp.arange(width, dtype=jnp.int32)[:, None]
    cols = jnp.arange(bins, dtype=jnp.int32)[None, :] + 1
    phase = (rows * cols % width).astype(jnp.float32) * (2.0 * math.pi / width)
    hann = 0.5 - 0.5 * jnp.cos(
        jnp.arange(width, dtype=jnp.int32).astype(jnp.float32) * (2.0 * math.pi / width)
    )
    return jnp.concatenate(
        [hann[:, None] * jnp.cos(phase), -hann[:, None] * jnp.sin(phase)], 1
    ).astype(jnp.bfloat16)


def make_lagmap(width, bins, lags):
    rows = jnp.arange(bins, dtype=jnp.int32)[:, None] + 1
    cols = jnp.arange(lags, dtype=jnp.int32)[None, :] - lags // 2 + width
    phase = (rows * cols % width).astype(jnp.float32) * (2.0 * math.pi / width)
    scale = 2.0 / math.sqrt(bins)
    return jnp.concatenate([scale * jnp.cos(phase), -scale * jnp.sin(phase)], 0).astype(
        jnp.bfloat16
    )


def whiten(spectra, live, bins):
    real_part = spectra[..., :bins]
    imag_part = spectra[..., bins:]
    amp = jnp.sqrt(real_part * real_part + imag_part * imag_part)
    level = jnp.mean(amp, axis=-1, keepdims=True) + 1e-06
    factor = live[..., None] / (amp + level)
    return jnp.concatenate([real_part * factor, imag_part * factor], -1).astype(jnp.bfloat16)


def cross_pair(left, right, left_live, right_live, bins):
    left = left.astype(jnp.float32)
    right = right.astype(jnp.float32)
    a_re, a_im = (left[..., :bins], left[..., bins:])
    b_re, b_im = (right[..., :bins], right[..., bins:])
    cross_re = jnp.sum(a_re * b_re + a_im * b_im, axis=0)
    cross_im = jnp.sum(a_re * b_im - a_im * b_re, axis=0)
    count = jnp.sum(left_live * right_live, axis=0)
    scale = 1.0 / jnp.maximum(count, 1.0)
    return (jnp.concatenate([cross_re, cross_im], -1) * scale[:, None]).astype(jnp.bfloat16)


def fetch_runs(white, live_wire, sign):
    run_white = white[None]
    run_live = live_wire[None]
    have = 1
    while have < REACH + 1:
        take = min(have, REACH + 1 - have)
        got_white, got_live = passed_along(
            (run_white[:take], run_live[:take]), "chan", -sign * have
        )
        run_white = jnp.concatenate([run_white, got_white], 0)
        run_live = jnp.concatenate([run_live, got_live], 0)
        have = have + take
    return (run_white, run_live)


def body(records, dead, glitch, pairs):
    windows, block, width = records.shape
    bins = width // 2
    here = lax.axis_index("chan")
    basis = make_basis(width, bins)
    spectra = jnp.dot(
        records.reshape(windows * block, width), basis, preferred_element_type=jnp.float32
    )
    spectra = spectra.reshape(windows, block, 2 * bins)
    live = dead[None, :].astype(jnp.float32) * glitch.astype(jnp.float32)
    white = whiten(spectra, live, bins)
    live_wire = live.astype(jnp.bfloat16)
    ahead_white, ahead_live = fetch_runs(white, live_wire, 1)
    behind_white, behind_live = fetch_runs(white, live_wire, -1)
    near_white = jnp.concatenate([behind_white[::-1], ahead_white[1:]], 0)
    near_live = jnp.concatenate([behind_live[::-1], ahead_live[1:]], 0)
    lagmap = make_lagmap(width, bins, LAGS)

    def one_slot(row):
        first, second = (row[0], row[1])
        valid = (first >= 0) & (second >= 0)
        place_a = jnp.clip(first - here + REACH, 0, 2 * REACH)
        place_b = jnp.clip(second - here + REACH, 0, 2 * REACH)
        left = lax.dynamic_index_in_dim(near_white, place_a, 0, keepdims=False)
        right = lax.dynamic_index_in_dim(near_white, place_b, 0, keepdims=False)
        left_live = lax.dynamic_index_in_dim(near_live, place_a, 0, keepdims=False).astype(
            jnp.float32
        )
        right_live = lax.dynamic_index_in_dim(near_live, place_b, 0, keepdims=False).astype(
            jnp.float32
        )
        cross = cross_pair(left, right, left_live, right_live, bins)
        return jnp.where(valid, cross, jnp.zeros_like(cross))

    crosses = lax.map(one_slot, pairs)
    slots = crosses.shape[0]
    stacked = jnp.dot(
        crosses.reshape(slots * block, 2 * bins), lagmap, preferred_element_type=jnp.float32
    )
    return stacked.reshape(slots, block, LAGS)


def solution(mesh):
    placed = (
        P(None, ("group", "chan"), None),
        P(("group", "chan")),
        P(None, ("group", "chan")),
        P(("group", "chan"), None),
    )
    return jax.shard_map(
        body,
        mesh=mesh,
        in_specs=placed,
        out_specs=P(("group", "chan"), None, None),
        check_vma=False,
    )
```

profile of v0, /device:TPU:11, one launch (start us, length us, event | category | flops | bytes accessed | tf_op | source)
XLA Modules:
  0.0 488.0 jit_solution(9288398573543241275)
XLA Ops:
  0.1 34.5 %multiply_convert_fusion.1 = (bf16[2048,1024]{1,0:T(8,128)(2,1)S(1)}, bf16[2048,1024]{1,0:T(8,128)(2,1)S(1)}) fusion(s32[1024]{0:T(1024)S(1)} %iota_add_fusion, f32[2048]{0:T(1024)S(1)} %get-tuple-element.68, f32[2048]{0:T(1024)S(1)} %get-tuple-element.69), kind=kLoop, calls=%fused_computation.26 | loop fusion | flops 37748736 | bytes 8409088 | tf_op jit(solution)/shard_map/convert.8
  34.6 4.6 fusion.6
  40.1 1.1 fusion.19
  41.2 1.6 pad_maximum_fusion.5
  42.8 3.7 collective-permute-start
  46.5 1.9 collective-permute-start.3
  48.4 43.8 %collective-permute-done = bf16[1,4,128,2048]{3,2,1,0:T(8,128)(2,1)S(1)} collective-permute-done((bf16[1,4,128,2048]{3,2,1,0:T(8,128)(2,1)}, bf16[1,4,128,2048]{3,2,1,0:T(8,128)(2,1)S(1)}, u32[]{:S(2)}, u32[]{:S(2)}) %collective-permute-start) | collective-permute-done | bytes 2097184 | tf_op jit(solution)/shard_map/ppermute | solution.py:15
  92.2 1.5 collective-permute-done.3
  93.7 4.0 pad_maximum_fusion.2
  97.7 1.9 collective-permute-start.1
  99.6 4.3 collective-permute-start.4
  103.9 3.2 collective-permute-start.2
  107.1 3.4 collective-permute-start.5
  110.5 3.6 collective-permute-start.6
  114.1 164.0 %collective-permute-done.6 = bf16[1,4,128]{2,1,0:T(4,128)(2,1)S(1)} collective-permute-done((bf16[1,4,128]{2,1,0:T(4,128)(2,1)S(1)}, bf16[1,4,128]{2,1,0:T(4,128)(2,1)S(1)}, u32[]{:S(2)}, u32[]{:S(2)}) %collective-permute-start.6) | collective-permute-done | bytes 1056 | tf_op jit(solution)/shard_map/ppermute | solution.py:15
  278.1 1.9 collective-permute-start.9
  280.0 3.6 collective-permute-done.9
  283.6 3.2 collective-permute-start.8
  287.9 1.9 collective-permute-start.11
  289.9 2.4 collective-permute-done.11
  292.2 1.9 collective-permute-start.7
  294.2 9.9 %multiply_convert_fusion.3 = (bf16[1024,512]{1,0:T(8,128)(2,1)S(1)}, bf16[1024,512]{1,0:T(8,128)(2,1)}) fusion(s32[512]{0:T(512)S(1)} %iota_add_fusion.1, s32[1024]{0:T(1024)S(1)} %iota_add_fusion), kind=kLoop, calls=%fused_computation.47 | loop fusion | flops 9437184 | bytes 2103296 | tf_op jit(solution)/shard_map/convert.2
  304.0 4.4 collective-permute-start.10
  309.4 7.8 %pad_maximum_fusion.1 = bf16[5,4,128,2048]{3,2,1,0:T(8,128)(2,1)} fusion(bf16[1,4,128,2048]{3,2,1,0:T(8,128)(2,1)} %collective-permute-done.2, bf16[2,4,128,2048]{3,2,1,0:T(8,128)(2,1)} %collective-permute-done.1, bf16[1,4,128,2048]{3,2,1,0:T(8,128)(2,1)} %copy-done.4, bf16[1,4,128,1024]{3,2,1,0:T(8,128)(2,1)S(1)} %get-tuple-element.59, ...), kind=kLoop, calls=%fused_computation.17 | loop fusion | flops 52428800 | bytes 20971520 | tf_op jit(solution)/shard_map/concatenate | solution.py:70
  317.2 10.2 %rev.6 = bf16[5,4,128,2048]{3,2,1,0:T(8,128)(2,1)} reverse(bf16[5,4,128,2048]{3,2,1,0:T(8,128)(2,1)} %pad_maximum_fusion.1), dimensions={0} | reverse | bytes 20971520 | tf_op jit(solution)/shard_map/rev | solution.py:90
  327.4 14.7 %pad_maximum_fusion = bf16[9,4,128,2048]{3,2,1,0:T(8,128)(2,1)} fusion(bf16[1,4,128,2048]{3,2,1,0:T(8,128)(2,1)} %collective-permute-done.5, bf16[2,4,128,2048]{3,2,1,0:T(8,128)(2,1)} %collective-permute-done.4, bf16[1,4,128,2048]{3,2,1,0:T(8,128)(2,1)S(1)} %copy-done.3, bf16[5,4,128,2048]{3,2,1,0:T(8,128)(2,1)} %rev.6), kind=kLoop, calls=%fused_computation.13 | loop fusion | flops 28311552 | bytes 37748736 | tf_op jit(solution)/shard_map/concatenate | solution.py:90
  342.1 135.5 %while.10 = (s32[]{:T(128)}, bf16[16,128,2048]{2,1,0:T(8,128)(2,1)}, s32[16,2]{0,1:T(2,128)S(1)}, s32[]{:T(128)}, bf16[9,4,128,2048]{3,2,1,0:T(8,128)(2,1)}, /*i...) while((s32[]{:T(128)}, bf16[16,128,2048]{2,1,0:T(8,128)(2,1)}, ...), condition=%wide.region_5.6_spmd, body=%wide.region_1.5_spmd.sunk | while | flops 7080077 | bytes 23597836 | solution.py:110
  344.0 3.3 bitcast_convert_fusion.3
  347.3 1.1 add_reduce_fusion.2
  352.5 3.3 bitcast_convert_fusion.3
  360.9 3.3 bitcast_convert_fusion.3
  369.4 3.3 bitcast_convert_fusion.3
  372.7 1.1 add_reduce_fusion.2
  377.9 3.3 bitcast_convert_fusion.3
  386.3 3.3 bitcast_convert_fusion.3
  389.6 1.1 add_reduce_fusion.2
  394.8 3.3 bitcast_convert_fusion.3
  403.3 3.3 bitcast_convert_fusion.3
  406.6 1.1 add_reduce_fusion.2
  411.8 3.3 bitcast_convert_fusion.3
  420.2 3.3 bitcast_convert_fusion.3
  428.7 3.3 bitcast_convert_fusion.3
  437.2 3.3 bitcast_convert_fusion.3
  445.6 3.3 bitcast_convert_fusion.3
  454.1 3.3 bitcast_convert_fusion.3
  462.5 3.3 bitcast_convert_fusion.3
  471.0 3.3 bitcast_convert_fusion.3
  477.7 10.3 %fusion.16 = f32[16,128,512]{2,1,0:T(8,128)} fusion(bf16[16,128,2048]{2,1,0:T(8,128)(2,1)} %get-tuple-element.37, bf16[1024,512]{1,0:T(8,128)(2,1)} %get-tuple-element.63, bf16[1024,512]{1,0:T(8,128)(2,1)S(1)} %get-tuple-element.62), kind=kOutput, calls=%fused_computation.43 | convolution fusion | flops 4299161600 | bytes 14680064 | tf_op jit(solution)/shard_map/dot_general | solution.py:112
  (127 shorter events, 41.7 us)
Async XLA Ops:
  0.0 34.6 %copy-start = (bf16[4,128,2048]{2,1,0:T(8,128)(2,1)S(1)}, bf16[4,128,2048]{2,1,0:T(8,128)(2,1)}, u32[]{:S(2)}) copy-start(bf16[4,128,2048]{2,1,0:T(8,128)(2,1)} %param.6) | copy-start | bytes 6291460
  39.2 0.9 copy-start.7
  39.2 0.9 copy-start.6
  42.8 49.4 %collective-permute-start = (bf16[1,4,128,2048]{3,2,1,0:T(8,128)(2,1)}, bf16[1,4,128,2048]{3,2,1,0:T(8,128)(2,1)S(1)}, u32[]{:S(2)}, u32[]{:S(2)}) collective-permute-start(bf16[1,4,128,2048]{3,2,1,0:T(8,128)(2,1)} %pad_maximum_fusion.5), channel_id=1, source_target_pairs={{0,1},{1,2},{2,3},{3,4},{4,5},{5,6},{6,7},{7,8},{8,9},{9,10},{10,1... | collective-permute-start | bytes 6291464 | tf_op jit(solution)/shard_map/ppermute | solution.py:15
  46.5 47.2 %collective-permute-start.3 = (bf16[1,4,128,2048]{3,2,1,0:T(8,128)(2,1)}, bf16[1,4,128,2048]{3,2,1,0:T(8,128)(2,1)S(1)}, u32[]{:S(2)}, u32[]{:S(2)}) collective-permute-start(bf16[1,4,128,2048]{3,2,1,0:T(8,128)(2,1)} %pad_maximum_fusion.5), channel_id=1, source_target_pairs={{1,0},{2,1},{3,2},{4,3},{5,4},{6,5},{7,6},{8,7},{9,8},{10,9},{11,1... | collective-permute-start | bytes 6291464 | tf_op jit(solution)/shard_map/ppermute | solution.py:15
  92.2 5.5 %copy-start.4 = (bf16[1,4,128,2048]{3,2,1,0:T(8,128)(2,1)}, bf16[1,4,128,2048]{3,2,1,0:T(8,128)(2,1)S(1)}, u32[]{:S(2)}) copy-start(bf16[1,4,128,2048]{3,2,1,0:T(8,128)(2,1)S(1)} %collective-permute-done) | copy-start | bytes 6291460
  93.7 4.0 copy-start.2
  97.7 211.7 %collective-permute-start.1 = (bf16[2,4,128,2048]{3,2,1,0:T(8,128)(2,1)}, bf16[2,4,128,2048]{3,2,1,0:T(8,128)(2,1)}, u32[]{:S(2)}, u32[]{:S(2)}) collective-permute-start(bf16[2,4,128,2048]{3,2,1,0:T(8,128)(2,1)} %get-tuple-element.60), channel_id=1, source_target_pairs={{0,2},{1,3},{2,4},{3,5},{4,6},{5,7},{6,8},{7,9},{8,10},{9,11},{10,... | collective-permute-start | bytes 12582920 | tf_op jit(solution)/shard_map/ppermute | solution.py:15
  99.6 227.8 %collective-permute-start.4 = (bf16[2,4,128,2048]{3,2,1,0:T(8,128)(2,1)}, bf16[2,4,128,2048]{3,2,1,0:T(8,128)(2,1)}, u32[]{:S(2)}, u32[]{:S(2)}) collective-permute-start(bf16[2,4,128,2048]{3,2,1,0:T(8,128)(2,1)} %get-tuple-element.61), channel_id=1, source_target_pairs={{2,0},{3,1},{4,2},{5,3},{6,4},{7,5},{8,6},{9,7},{10,8},{11,9},{12,... | collective-permute-start | bytes 12582920 | tf_op jit(solution)/shard_map/ppermute | solution.py:15
  103.9 205.5 %collective-permute-start.2 = (bf16[1,4,128,2048]{3,2,1,0:T(8,128)(2,1)}, bf16[1,4,128,2048]{3,2,1,0:T(8,128)(2,1)}, u32[]{:S(2)}, u32[]{:S(2)}) collective-permute-start(bf16[1,4,128,2048]{3,2,1,0:T(8,128)(2,1)} %pad_maximum_fusion.5), channel_id=1, source_target_pairs={{0,4},{1,5},{2,6},{3,7},{4,8},{5,9},{6,10},{7,11},{8,12},{9,13},{1... | collective-permute-start | bytes 6291464 | tf_op jit(solution)/shard_map/ppermute | solution.py:15
  107.1 220.3 %collective-permute-start.5 = (bf16[1,4,128,2048]{3,2,1,0:T(8,128)(2,1)}, bf16[1,4,128,2048]{3,2,1,0:T(8,128)(2,1)}, u32[]{:S(2)}, u32[]{:S(2)}) collective-permute-start(bf16[1,4,128,2048]{3,2,1,0:T(8,128)(2,1)} %pad_maximum_fusion.5), channel_id=1, source_target_pairs={{4,0},{5,1},{6,2},{7,3},{8,4},{9,5},{10,6},{11,7},{12,8},{13,9},{1... | collective-permute-start | bytes 6291464 | tf_op jit(solution)/shard_map/ppermute | solution.py:15
  110.5 167.6 %collective-permute-start.6 = (bf16[1,4,128]{2,1,0:T(4,128)(2,1)S(1)}, bf16[1,4,128]{2,1,0:T(4,128)(2,1)S(1)}, u32[]{:S(2)}, u32[]{:S(2)}) collective-permute-start(bf16[1,4,128]{2,1,0:T(4,128)(2,1)S(1)} %get-tuple-element.52), channel_id=1, source_target_pairs={{0,1},{1,2},{2,3},{3,4},{4,5},{5,6},{6,7},{7,8},{8,9},{9,10},{10,1... | collective-permute-start | bytes 3080 | tf_op jit(solution)/shard_map/ppermute | solution.py:15
  278.1 5.5 %collective-permute-start.9 = (bf16[1,4,128]{2,1,0:T(4,128)(2,1)S(1)}, bf16[1,4,128]{2,1,0:T(4,128)(2,1)S(1)}, u32[]{:S(2)}, u32[]{:S(2)}) collective-permute-start(bf16[1,4,128]{2,1,0:T(4,128)(2,1)S(1)} %get-tuple-element.52), channel_id=1, source_target_pairs={{1,0},{2,1},{3,2},{4,3},{5,4},{6,5},{7,6},{8,7},{9,8},{10,9},{11,1... | collective-permute-start | bytes 3080 | tf_op jit(solution)/shard_map/ppermute | solution.py:15
  283.6 4.3 collective-permute-start.8
  287.9 4.3 collective-permute-start.11
  292.2 11.8 %collective-permute-start.7 = (bf16[2,4,128]{2,1,0:T(4,128)(2,1)S(1)}, bf16[2,4,128]{2,1,0:T(4,128)(2,1)S(1)}, u32[]{:S(2)}, u32[]{:S(2)}) collective-permute-start(bf16[2,4,128]{2,1,0:T(4,128)(2,1)S(1)} %get-tuple-element.66), channel_id=1, source_target_pairs={{0,2},{1,3},{2,4},{3,5},{4,6},{5,7},{6,8},{7,9},{8,10},{9,11},{10,... | collective-permute-start | bytes 6152 | tf_op jit(solution)/shard_map/ppermute | solution.py:15
  304.0 5.3 %collective-permute-start.10 = (bf16[2,4,128]{2,1,0:T(4,128)(2,1)S(1)}, bf16[2,4,128]{2,1,0:T(4,128)(2,1)S(1)}, u32[]{:S(2)}, u32[]{:S(2)}) collective-permute-start(bf16[2,4,128]{2,1,0:T(4,128)(2,1)S(1)} %get-tuple-element.67), channel_id=1, source_target_pairs={{2,0},{3,1},{4,2},{5,3},{6,4},{7,5},{8,6},{9,7},{10,8},{11,9},{12,... | collective-permute-start | bytes 6152 | tf_op jit(solution)/shard_map/ppermute | solution.py:15
  317.2 10.2 %copy-start.3 = (bf16[1,4,128,2048]{3,2,1,0:T(8,128)(2,1)S(1)}, bf16[1,4,128,2048]{3,2,1,0:T(8,128)(2,1)}, u32[]{:S(2)}) copy-start(bf16[1,4,128,2048]{3,2,1,0:T(8,128)(2,1)} %copy-done.2) | copy-start | bytes 6291460
  327.4 14.8 %copy-start.5 = (s32[16,2]{0,1:T(2,128)S(1)}, s32[16,2]{0,1:T(2,128)}, u32[]{:S(2)}) copy-start(s32[16,2]{0,1:T(2,128)} %param.9) | copy-start | bytes 388
  477.7 10.3 %copy-start.1 = (bf16[4,128,2048]{2,1,0:T(8,128)(2,1)S(1)}, bf16[4,128,2048]{2,1,0:T(8,128)(2,1)}, u32[]{:S(2)}) copy-start(bf16[4,128,2048]{2,1,0:T(8,128)(2,1)} %param.6) | copy-start | bytes 6291460
where the time goes:
time: 492 us; the launch traced here: 488 us
  waiting for transfers between devices  217 us (44%)
  other arithmetic  161 us (33%)
  loops' own time  39.6 us (8%)
  starting transfers between devices  35.4 us (7%)
  local copies, waits for them, and re-layouts  19.7 us (4%)
  matrix products  14.9 us (3%)
    ppermute x12, waiting for transfers between devices, passed_along(): lax.ppermute(value, axis, [(source, source + steps) for source in range(l...  217 us
    convert_element_type x16, other arithmetic, cross_pair(): left = left.astype(jnp.float32)  52.7 us
    another operation x2, other arithmetic  44.4 us
    another operation x1, loops' own time, body(): crosses = lax.map(one_slot, pairs)  39.6 us
    ppermute x12, starting transfers between devices, passed_along(): lax.ppermute(value, axis, [(source, source + steps) for source in range(l...  35.4 us
    reduce_sum x16, other arithmetic, cross_pair(): cross_re = jnp.sum(a_re * b_re + a_im * b_im, axis=0)  17.7 us
    dynamic_update_slice x16, other arithmetic, body(): crosses = lax.map(one_slot, pairs)  15.5 us
    concatenate x1, other arithmetic, body(): near_white = jnp.concatenate([behind_white[::-1], ahead_white[1:]], 0)  14.7 us
  transfers between devices with their start and end apart: 12, of which 7 were waited for; matrix products, arithmetic and copies ran while one was open for 6% of the time, Pallas kernels for 0%

commit v1 on v0

v1 whole, which is shorter than its diff:
```python
import functools
import math

import jax
import jax.numpy as jnp
import numpy as np
from jax import lax
from jax.experimental import pallas as pl
from jax.experimental.pallas import tpu as pltpu
from jax.sharding import PartitionSpec as P

LAGS = 512
QUAD = 4
CHUNKS = (8, 8, 8, 8)


def make_basis(width, bins):
    rows = np.arange(width, dtype=np.int64)[:, None]
    cols = np.arange(bins, dtype=np.int64)[None, :] + 1
    phase = (rows * cols % width) * (2.0 * math.pi / width)
    hann = 0.5 - 0.5 * np.cos(np.arange(width) * (2.0 * math.pi / width))
    table = np.concatenate([hann[:, None] * np.cos(phase), -hann[:, None] * np.sin(phase)], 1)
    return table.astype(np.float32).astype(jnp.bfloat16)


def make_lagmap(width, bins, lags):
    rows = np.arange(bins, dtype=np.int64)[:, None] + 1
    cols = np.arange(lags, dtype=np.int64)[None, :] - lags // 2 + width
    phase = (rows * cols % width) * (2.0 * math.pi / width)
    scale = 2.0 / math.sqrt(bins)
    table = np.concatenate([scale * np.cos(phase), -scale * np.sin(phase)], 0)
    return table.astype(np.float32).astype(jnp.bfloat16)


def to_quad_peer(value, mask):
    count = lax.axis_size("chan")
    return lax.ppermute(value, "chan", [(s, s ^ mask) for s in range(count)])


def to_next_quad(value, steps):
    count = lax.axis_size("chan")
    first, last = max(0, -steps), min(count, count - steps)
    return lax.ppermute(value, "chan", [(s, s + steps) for s in range(first, last)])


def whiten_kernel(x0, x1, x2, x3, live, basis, out, rows, re_s, im_s, amp_s):
    part = x0.shape[0]
    bins = basis.shape[1] // 2
    for m, x in enumerate((x0, x1, x2, x3)):
        rows[pl.ds(m * part, part), :] = x[...]
    step = 256
    total = jnp.zeros((QUAD * part, 128), jnp.float32)
    for j in range(0, bins, step):
        re = jnp.dot(rows[...], basis[:, j : j + step], preferred_element_type=jnp.float32)
        im = jnp.dot(
            rows[...], basis[:, bins + j : bins + j + step], preferred_element_type=jnp.float32
        )
        amp = jnp.sqrt(re * re + im * im)
        re_s[:, j : j + step] = re
        im_s[:, j : j + step] = im
        amp_s[:, j : j + step] = amp
        for i in range(0, step, 128):
            total = total + amp[:, i : i + 128]
    level = jnp.sum(total, axis=-1, keepdims=True) * (1.0 / bins) + 1e-06
    flag = live[:, 0:1]
    for j in range(0, bins, step):
        factor = flag / (amp_s[:, j : j + step] + level)
        out[:, j : j + step] = (re_s[:, j : j + step] * factor).astype(jnp.bfloat16)
        out[:, bins + j : bins + j + step] = (im_s[:, j : j + step] * factor).astype(jnp.bfloat16)


def whiten(parts, live, basis):
    part, width = parts[0].shape
    total = QUAD * part
    bins = width // 2
    return pl.pallas_call(
        whiten_kernel,
        out_shape=jax.ShapeDtypeStruct((total, width), jnp.bfloat16),
        in_specs=[pl.BlockSpec(memory_space=pltpu.VMEM)] * 6,
        out_specs=pl.BlockSpec(memory_space=pltpu.VMEM),
        scratch_shapes=[
            pltpu.VMEM((total, width), jnp.bfloat16),
            pltpu.VMEM((total, bins), jnp.float32),
            pltpu.VMEM((total, bins), jnp.float32),
            pltpu.VMEM((total, bins), jnp.float32),
        ],
        compiler_params=pltpu.CompilerParams(vmem_limit_bytes=24 << 20),
        cost_estimate=pl.CostEstimate(
            flops=2 * total * width * width, bytes_accessed=8 << 20, transcendentals=0
        ),
        name="whiten",
    )(*parts, live, basis)


def cross_kernel(windows, place, valid, behind, mine, ahead, live, lagmap, out, near, cross):
    rows, width = behind.shape
    bins = width // 2
    chans = rows // (QUAD * windows)
    for i, block in enumerate((behind, mine, ahead)):
        near[pl.ds(i * rows, rows), :] = block[...].astype(jnp.float32)
    span = windows * chans
    pairs = place.shape[0]

    def one(p):
        a = pl.multiple_of(place[p, 0] * span, span)
        b = pl.multiple_of(place[p, 1] * span, span)
        count = jnp.zeros((chans, 128), jnp.float32)
        for w in range(windows):
            count = count + live[pl.ds(a + w * chans, chans), :] * live[pl.ds(b + w * chans, chans), :]
        scale = valid[p] * (1.0 / jnp.maximum(count, 1.0))
        res, ims = [], []
        for j in range(0, bins, 128):
            re = jnp.zeros((chans, 128), jnp.float32)
            im = jnp.zeros((chans, 128), jnp.float32)
            for w in range(windows):
                ra = near[pl.ds(a + w * chans, chans), pl.ds(j, 128)]
                ia = near[pl.ds(a + w * chans, chans), pl.ds(bins + j, 128)]
                rb = near[pl.ds(b + w * chans, chans), pl.ds(j, 128)]
                ib = near[pl.ds(b + w * chans, chans), pl.ds(bins + j, 128)]
                re = re + (ra * rb + ia * ib)
                im = im + (ra * ib - ia * rb)
            res.append(re * scale)
            ims.append(im * scale)
        return res + ims

    def two(h, carry):
        first = one(2 * h)
        second = one(2 * h + 1)
        for j, (u, v) in enumerate(zip(first, second)):
            cross[pl.ds(pl.multiple_of(2 * h * chans, 2 * chans), 2 * chans), pl.ds(j * 128, 128)] = (
                jnp.concatenate([u, v], 0).astype(jnp.bfloat16)
            )
        return carry

    lax.fori_loop(0, pairs // 2, two, 0)
    out[...] = jnp.dot(cross[...], lagmap[...], preferred_element_type=jnp.float32).astype(
        jnp.bfloat16
    )


def cross_stack(windows, place, valid, behind, mine, ahead, live, lagmap):
    rows, width = mine.shape
    chans = rows // (QUAD * windows)
    pairs = place.shape[0]

    smem = pl.BlockSpec(memory_space=pltpu.SMEM)
    vmem = pl.BlockSpec(memory_space=pltpu.VMEM)
    return pl.pallas_call(
        functools.partial(cross_kernel, windows),
        out_shape=jax.ShapeDtypeStruct((pairs * chans, LAGS), jnp.bfloat16),
        in_specs=[smem, smem] + [vmem] * 5,
        out_specs=vmem,
        scratch_shapes=[
            pltpu.VMEM((3 * rows, width), jnp.float32),
            pltpu.VMEM((pairs * chans, width), jnp.bfloat16),
        ],
        compiler_params=pltpu.CompilerParams(vmem_limit_bytes=24 << 20),
        cost_estimate=pl.CostEstimate(
            flops=2 * pairs * chans * width * LAGS * 3, bytes_accessed=8 << 20, transcendentals=0
        ),
        name="cross_stack",
    )(place, valid, behind, mine, ahead, live, lagmap)


def place_kernel(chans, slot, r0, r1, r2, r3, *refs):
    out = refs[-1]
    for m, r in enumerate((r0, r1, r2, r3)):
        at = pl.multiple_of(slot[m] * chans, chans)
        for p in range(out.shape[0]):
            out[p, pl.ds(at, chans), :] = r[pl.ds(p * chans, chans), :].astype(jnp.float32)


def place_stacks(chunk, chans, slot, parts, held, shape):

    smem = pl.BlockSpec(memory_space=pltpu.SMEM)
    extra = [] if held is None else [held]
    pairs = shape[0]
    full = lambda i: (0, 0)
    return pl.pallas_call(
        functools.partial(place_kernel, chans),
        out_shape=jax.ShapeDtypeStruct(shape, jnp.float32),
        grid=(1,),
        in_specs=[smem]
        + [pl.BlockSpec((pairs * chans, LAGS), full)] * 4
        + [pl.BlockSpec(memory_space=pl.ANY)] * len(extra),
        out_specs=pl.BlockSpec((pairs, QUAD * chans, LAGS), lambda i: (0, chunk, 0)),
        input_output_aliases={5: 0} if extra else {},
        compiler_params=pltpu.CompilerParams(vmem_limit_bytes=16 << 20),
        cost_estimate=pl.CostEstimate(flops=0, bytes_accessed=2 << 20, transcendentals=0),
        name="place_stacks",
    )(slot, *parts, *extra)


def body(records, dead, glitch, pairs):
    windows, block, width = records.shape
    bins = width // 2
    here = lax.axis_index("chan")
    mine = here % QUAD
    quad = here // QUAD
    basis = jnp.asarray(make_basis(width, bins))
    lagmap = jnp.asarray(make_lagmap(width, bins, LAGS))
    order = [mine ^ m for m in range(QUAD)]

    live = dead[None, :] * glitch
    notes = jnp.concatenate([live.reshape(-1), pairs.reshape(-1)])
    notes = lax.all_gather(notes, "chan")
    all_live = notes[:, : windows * block].reshape(-1, windows, block)
    all_pairs = notes[:, windows * block :].reshape(-1, pairs.shape[0], 2)
    near_live = lax.dynamic_slice_in_dim(
        jnp.pad(all_live, ((QUAD, QUAD), (0, 0), (0, 0))), quad * QUAD, 3 * QUAD, 0
    ).astype(jnp.float32)
    near_live = near_live.reshape(3, QUAD, windows, block)
    near_live = jnp.stack([lax.dynamic_index_in_dim(near_live, o, 1, False) for o in order], 1)
    quad_pairs = jnp.stack(
        [lax.dynamic_index_in_dim(all_pairs, quad * QUAD + o, 0, False) for o in order], 0
    ).reshape(-1, 2)
    valid = ((quad_pairs[:, 0] >= 0) & (quad_pairs[:, 1] >= 0)).astype(jnp.float32)
    place = (quad_pairs // QUAD - quad + 1) * QUAD + ((quad_pairs % QUAD) ^ mine)
    place = jnp.where(valid[:, None] > 0, jnp.clip(place, 0, 3 * QUAD - 1), 0)
    slot = jnp.stack(order)

    held = None
    base = 0
    for chunk, chans in enumerate(CHUNKS):
        sent = records[:, base : base + QUAD * chans, :].reshape(windows, QUAD, chans, width)
        parts = []
        for m in range(QUAD):
            piece = lax.dynamic_index_in_dim(sent, order[m], 1, False).reshape(-1, width)
            parts.append(to_quad_peer(piece, m) if m else piece)
        lives = near_live[..., base : base + QUAD * chans].reshape(3, QUAD, windows, QUAD, chans)
        lives = lax.dynamic_index_in_dim(lives, mine, 3, False).reshape(3, -1, 1)
        lives = jnp.broadcast_to(lives, lives.shape[:2] + (128,))
        white = whiten(parts, lives[1], basis)
        behind = to_next_quad(white, QUAD)
        ahead = to_next_quad(white, -QUAD)
        stacks = cross_stack(
            windows, place, valid, behind, white, ahead, lives.reshape(-1, 128), lagmap
        )
        stacks = stacks.reshape(QUAD, -1, LAGS)
        back = [to_quad_peer(stacks[m], m) if m else stacks[m] for m in range(QUAD)]
        held = place_stacks(chunk, chans, slot, back, held, (pairs.shape[0], block, LAGS))
        base = base + QUAD * chans
    return held


def solution(mesh):
    placed = (
        P(None, ("group", "chan"), None),
        P(("group", "chan")),
        P(None, ("group", "chan")),
        P(("group", "chan"), None),
    )
    return jax.shard_map(
        body,
        mesh=mesh,
        in_specs=placed,
        out_specs=P(("group", "chan"), None, None),
        check_vma=False,
    )
```

time: 492 us -> 168 us (0.34)
  waiting for transfers between devices: 217 us -> 12.7 us
  other arithmetic: 161 us -> 1.8 us
  blocking collectives: 0 us -> 49.3 us
  loops' own time: 39.6 us -> 0 us
  Pallas kernels: 0 us -> 38 us
  starting transfers between devices: 35.4 us -> 52.3 us
  matrix products: 14.9 us -> 0 us
  local copies, waits for them, and re-layouts: 19.7 us -> 11.4 us
    ppermute x12 -> x32, waiting for transfers between devices: 217 us -> 12.7 us  [the longest x8 7.78 us: to_next_quad(): lax.ppermute(value, 'chan', [(s, s + steps) for s in range(first, last)])]
    convert_element_type x17 -> x1, other arithmetic: 52.8 us -> 0.03 us  [body(): near_live = lax.dynamic_slice_in_dim(jnp.pad(all_live, ((QUAD, QUAD), (0,...]
    unnamed x0 -> x1, blocking collectives: none -> 49.3 us
    another operation x2 -> x3, other arithmetic: 44.4 us -> 0.81 us  [the longest x1 0.72 us: body(): jnp.stack([lax.dynamic_index_in_dim(near_live, o, 1, False) for o in orde...]
    another operation x1 -> x0, loops' own time: 39.6 us -> none  [body(): crosses = lax.map(one_slot, pairs)]
    pallas_call x0 -> x12, Pallas kernels: none -> 38 us  [the longest x4 25.6 us: cross_stack(): pl.pallas_call(functools.partial(cross_kernel, windows), out_shape=jax.Sh...]
    concatenate x8 -> x0, other arithmetic: 29.2 us -> none  [the longest x1 14.7 us: body(): near_white = jnp.concatenate([behind_white[::-1], ahead_white[1:]], 0)]
    reduce_sum x33 -> x0, other arithmetic: 19 us -> none  [the longest x16 17.7 us: cross_pair(): cross_re = jnp.sum(a_re * b_re + a_im * b_im, axis=0)]
  transfers between devices with their start and end apart: 12 -> 32, of which waited for: 7 -> 8; matrix products, arithmetic and copies ran while one was open for 6% -> 5% of each run, Pallas kernels for 0% -> 22%
where the time goes in v1:
time: 168 us; the launch traced here: 167 us
  starting transfers between devices  52.3 us (31%)
  blocking collectives  49.3 us (29%)
  Pallas kernels  38 us (23%)
  waiting for transfers between devices  12.7 us (8%)
  local copies, waits for them, and re-layouts  11.4 us (7%)
  other arithmetic  1.8 us (1%)
    unnamed x1, blocking collectives  49.3 us
    ppermute x8, starting transfers between devices, to_next_quad(): lax.ppermute(value, 'chan', [(s, s + steps) for s in range(first, last)])  28.2 us
    pallas_call x4, Pallas kernels, cross_stack(): pl.pallas_call(functools.partial(cross_kernel, windows), out_shape=jax.Sh...  25.6 us
    ppermute x24, starting transfers between devices, to_quad_peer(): return lax.ppermute(value, 'chan', [(s, s ^ mask) for s in range(count)])  24.1 us
    ppermute x8, waiting for transfers between devices, to_next_quad(): lax.ppermute(value, 'chan', [(s, s + steps) for s in range(first, last)])  7.78 us
    pallas_call x4, Pallas kernels, place_stacks(): pl.pallas_call(functools.partial(place_kernel, chans), out_shape=jax.Shap...  6.35 us
    pallas_call x4, Pallas kernels, whiten(): pl.pallas_call(whiten_kernel, out_shape=jax.ShapeDtypeStruct((total, widt...  6.04 us
    ppermute x24, waiting for transfers between devices, to_quad_peer(): return lax.ppermute(value, 'chan', [(s, s ^ mask) for s in range(count)])  4.93 us
  transfers between devices with their start and end apart: 32, of which 8 were waited for; matrix products, arithmetic and copies ran while one was open for 5% of the time, Pallas kernels for 22%

profile of v1, /device:TPU:11, one launch (start us, length us, event | category | flops | bytes accessed | tf_op | source)
XLA Modules:
  0.0 166.7 jit_solution(10123414983465978936)
XLA Ops:
  0.1 1.7 %slice_bitcast_fusion = (bf16[4,4,8,2048]{3,2,1,0:T(8,128)(2,1)S(1)}, bf16[4,4,8,2048]{3,2,1,0:T(8,128)(2,1)S(1)}, bf16[4,4,8,2048]{3,2,1,0:T(8,128)(2,1)S(1)}, bf16[4,4,8,2048]{3,2,1,0:T(8,128)(2,1)S(1)}) fusion(bf16[4,128,2048]{2,1,0:T(8,128)(2,1)} %param.6), kind=kLoop, calls=%fused_computation | loop fusion | bytes 4194304 | tf_op jit(solution)/shard_map/reshape | solution.py:225
  1.8 1.9 %collective-permute-start.10 = (bf16[32,2048]{1,0:T(8,128)(2,1)S(1)}, bf16[32,2048]{1,0:T(8,128)(2,1)S(1)}, u32[]{:S(2)}, u32[]{:S(2)}) collective-permute-start(bf16[32,2048]{1,0:T(8,128)(2,1)S(1)} %get-tuple-element.31), channel_id=1, source_target_pairs={{0,3},{1,2},{2,1},{3,0},{4,7},{5,6},{6,5},{7,4},{8,11},{9,10},{10,... | collective-permute-start | bytes 393224 | tf_op jit(solution)/shard_map/ppermute | solution.py:37
  4.2 1.5 collective-permute-start.18
  7.5 49.3 %all-reduce.1 = s32[8704]{0:T(1024)S(1)} all-reduce(s32[8704]{0:T(1024)S(1)} %add_dynamic-update-slice_fusion), channel_id=2, replica_groups=mesh['group'=2,'chan'=16] {'chan'}, use_global_device_ids=true, to_apply=%add.1 | all-reduce | flops 8704 | bytes 69632
  56.9 0.6 constant_dynamic-slice_fusion.6
  58.1 0.7 reshape.190
  58.9 0.7 pad_maximum_fusion
  59.7 5.1 %collective-permute-start.16 = (bf16[32,2048]{1,0:T(8,128)(2,1)S(1)}, bf16[32,2048]{1,0:T(8,128)(2,1)S(1)}, u32[]{:S(2)}, u32[]{:S(2)}) collective-permute-start(bf16[32,2048]{1,0:T(8,128)(2,1)S(1)} %get-tuple-element.25), channel_id=1, source_target_pairs={{0,1},{1,0},{2,3},{3,2},{4,5},{5,4},{6,7},{7,6},{8,9},{9,8},{10,11... | collective-permute-start | bytes 393224 | tf_op jit(solution)/shard_map/ppermute | solution.py:37
  64.8 0.8 compare_bitcast_fusion
  65.6 0.8 copy.83
  68.2 1.3 collective-permute-start.1
  69.6 3.4 %copy-done = bf16[2048,2048]{1,0:T(8,128)(2,1)S(1)} copy-done((bf16[2048,2048]{1,0:T(8,128)(2,1)S(1)}, bf16[2048,2048]{1,0:T(8,128)(2,1)}, u32[]{:S(2)}) %copy-start) | copy-done | bytes 8388632
  73.0 1.5 whiten.6.mine
  74.5 0.9 collective-permute-start
  75.4 10.1 %collective-permute-start.20 = (bf16[128,2048]{1,0:T(8,128)(2,1)S(1)}, bf16[128,2048]{1,0:T(8,128)(2,1)S(1)}, u32[]{:S(2)}, u32[]{:S(2)}) collective-permute-start(bf16[128,2048]{1,0:T(8,128)(2,1)S(1)} %whiten.6.mine), channel_id=1, source_target_pairs={{4,0},{5,1},{6,2},{7,3},{8,4},{9,5},{10,6},{11,7},{12,8},{13,9},{1... | collective-permute-start | bytes 1572872 | tf_op jit(solution)/shard_map/ppermute | solution.py:43
  85.5 1.9 %collective-permute-start.19 = (bf16[128,2048]{1,0:T(8,128)(2,1)S(1)}, bf16[128,2048]{1,0:T(8,128)(2,1)S(1)}, u32[]{:S(2)}, u32[]{:S(2)}) collective-permute-start(bf16[128,2048]{1,0:T(8,128)(2,1)S(1)} %whiten.6.mine), channel_id=1, source_target_pairs={{0,4},{1,5},{2,6},{3,7},{4,8},{5,9},{6,10},{7,11},{8,12},{9,13},{1... | collective-permute-start | bytes 1572872 | tf_op jit(solution)/shard_map/ppermute | solution.py:43
  87.6 1.6 collective-permute-start.25
  89.8 1.5 whiten.5.mine
  91.4 1.5 whiten.4.mine
  92.9 0.6 collective-permute-done.26.x3
  93.6 3.5 %collective-permute-start.4 = (bf16[128,2048]{1,0:T(8,128)(2,1)S(1)}, bf16[128,2048]{1,0:T(8,128)(2,1)S(1)}, u32[]{:S(2)}, u32[]{:S(2)}) collective-permute-start(bf16[128,2048]{1,0:T(8,128)(2,1)S(1)} %whiten.4.mine), channel_id=1, source_target_pairs={{4,0},{5,1},{6,2},{7,3},{8,4},{9,5},{10,6},{11,7},{12,8},{13,9},{1... | collective-permute-start | bytes 1572872 | tf_op jit(solution)/shard_map/ppermute | solution.py:43
  97.0 1.9 %collective-permute-start.3 = (bf16[128,2048]{1,0:T(8,128)(2,1)S(1)}, bf16[128,2048]{1,0:T(8,128)(2,1)S(1)}, u32[]{:S(2)}, u32[]{:S(2)}) collective-permute-start(bf16[128,2048]{1,0:T(8,128)(2,1)S(1)} %whiten.4.mine), channel_id=1, source_target_pairs={{0,4},{1,5},{2,6},{3,7},{4,8},{5,9},{6,10},{7,11},{8,12},{9,13},{1... | collective-permute-start | bytes 1572872 | tf_op jit(solution)/shard_map/ppermute | solution.py:43
  99.0 3.4 %collective-permute-start.12 = (bf16[128,2048]{1,0:T(8,128)(2,1)S(1)}, bf16[128,2048]{1,0:T(8,128)(2,1)S(1)}, u32[]{:S(2)}, u32[]{:S(2)}) collective-permute-start(bf16[128,2048]{1,0:T(8,128)(2,1)S(1)} %whiten.5.mine), channel_id=1, source_target_pairs={{4,0},{5,1},{6,2},{7,3},{8,4},{9,5},{10,6},{11,7},{12,8},{13,9},{1... | collective-permute-start | bytes 1572872 | tf_op jit(solution)/shard_map/ppermute | solution.py:43
  102.5 1.5 whiten.7.mine
  104.0 1.9 %collective-permute-start.11 = (bf16[128,2048]{1,0:T(8,128)(2,1)S(1)}, bf16[128,2048]{1,0:T(8,128)(2,1)S(1)}, u32[]{:S(2)}, u32[]{:S(2)}) collective-permute-start(bf16[128,2048]{1,0:T(8,128)(2,1)S(1)} %whiten.5.mine), channel_id=1, source_target_pairs={{0,4},{1,5},{2,6},{3,7},{4,8},{5,9},{6,10},{7,11},{8,12},{9,13},{1... | collective-permute-start | bytes 1572872 | tf_op jit(solution)/shard_map/ppermute | solution.py:43
  105.9 3.4 %collective-permute-start.28 = (bf16[128,2048]{1,0:T(8,128)(2,1)S(1)}, bf16[128,2048]{1,0:T(8,128)(2,1)S(1)}, u32[]{:S(2)}, u32[]{:S(2)}) collective-permute-start(bf16[128,2048]{1,0:T(8,128)(2,1)S(1)} %whiten.7.mine), channel_id=1, source_target_pairs={{4,0},{5,1},{6,2},{7,3},{8,4},{9,5},{10,6},{11,7},{12,8},{13,9},{1... | collective-permute-start | bytes 1572872 | tf_op jit(solution)/shard_map/ppermute | solution.py:43
  109.5 6.4 %cross_stack.6 = bf16[512,512]{1,0:T(8,128)(2,1)S(1)} custom-call(s32[64,2]{1,0:T(8,128)S(1)} %fusion.5.place, f32[64]{0:T(128)S(1)} %bitcast.88, bf16[128,2048]{1,0:T(8,128)(2,1)S(1)} %collective-permute-done.19.behind, bf16[128,2048]{1,0:T(8,128)(2,1)S(1)} %whiten.6.mine, bf16[128,2048]{1,0:T(8,128)(2,1)S(1)} %collective-permute-done.20.ahead, ...), custom_call_target="tpu_custom_call" | custom-call | flops 3221225472 | bytes 8388608 | tf_op jit(solution)/shard_map/cross_stack/pallas_call | solution.py:148
  115.9 4.4 %collective-permute-done.12.ahead = bf16[128,2048]{1,0:T(8,128)(2,1)S(1)} collective-permute-done((bf16[128,2048]{1,0:T(8,128)(2,1)S(1)}, bf16[128,2048]{1,0:T(8,128)(2,1)S(1)}, u32[]{:S(2)}, u32[]{:S(2)}) %collective-permute-start.12) | collective-permute-done | bytes 524320 | tf_op jit(solution)/shard_map/ppermute | solution.py:43
  120.3 2.1 %collective-permute-start.27 = (bf16[128,2048]{1,0:T(8,128)(2,1)S(1)}, bf16[128,2048]{1,0:T(8,128)(2,1)S(1)}, u32[]{:S(2)}, u32[]{:S(2)}) collective-permute-start(bf16[128,2048]{1,0:T(8,128)(2,1)S(1)} %whiten.7.mine), channel_id=1, source_target_pairs={{0,4},{1,5},{2,6},{3,7},{4,8},{5,9},{6,10},{7,11},{8,12},{9,13},{1... | collective-permute-start | bytes 1572872 | tf_op jit(solution)/shard_map/ppermute | solution.py:43
  122.4 0.8 collective-permute-done.11.behind
  123.2 1.3 collective-permute-start.23
  124.6 6.4 %cross_stack.5 = bf16[512,512]{1,0:T(8,128)(2,1)S(1)} custom-call(s32[64,2]{1,0:T(8,128)S(1)} %fusion.5.place, f32[64]{0:T(128)S(1)} %bitcast.89, bf16[128,2048]{1,0:T(8,128)(2,1)S(1)} %collective-permute-done.11.behind, bf16[128,2048]{1,0:T(8,128)(2,1)S(1)} %whiten.5.mine, bf16[128,2048]{1,0:T(8,128)(2,1)S(1)} %collective-permute-done.12.ahead, ...), custom_call_target="tpu_custom_call" | custom-call | flops 3221225472 | bytes 8388608 | tf_op jit(solution)/shard_map/cross_stack/pallas_call | solution.py:148
  131.6 1.0 collective-permute-start.22
  132.5 2.1 %collective-permute-done.27.behind = bf16[128,2048]{1,0:T(8,128)(2,1)S(1)} collective-permute-done((bf16[128,2048]{1,0:T(8,128)(2,1)S(1)}, bf16[128,2048]{1,0:T(8,128)(2,1)S(1)}, u32[]{:S(2)}, u32[]{:S(2)}) %collective-permute-start.27) | collective-permute-done | bytes 524320 | tf_op jit(solution)/shard_map/ppermute | solution.py:43
  134.6 1.9 %collective-permute-start.21 = (bf16[128,512]{1,0:T(8,128)(2,1)S(1)}, bf16[128,512]{1,0:T(8,128)(2,1)S(1)}, u32[]{:S(2)}, u32[]{:S(2)}) collective-permute-start(bf16[128,512]{1,0:T(8,128)(2,1)S(1)} %get-tuple-element.21), channel_id=1, source_target_pairs={{0,1},{1,0},{2,3},{3,2},{4,5},{5,4},{6,7},{7,6},{8,9},{9,8},{10,11... | collective-permute-start | bytes 393224 | tf_op jit(solution)/shard_map/ppermute | solution.py:37
  136.7 6.4 %cross_stack.7 = bf16[512,512]{1,0:T(8,128)(2,1)S(1)} custom-call(s32[64,2]{1,0:T(8,128)S(1)} %fusion.5.place, f32[64]{0:T(128)S(1)} %bitcast.90, bf16[128,2048]{1,0:T(8,128)(2,1)S(1)} %collective-permute-done.27.behind, bf16[128,2048]{1,0:T(8,128)(2,1)S(1)} %whiten.7.mine, bf16[128,2048]{1,0:T(8,128)(2,1)S(1)} %collective-permute-done.28.ahead, ...), custom_call_target="tpu_custom_call" | custom-call | flops 3221225472 | bytes 8388608 | tf_op jit(solution)/shard_map/cross_stack/pallas_call | solution.py:148
  143.2 1.7 %collective-permute-start.31 = (bf16[128,512]{1,0:T(8,128)(2,1)S(1)}, bf16[128,512]{1,0:T(8,128)(2,1)S(1)}, u32[]{:S(2)}, u32[]{:S(2)}) collective-permute-start(bf16[128,512]{1,0:T(8,128)(2,1)S(1)} %get-tuple-element.11), channel_id=1, source_target_pairs={{0,3},{1,2},{2,1},{3,0},{4,7},{5,6},{6,5},{7,4},{8,11},{9,10},{10,... | collective-permute-start | bytes 393224 | tf_op jit(solution)/shard_map/ppermute | solution.py:37
  145.0 6.4 %cross_stack.4 = bf16[512,512]{1,0:T(8,128)(2,1)S(1)} custom-call(s32[64,2]{1,0:T(8,128)S(1)} %fusion.5.place, f32[64]{0:T(128)S(1)} %bitcast.91, bf16[128,2048]{1,0:T(8,128)(2,1)S(1)} %collective-permute-done.3.behind, bf16[128,2048]{1,0:T(8,128)(2,1)S(1)} %whiten.4.mine, bf16[128,2048]{1,0:T(8,128)(2,1)S(1)} %collective-permute-done.4.ahead, ...), custom_call_target="tpu_custom_call" | custom-call | flops 3221225472 | bytes 8388608 | tf_op jit(solution)/shard_map/cross_stack/pallas_call | solution.py:148
  152.1 1.4 collective-permute-start.7
  153.6 0.7 collective-permute-start.13
  154.3 2.3 %collective-permute-done.30.r2 = bf16[128,512]{1,0:T(8,128)(2,1)S(1)} collective-permute-done((bf16[128,512]{1,0:T(8,128)(2,1)S(1)}, bf16[128,512]{1,0:T(8,128)(2,1)S(1)}, u32[]{:S(2)}, u32[]{:S(2)}) %collective-permute-start.30) | collective-permute-done | bytes 131104 | tf_op jit(solution)/shard_map/ppermute | solution.py:37
  156.7 1.7 %collective-permute-start.5 = (bf16[128,512]{1,0:T(8,128)(2,1)S(1)}, bf16[128,512]{1,0:T(8,128)(2,1)S(1)}, u32[]{:S(2)}, u32[]{:S(2)}) collective-permute-start(bf16[128,512]{1,0:T(8,128)(2,1)S(1)} %get-tuple-element.37), channel_id=1, source_target_pairs={{0,1},{1,0},{2,3},{3,2},{4,5},{5,4},{6,7},{7,6},{8,9},{9,8},{10,11... | collective-permute-start | bytes 393224 | tf_op jit(solution)/shard_map/ppermute | solution.py:37
  158.4 1.6 place_stacks.4.refs_0_
  160.0 1.6 place_stacks.5.refs_0_
  161.6 0.7 collective-permute-done.14.r2
  162.3 1.6 place_stacks.6.refs_0_
  163.9 1.2 collective-permute-done.6.r2
  165.1 1.6 place_stacks.7
  (105 shorter events, 7.2 us)
Async XLA Ops:
  0.0 6.1 %copy-start.5 = (u32[32]{0:T(128)S(1)}, u32[32]{0:T(128)}, u32[]{:S(2)}) copy-start(u32[32]{0:T(128)} %constant.136) | copy-start | bytes 388
  0.0 5.9 %copy-start.3 = (s32[16,2]{0,1:T(2,128)S(1)}, s32[16,2]{0,1:T(2,128)}, u32[]{:S(2)}) copy-start(s32[16,2]{0,1:T(2,128)} %param.9) | copy-start | bytes 388
  0.0 7.3 %copy-start.2 = (s32[4,128]{1,0:T(4,128)S(1)}, s32[4,128]{1,0:T(4,128)}, u32[]{:S(2)}) copy-start(s32[4,128]{1,0:T(4,128)} %param.8) | copy-start | bytes 6148
  0.0 7.3 %copy-start.4 = (s32[128]{0:T(128)S(1)}, s32[128]{0:T(128)}, u32[]{:S(2)}) copy-start(s32[128]{0:T(128)} %param.7) | copy-start | bytes 1540
  1.8 72.7 %collective-permute-start.10 = (bf16[32,2048]{1,0:T(8,128)(2,1)S(1)}, bf16[32,2048]{1,0:T(8,128)(2,1)S(1)}, u32[]{:S(2)}, u32[]{:S(2)}) collective-permute-start(bf16[32,2048]{1,0:T(8,128)(2,1)S(1)} %get-tuple-element.31), channel_id=1, source_target_pairs={{0,3},{1,2},{2,1},{3,0},{4,7},{5,6},{6,5},{7,4},{8,11},{9,10},{10,... | collective-permute-start | bytes 393224 | tf_op jit(solution)/shard_map/ppermute | solution.py:37
  3.7 71.7 %collective-permute-start.9 = (bf16[32,2048]{1,0:T(8,128)(2,1)S(1)}, bf16[32,2048]{1,0:T(8,128)(2,1)S(1)}, u32[]{:S(2)}, u32[]{:S(2)}) collective-permute-start(bf16[32,2048]{1,0:T(8,128)(2,1)S(1)} %get-tuple-element.32), channel_id=1, source_target_pairs={{0,2},{1,3},{2,0},{3,1},{4,6},{5,7},{6,4},{7,5},{8,10},{9,11},{10,... | collective-permute-start | bytes 393224 | tf_op jit(solution)/shard_map/ppermute | solution.py:37
  3.9 81.6 %collective-permute-start.8 = (bf16[32,2048]{1,0:T(8,128)(2,1)S(1)}, bf16[32,2048]{1,0:T(8,128)(2,1)S(1)}, u32[]{:S(2)}, u32[]{:S(2)}) collective-permute-start(bf16[32,2048]{1,0:T(8,128)(2,1)S(1)} %get-tuple-element.33), channel_id=1, source_target_pairs={{0,1},{1,0},{2,3},{3,2},{4,5},{5,4},{6,7},{7,6},{8,9},{9,8},{10,11... | collective-permute-start | bytes 393224 | tf_op jit(solution)/shard_map/ppermute | solution.py:37
  4.2 55.5 %collective-permute-start.18 = (bf16[32,2048]{1,0:T(8,128)(2,1)S(1)}, bf16[32,2048]{1,0:T(8,128)(2,1)S(1)}, u32[]{:S(2)}, u32[]{:S(2)}) collective-permute-start(bf16[32,2048]{1,0:T(8,128)(2,1)S(1)} %get-tuple-element.23), channel_id=1, source_target_pairs={{0,3},{1,2},{2,1},{3,0},{4,7},{5,6},{6,5},{7,4},{8,11},{9,10},{10,... | collective-permute-start | bytes 393224 | tf_op jit(solution)/shard_map/ppermute | solution.py:37
  5.7 62.4 %collective-permute-start.17 = (bf16[32,2048]{1,0:T(8,128)(2,1)S(1)}, bf16[32,2048]{1,0:T(8,128)(2,1)S(1)}, u32[]{:S(2)}, u32[]{:S(2)}) collective-permute-start(bf16[32,2048]{1,0:T(8,128)(2,1)S(1)} %get-tuple-element.24), channel_id=1, source_target_pairs={{0,2},{1,3},{2,0},{3,1},{4,6},{5,7},{6,4},{7,5},{8,10},{9,11},{10,... | collective-permute-start | bytes 393224 | tf_op jit(solution)/shard_map/ppermute | solution.py:37
  59.7 8.4 %collective-permute-start.16 = (bf16[32,2048]{1,0:T(8,128)(2,1)S(1)}, bf16[32,2048]{1,0:T(8,128)(2,1)S(1)}, u32[]{:S(2)}, u32[]{:S(2)}) collective-permute-start(bf16[32,2048]{1,0:T(8,128)(2,1)S(1)} %get-tuple-element.25), channel_id=1, source_target_pairs={{0,1},{1,0},{2,3},{3,2},{4,5},{5,4},{6,7},{7,6},{8,9},{9,8},{10,11... | collective-permute-start | bytes 393224 | tf_op jit(solution)/shard_map/ppermute | solution.py:37
  68.1 19.4 %collective-permute-start.2 = (bf16[32,2048]{1,0:T(8,128)(2,1)S(1)}, bf16[32,2048]{1,0:T(8,128)(2,1)S(1)}, u32[]{:S(2)}, u32[]{:S(2)}) collective-permute-start(bf16[32,2048]{1,0:T(8,128)(2,1)S(1)} %get-tuple-element.39), channel_id=1, source_target_pairs={{0,3},{1,2},{2,1},{3,0},{4,7},{5,6},{6,5},{7,4},{8,11},{9,10},{10,... | collective-permute-start | bytes 393224 | tf_op jit(solution)/shard_map/ppermute | solution.py:37
  68.2 19.4 %collective-permute-start.1 = (bf16[32,2048]{1,0:T(8,128)(2,1)S(1)}, bf16[32,2048]{1,0:T(8,128)(2,1)S(1)}, u32[]{:S(2)}, u32[]{:S(2)}) collective-permute-start(bf16[32,2048]{1,0:T(8,128)(2,1)S(1)} %get-tuple-element.40), channel_id=1, source_target_pairs={{0,2},{1,3},{2,0},{3,1},{4,6},{5,7},{6,4},{7,5},{8,10},{9,11},{10,... | collective-permute-start | bytes 393224 | tf_op jit(solution)/shard_map/ppermute | solution.py:37
  69.6 3.4 %copy-start = (bf16[2048,2048]{1,0:T(8,128)(2,1)S(1)}, bf16[2048,2048]{1,0:T(8,128)(2,1)}, u32[]{:S(2)}) copy-start(bf16[2048,2048]{1,0:T(8,128)(2,1)} %constant.129.clone.basis) | copy-start | bytes 25165828
  73.0 18.4 %slice-start = ((s8[8388608]{0:T(1024)(128)(4,1)}), s8[4194304]{0:T(1024)(128)(4,1)S(1)}, s32[]{:S(2)}) async-start(s8[8388608]{0:T(1024)(128)(4,1)} %bitcast.86), calls=%async_computation | async-start | bytes 8388608
  74.5 14.7 %collective-permute-start = (bf16[32,2048]{1,0:T(8,128)(2,1)S(1)}, bf16[32,2048]{1,0:T(8,128)(2,1)S(1)}, u32[]{:S(2)}, u32[]{:S(2)}) collective-permute-start(bf16[32,2048]{1,0:T(8,128)(2,1)S(1)} %get-tuple-element.41), channel_id=1, source_target_pairs={{0,1},{1,0},{2,3},{3,2},{4,5},{5,4},{6,7},{7,6},{8,9},{9,8},{10,11... | collective-permute-start | bytes 393224 | tf_op jit(solution)/shard_map/ppermute | solution.py:37
  75.4 28.6 %collective-permute-start.20 = (bf16[128,2048]{1,0:T(8,128)(2,1)S(1)}, bf16[128,2048]{1,0:T(8,128)(2,1)S(1)}, u32[]{:S(2)}, u32[]{:S(2)}) collective-permute-start(bf16[128,2048]{1,0:T(8,128)(2,1)S(1)} %whiten.6.mine), channel_id=1, source_target_pairs={{4,0},{5,1},{6,2},{7,3},{8,4},{9,5},{10,6},{11,7},{12,8},{13,9},{1... | collective-permute-start | bytes 1572872 | tf_op jit(solution)/shard_map/ppermute | solution.py:43
  85.5 20.4 %collective-permute-start.19 = (bf16[128,2048]{1,0:T(8,128)(2,1)S(1)}, bf16[128,2048]{1,0:T(8,128)(2,1)S(1)}, u32[]{:S(2)}, u32[]{:S(2)}) collective-permute-start(bf16[128,2048]{1,0:T(8,128)(2,1)S(1)} %whiten.6.mine), channel_id=1, source_target_pairs={{0,4},{1,5},{2,6},{3,7},{4,8},{5,9},{6,10},{7,11},{8,12},{9,13},{1... | collective-permute-start | bytes 1572872 | tf_op jit(solution)/shard_map/ppermute | solution.py:43
  87.5 6.1 %collective-permute-start.26 = (bf16[32,2048]{1,0:T(8,128)(2,1)S(1)}, bf16[32,2048]{1,0:T(8,128)(2,1)S(1)}, u32[]{:S(2)}, u32[]{:S(2)}) collective-permute-start(bf16[32,2048]{1,0:T(8,128)(2,1)S(1)} %get-tuple-element.15), channel_id=1, source_target_pairs={{0,3},{1,2},{2,1},{3,0},{4,7},{5,6},{6,5},{7,4},{8,11},{9,10},{10,... | collective-permute-start | bytes 393224 | tf_op jit(solution)/shard_map/ppermute | solution.py:37
  87.6 9.4 %collective-permute-start.25 = (bf16[32,2048]{1,0:T(8,128)(2,1)S(1)}, bf16[32,2048]{1,0:T(8,128)(2,1)S(1)}, u32[]{:S(2)}, u32[]{:S(2)}) collective-permute-start(bf16[32,2048]{1,0:T(8,128)(2,1)S(1)} %get-tuple-element.16), channel_id=1, source_target_pairs={{0,2},{1,3},{2,0},{3,1},{4,6},{5,7},{6,4},{7,5},{8,10},{9,11},{10,... | collective-permute-start | bytes 393224 | tf_op jit(solution)/shard_map/ppermute | solution.py:37
  89.2 2.2 %slice-start.1 = ((s8[8388608]{0:T(1024)(128)(4,1)}), s8[4194304]{0:T(1024)(128)(4,1)S(1)}, s32[]{:S(2)}) async-start(s8[8388608]{0:T(1024)(128)(4,1)} %bitcast.86), calls=%async_computation.1 | async-start | bytes 8388608
  89.2 9.7 %collective-permute-start.24 = (bf16[32,2048]{1,0:T(8,128)(2,1)S(1)}, bf16[32,2048]{1,0:T(8,128)(2,1)S(1)}, u32[]{:S(2)}, u32[]{:S(2)}) collective-permute-start(bf16[32,2048]{1,0:T(8,128)(2,1)S(1)} %get-tuple-element.17), channel_id=1, source_target_pairs={{0,1},{1,0},{2,3},{3,2},{4,5},{5,4},{6,7},{7,6},{8,9},{9,8},{10,11... | collective-permute-start | bytes 393224 | tf_op jit(solution)/shard_map/ppermute | solution.py:37
  93.6 49.5 %collective-permute-start.4 = (bf16[128,2048]{1,0:T(8,128)(2,1)S(1)}, bf16[128,2048]{1,0:T(8,128)(2,1)S(1)}, u32[]{:S(2)}, u32[]{:S(2)}) collective-permute-start(bf16[128,2048]{1,0:T(8,128)(2,1)S(1)} %whiten.4.mine), channel_id=1, source_target_pairs={{4,0},{5,1},{6,2},{7,3},{8,4},{9,5},{10,6},{11,7},{12,8},{13,9},{1... | collective-permute-start | bytes 1572872 | tf_op jit(solution)/shard_map/ppermute | solution.py:43
  97.0 46.1 %collective-permute-start.3 = (bf16[128,2048]{1,0:T(8,128)(2,1)S(1)}, bf16[128,2048]{1,0:T(8,128)(2,1)S(1)}, u32[]{:S(2)}, u32[]{:S(2)}) collective-permute-start(bf16[128,2048]{1,0:T(8,128)(2,1)S(1)} %whiten.4.mine), channel_id=1, source_target_pairs={{0,4},{1,5},{2,6},{3,7},{4,8},{5,9},{6,10},{7,11},{8,12},{9,13},{1... | collective-permute-start | bytes 1572872 | tf_op jit(solution)/shard_map/ppermute | solution.py:43
  99.0 21.3 %collective-permute-start.12 = (bf16[128,2048]{1,0:T(8,128)(2,1)S(1)}, bf16[128,2048]{1,0:T(8,128)(2,1)S(1)}, u32[]{:S(2)}, u32[]{:S(2)}) collective-permute-start(bf16[128,2048]{1,0:T(8,128)(2,1)S(1)} %whiten.5.mine), channel_id=1, source_target_pairs={{4,0},{5,1},{6,2},{7,3},{8,4},{9,5},{10,6},{11,7},{12,8},{13,9},{1... | collective-permute-start | bytes 1572872 | tf_op jit(solution)/shard_map/ppermute | solution.py:43
  102.5 7.0 %copy-start.1 = (bf16[2048,512]{1,0:T(8,128)(2,1)S(1)}, bf16[2048,512]{1,0:T(8,128)(2,1)}, u32[]{:S(2)}) copy-start(bf16[2048,512]{1,0:T(8,128)(2,1)} %constant.130.clone.lagmap) | copy-start | bytes 6291460
  104.0 19.2 %collective-permute-start.11 = (bf16[128,2048]{1,0:T(8,128)(2,1)S(1)}, bf16[128,2048]{1,0:T(8,128)(2,1)S(1)}, u32[]{:S(2)}, u32[]{:S(2)}) collective-permute-start(bf16[128,2048]{1,0:T(8,128)(2,1)S(1)} %whiten.5.mine), channel_id=1, source_target_pairs={{0,4},{1,5},{2,6},{3,7},{4,8},{5,9},{6,10},{7,11},{8,12},{9,13},{1... | collective-permute-start | bytes 1572872 | tf_op jit(solution)/shard_map/ppermute | solution.py:43
  105.9 25.6 %collective-permute-start.28 = (bf16[128,2048]{1,0:T(8,128)(2,1)S(1)}, bf16[128,2048]{1,0:T(8,128)(2,1)S(1)}, u32[]{:S(2)}, u32[]{:S(2)}) collective-permute-start(bf16[128,2048]{1,0:T(8,128)(2,1)S(1)} %whiten.7.mine), channel_id=1, source_target_pairs={{4,0},{5,1},{6,2},{7,3},{8,4},{9,5},{10,6},{11,7},{12,8},{13,9},{1... | collective-permute-start | bytes 1572872 | tf_op jit(solution)/shard_map/ppermute | solution.py:43
  120.3 14.3 %collective-permute-start.27 = (bf16[128,2048]{1,0:T(8,128)(2,1)S(1)}, bf16[128,2048]{1,0:T(8,128)(2,1)S(1)}, u32[]{:S(2)}, u32[]{:S(2)}) collective-permute-start(bf16[128,2048]{1,0:T(8,128)(2,1)S(1)} %whiten.7.mine), channel_id=1, source_target_pairs={{0,4},{1,5},{2,6},{3,7},{4,8},{5,9},{6,10},{7,11},{8,12},{9,13},{1... | collective-permute-start | bytes 1572872 | tf_op jit(solution)/shard_map/ppermute | solution.py:43
  123.2 28.3 %collective-permute-start.23 = (bf16[128,512]{1,0:T(8,128)(2,1)S(1)}, bf16[128,512]{1,0:T(8,128)(2,1)S(1)}, u32[]{:S(2)}, u32[]{:S(2)}) collective-permute-start(bf16[128,512]{1,0:T(8,128)(2,1)S(1)} %get-tuple-element.19), channel_id=1, source_target_pairs={{0,3},{1,2},{2,1},{3,0},{4,7},{5,6},{6,5},{7,4},{8,11},{9,10},{10,... | collective-permute-start | bytes 393224 | tf_op jit(solution)/shard_map/ppermute | solution.py:37
  131.6 20.0 %collective-permute-start.22 = (bf16[128,512]{1,0:T(8,128)(2,1)S(1)}, bf16[128,512]{1,0:T(8,128)(2,1)S(1)}, u32[]{:S(2)}, u32[]{:S(2)}) collective-permute-start(bf16[128,512]{1,0:T(8,128)(2,1)S(1)} %get-tuple-element.20), channel_id=1, source_target_pairs={{0,2},{1,3},{2,0},{3,1},{4,6},{5,7},{6,4},{7,5},{8,10},{9,11},{10,... | collective-permute-start | bytes 393224 | tf_op jit(solution)/shard_map/ppermute | solution.py:37
  134.6 17.4 %collective-permute-start.21 = (bf16[128,512]{1,0:T(8,128)(2,1)S(1)}, bf16[128,512]{1,0:T(8,128)(2,1)S(1)}, u32[]{:S(2)}, u32[]{:S(2)}) collective-permute-start(bf16[128,512]{1,0:T(8,128)(2,1)S(1)} %get-tuple-element.21), channel_id=1, source_target_pairs={{0,1},{1,0},{2,3},{3,2},{4,5},{5,4},{6,7},{7,6},{8,9},{9,8},{10,11... | collective-permute-start | bytes 393224 | tf_op jit(solution)/shard_map/ppermute | solution.py:37
  143.1 10.4 %collective-permute-start.15 = (bf16[128,512]{1,0:T(8,128)(2,1)S(1)}, bf16[128,512]{1,0:T(8,128)(2,1)S(1)}, u32[]{:S(2)}, u32[]{:S(2)}) collective-permute-start(bf16[128,512]{1,0:T(8,128)(2,1)S(1)} %get-tuple-element.27), channel_id=1, source_target_pairs={{0,3},{1,2},{2,1},{3,0},{4,7},{5,6},{6,5},{7,4},{8,11},{9,10},{10,... | collective-permute-start | bytes 393224 | tf_op jit(solution)/shard_map/ppermute | solution.py:37
  143.2 10.4 %collective-permute-start.31 = (bf16[128,512]{1,0:T(8,128)(2,1)S(1)}, bf16[128,512]{1,0:T(8,128)(2,1)S(1)}, u32[]{:S(2)}, u32[]{:S(2)}) collective-permute-start(bf16[128,512]{1,0:T(8,128)(2,1)S(1)} %get-tuple-element.11), channel_id=1, source_target_pairs={{0,3},{1,2},{2,1},{3,0},{4,7},{5,6},{6,5},{7,4},{8,11},{9,10},{10,... | collective-permute-start | bytes 393224 | tf_op jit(solution)/shard_map/ppermute | solution.py:37
  151.5 5.2 %collective-permute-start.30 = (bf16[128,512]{1,0:T(8,128)(2,1)S(1)}, bf16[128,512]{1,0:T(8,128)(2,1)S(1)}, u32[]{:S(2)}, u32[]{:S(2)}) collective-permute-start(bf16[128,512]{1,0:T(8,128)(2,1)S(1)} %get-tuple-element.12), channel_id=1, source_target_pairs={{0,2},{1,3},{2,0},{3,1},{4,6},{5,7},{6,4},{7,5},{8,10},{9,11},{10,... | collective-permute-start | bytes 393224 | tf_op jit(solution)/shard_map/ppermute | solution.py:37
  151.5 5.1 %collective-permute-start.29 = (bf16[128,512]{1,0:T(8,128)(2,1)S(1)}, bf16[128,512]{1,0:T(8,128)(2,1)S(1)}, u32[]{:S(2)}, u32[]{:S(2)}) collective-permute-start(bf16[128,512]{1,0:T(8,128)(2,1)S(1)} %get-tuple-element.13), channel_id=1, source_target_pairs={{0,1},{1,0},{2,3},{3,2},{4,5},{5,4},{6,7},{7,6},{8,9},{9,8},{10,11... | collective-permute-start | bytes 393224 | tf_op jit(solution)/shard_map/ppermute | solution.py:37
  152.1 11.8 %collective-permute-start.7 = (bf16[128,512]{1,0:T(8,128)(2,1)S(1)}, bf16[128,512]{1,0:T(8,128)(2,1)S(1)}, u32[]{:S(2)}, u32[]{:S(2)}) collective-permute-start(bf16[128,512]{1,0:T(8,128)(2,1)S(1)} %get-tuple-element.35), channel_id=1, source_target_pairs={{0,3},{1,2},{2,1},{3,0},{4,7},{5,6},{6,5},{7,4},{8,11},{9,10},{10,... | collective-permute-start | bytes 393224 | tf_op jit(solution)/shard_map/ppermute | solution.py:37
  153.5 8.8 %collective-permute-start.14 = (bf16[128,512]{1,0:T(8,128)(2,1)S(1)}, bf16[128,512]{1,0:T(8,128)(2,1)S(1)}, u32[]{:S(2)}, u32[]{:S(2)}) collective-permute-start(bf16[128,512]{1,0:T(8,128)(2,1)S(1)} %get-tuple-element.28), channel_id=1, source_target_pairs={{0,2},{1,3},{2,0},{3,1},{4,6},{5,7},{6,4},{7,5},{8,10},{9,11},{10,... | collective-permute-start | bytes 393224 | tf_op jit(solution)/shard_map/ppermute | solution.py:37
  153.6 8.7 %collective-permute-start.13 = (bf16[128,512]{1,0:T(8,128)(2,1)S(1)}, bf16[128,512]{1,0:T(8,128)(2,1)S(1)}, u32[]{:S(2)}, u32[]{:S(2)}) collective-permute-start(bf16[128,512]{1,0:T(8,128)(2,1)S(1)} %get-tuple-element.29), channel_id=1, source_target_pairs={{0,1},{1,0},{2,3},{3,2},{4,5},{5,4},{6,7},{7,6},{8,9},{9,8},{10,11... | collective-permute-start | bytes 393224 | tf_op jit(solution)/shard_map/ppermute | solution.py:37
  156.6 8.4 %collective-permute-start.6 = (bf16[128,512]{1,0:T(8,128)(2,1)S(1)}, bf16[128,512]{1,0:T(8,128)(2,1)S(1)}, u32[]{:S(2)}, u32[]{:S(2)}) collective-permute-start(bf16[128,512]{1,0:T(8,128)(2,1)S(1)} %get-tuple-element.36), channel_id=1, source_target_pairs={{0,2},{1,3},{2,0},{3,1},{4,6},{5,7},{6,4},{7,5},{8,10},{9,11},{10,... | collective-permute-start | bytes 393224 | tf_op jit(solution)/shard_map/ppermute | solution.py:37
  156.7 8.4 %collective-permute-start.5 = (bf16[128,512]{1,0:T(8,128)(2,1)S(1)}, bf16[128,512]{1,0:T(8,128)(2,1)S(1)}, u32[]{:S(2)}, u32[]{:S(2)}) collective-permute-start(bf16[128,512]{1,0:T(8,128)(2,1)S(1)} %get-tuple-element.37), channel_id=1, source_target_pairs={{0,1},{1,0},{2,3},{3,2},{4,5},{5,4},{6,7},{7,6},{8,9},{9,8},{10,11... | collective-permute-start | bytes 393224 | tf_op jit(solution)/shard_map/ppermute | solution.py:37

commit v2 on v0

v2 whole, which is shorter than its diff:
```python
import functools
import math

import jax
import jax.numpy as jnp
import numpy as np
from jax import lax
from jax.experimental import pallas as pl
from jax.experimental.pallas import tpu as pltpu
from jax.sharding import PartitionSpec as P

LAGS = 512
QUAD = 4
CHANS = 8
STEP = 256
VMEM_BYTES = 50 << 20
MASKS = (0, 2, 1, 3)

SMEM = pl.BlockSpec(memory_space=pltpu.SMEM)
ANY = pl.BlockSpec(memory_space=pl.ANY)


def bin_order(bins):
    return np.concatenate([np.arange(2, bins + 1, 2), np.arange(1, bins + 1, 2)])


def make_basis(width, bins):
    rows = np.arange(width // 2, dtype=np.int64)[:, None]
    phase = (rows * bin_order(bins)[None, :] % width) * (2.0 * math.pi / width)
    table = np.stack([np.cos(phase), -np.sin(phase)]).reshape(2, width // 2, bins // STEP, STEP)
    table = table.transpose(2, 1, 0, 3).reshape(bins // STEP, width // 2, 2 * STEP)
    return table.astype(np.float32).astype(jnp.bfloat16)


def make_hann(width):
    hann = 0.5 - 0.5 * np.cos(np.arange(width // 2) * (2.0 * math.pi / width))
    return np.stack([hann, 1.0 - hann]).astype(np.float32)


def make_lagmap(width, bins, lags):
    rows = bin_order(bins)[:, None]
    cols = np.arange(lags, dtype=np.int64)[None, :] - lags // 2 + width
    phase = (rows * cols % width) * (2.0 * math.pi / width)
    scale = 2.0 / math.sqrt(bins)
    table = np.concatenate([scale * np.cos(phase), -scale * np.sin(phase)], 0)
    return table.astype(np.float32).astype(jnp.bfloat16)


def to_quad_peer(value, mask):
    count = lax.axis_size("chan")
    return lax.ppermute(value, "chan", [(s, s ^ mask) for s in range(count)])


def swap_quads(value, odd):
    count = lax.axis_size("chan")
    pairs = []
    for s in range(count):
        quad = s // QUAD
        other = s + QUAD if quad % 2 == odd else s - QUAD
        if 0 <= other < count:
            pairs.append((s, other))
    return lax.ppermute(value, "chan", pairs)


def after(value, *others):
    return lax.optimization_barrier((value,) + others)[0]


def whiten_kernel(chunks, first, core, own, got, own_peer, got_peer, curve, basis, *refs):
    outs = refs[:chunks]
    raw, table, hann, re_s, im_s, amp_s, result, sems, out_sem = refs[chunks:]
    windows, both = raw.shape[1:3]
    half = raw.shape[3] // 2
    steps = basis.shape[0]
    bins = steps * STEP
    copies = [
        pltpu.make_async_copy(own.at[:, pl.ds(first, both)], raw.at[0], sems.at[0]),
        pltpu.make_async_copy(got, raw.at[1], sems.at[1]),
        pltpu.make_async_copy(own_peer.at[:, pl.ds(first, both)], raw.at[2], sems.at[2]),
        pltpu.make_async_copy(got_peer, raw.at[3], sems.at[3]),
        pltpu.make_async_copy(curve, hann, sems.at[4]),
    ]
    tables = [
        pltpu.make_async_copy(basis.at[j], table.at[j], sems.at[QUAD + 1 + j])
        for j in range(steps)
    ]
    for copy in copies + tables:
        copy.start()
    for copy in copies:
        copy.wait()
    low = core[0] == 0
    sums, gaps = [], []
    for c in range(chunks):
        low_at = slice(2 * c * CHANS, (2 * c + 1) * CHANS)
        high_at = slice((2 * c + 1) * CHANS, (2 * c + 2) * CHANS)
        for r in range(QUAD):
            for w in range(windows):
                left = raw[r, w, :, 0:half].astype(jnp.float32)
                right = raw[r, w, :, half:].astype(jnp.float32)
                left = jnp.where(low, left[low_at], left[high_at]) * hann[0:1, :]
                right = jnp.where(low, right[low_at], right[high_at]) * hann[1:2, :]
                sums.append(left + right)
                gaps.append(left - right)
    folded = [jnp.concatenate(x, 0).astype(jnp.bfloat16) for x in (sums, gaps)]
    rows = QUAD * windows * CHANS
    total = jnp.zeros((chunks * rows, 128), jnp.float32)
    for j in range(steps):
        tables[j].wait()
        both_parts = jnp.dot(
            folded[2 * j // steps], table[j], preferred_element_type=jnp.float32
        )
        re, im = both_parts[:, :STEP], both_parts[:, STEP:]
        amp = jnp.sqrt(re * re + im * im)
        at = slice(j * STEP, (j + 1) * STEP)
        re_s[:, at] = re
        im_s[:, at] = im
        amp_s[:, at] = amp
        for i in range(0, STEP, 128):
            total = total + amp[:, i : i + 128]
    level = jnp.sum(total, axis=-1, keepdims=True) * (1.0 / bins) + 1e-06
    for j in range(0, bins, STEP):
        factor = 1.0 / (amp_s[:, j : j + STEP] + level)
        result[:, j : j + STEP] = (re_s[:, j : j + STEP] * factor).astype(jnp.bfloat16)
        result[:, bins + j : bins + j + STEP] = (im_s[:, j : j + STEP] * factor).astype(
            jnp.bfloat16
        )
    writes = [
        pltpu.make_async_copy(result.at[pl.ds(c * rows, rows)], outs[c], out_sem.at[c])
        for c in range(chunks)
    ]
    for write in writes:
        write.start()
    for write in writes:
        write.wait()


def whiten(first, core, own, got, own_peer, got_peer, hann, basis):
    windows, both, width = got.shape
    chunks = both // (2 * CHANS)
    rows = QUAD * windows * CHANS
    total = chunks * rows
    bins = width // 2
    return pl.pallas_call(
        functools.partial(whiten_kernel, chunks, first),
        out_shape=[jax.ShapeDtypeStruct((rows, width), jnp.bfloat16)] * chunks,
        in_specs=[SMEM] + [ANY] * 6,
        out_specs=[ANY] * chunks,
        scratch_shapes=[
            pltpu.VMEM((QUAD, windows, both, width), jnp.bfloat16),
            pltpu.VMEM(basis.shape, jnp.bfloat16),
            pltpu.VMEM(hann.shape, jnp.float32),
            pltpu.VMEM((total, bins), jnp.float32),
            pltpu.VMEM((total, bins), jnp.float32),
            pltpu.VMEM((total, bins), jnp.float32),
            pltpu.VMEM((total, width), jnp.bfloat16),
            pltpu.SemaphoreType.DMA((QUAD + 1 + basis.shape[0],)),
            pltpu.SemaphoreType.DMA((chunks,)),
        ],
        compiler_params=pltpu.CompilerParams(vmem_limit_bytes=VMEM_BYTES),
        cost_estimate=pl.CostEstimate(flops=1024, bytes_accessed=1024, transcendentals=0),
        name="whiten",
    )(core, own, got, own_peer, got_peer, hann, basis)


def cross_kernel(sides, chunk, spot, windows, place, filled, *refs):
    count = len(sides)
    blocks, flags, lagmap = refs[:3], refs[3], refs[4]
    outs = refs[-count - 8 : -8]
    raw, live, near, cross, table, result, sems, out_sems = refs[-8:]
    width = near.shape[-1]
    bins = width // 2
    pairs = place.shape[0] // 2
    copies = [pltpu.make_async_copy(b, raw.at[i], sems.at[i]) for i, b in enumerate(blocks)]
    copies.append(pltpu.make_async_copy(flags.at[chunk], live, sems.at[3]))
    load = pltpu.make_async_copy(lagmap, table, sems.at[4])
    for copy in copies:
        copy.start()
    load.start()
    for i, copy in enumerate(copies):
        copy.wait()
        if i < 3:
            near[pl.ds(i * QUAD, QUAD)] = (
                raw[i].astype(jnp.float32).reshape(QUAD, windows, CHANS, width)
            )

    def one(p):
        a, b = near.at[place[p, 0]], near.at[place[p, 1]]
        live_a, live_b = live.at[place[p, 0]], live.at[place[p, 1]]
        total = live_a[0] * live_b[0]
        for w in range(1, windows):
            total = total + live_a[w] * live_b[w]
        scale = jnp.where(filled[p] > 0, 1.0, 0.0) * (1.0 / jnp.maximum(total, 1.0))
        res, ims = [], []
        for j in range(0, bins, 128):
            re = im = None
            for w in range(windows):
                ra, ia = a[w, :, j : j + 128], a[w, :, bins + j : bins + j + 128]
                rb, ib = b[w, :, j : j + 128], b[w, :, bins + j : bins + j + 128]
                x, y = ra * rb + ia * ib, ra * ib - ia * rb
                re = x if re is None else re + x
                im = y if im is None else im + y
            res.append(re * scale)
            ims.append(im * scale)
        return res + ims

    writes = []
    for n, side in enumerate(sides):
        base = side * pairs

        def two(h, carry):
            p = base + 2 * h
            some = filled[p] + filled[p + 1] > 0

            @pl.when(some)
            def _():
                for j, (u, v) in enumerate(zip(one(p), one(p + 1))):
                    cross[h, :, j * 128 : (j + 1) * 128] = jnp.concatenate([u, v], 0).astype(
                        jnp.bfloat16
                    )

            @pl.when(jnp.logical_not(some))
            def _():
                cross[h] = jnp.zeros(cross.shape[1:], jnp.bfloat16)

            return carry

        lax.fori_loop(0, pairs // 2, two, 0)
        if n == 0:
            load.wait()
        result[n] = jnp.dot(
            cross[...].reshape(pairs * CHANS, width),
            table[...],
            preferred_element_type=jnp.float32,
        ).astype(jnp.bfloat16)
        write = pltpu.make_async_copy(result.at[n], outs[n].at[spot], out_sems.at[n])
        write.start()
        writes.append(write)
    for write in writes:
        write.wait()


def cross_stack(sides, chunk, spot, depth, place, filled, blocks, flags, lagmap, held):
    count = len(sides)
    pairs = place.shape[0] // 2
    rows, width = blocks[0].shape
    windows = flags.shape[2]
    return pl.pallas_call(
        functools.partial(cross_kernel, sides, chunk, spot, windows),
        out_shape=[jax.ShapeDtypeStruct((depth, pairs * CHANS, LAGS), jnp.bfloat16)] * count,
        in_specs=[SMEM, SMEM] + [ANY] * (5 + len(held)),
        out_specs=[ANY] * count,
        input_output_aliases={7 + n: n for n in range(len(held))},
        scratch_shapes=[
            pltpu.VMEM((3, rows, width), jnp.bfloat16),
            pltpu.VMEM(flags.shape[1:], jnp.float32),
            pltpu.VMEM((3 * QUAD, windows, CHANS, width), jnp.float32),
            pltpu.VMEM((pairs * CHANS // 16, 16, width), jnp.bfloat16),
            pltpu.VMEM((width, LAGS), jnp.bfloat16),
            pltpu.VMEM((count, pairs * CHANS, LAGS), jnp.bfloat16),
            pltpu.SemaphoreType.DMA((5,)),
            pltpu.SemaphoreType.DMA((count,)),
        ],
        compiler_params=pltpu.CompilerParams(vmem_limit_bytes=VMEM_BYTES),
        cost_estimate=pl.CostEstimate(flops=1024, bytes_accessed=1024, transcendentals=0),
        name="cross_stack",
    )(place, filled, *blocks, flags, lagmap, *held)


def place_kernel(slot, r0, r1, r2, r3, *refs):
    out = refs[-1]
    for m, r in enumerate((r0, r1, r2, r3)):
        at = pl.multiple_of(slot[m] % 2 * CHANS, CHANS)
        chip = slot[m] // 2
        for p in range(0, out.shape[0], 2):
            wide = r[0, 0, pl.ds(p * CHANS, 2 * CHANS), :].astype(jnp.float32)
            out[p, chip, pl.ds(at, CHANS), :] = wide[:CHANS]
            out[p + 1, chip, pl.ds(at, CHANS), :] = wide[CHANS:]


def place_stacks(first, slot, parts, held, shape):
    extra = [] if held is None else [held]
    step = 8
    depth = parts[0].shape[0]
    parts = [part.reshape(depth, 2, -1, LAGS) for part in parts]
    spot = [
        pl.BlockSpec((1, 1, step * CHANS, LAGS), lambda c, i, *_, k=k: (c, k, i, 0))
        for k in (0, 0, 1, 1)
    ]
    return pl.pallas_call(
        place_kernel,
        out_shape=jax.ShapeDtypeStruct(shape, jnp.float32),
        grid_spec=pltpu.PrefetchScalarGridSpec(
            num_scalar_prefetch=1,
            grid=(depth, shape[0] // step),
            in_specs=spot + [ANY] * len(extra),
            out_specs=pl.BlockSpec(
                (step, 2, 2 * CHANS, LAGS), lambda c, i, *_: (i, 0, first + c, 0)
            ),
        ),
        input_output_aliases={5: 0} if extra else {},
        compiler_params=pltpu.CompilerParams(vmem_limit_bytes=VMEM_BYTES),
        cost_estimate=pl.CostEstimate(flops=1024, bytes_accessed=1024, transcendentals=0),
        name="place_stacks",
    )(slot, *parts, *extra)


def body(records, dead, glitch, pairs):
    windows, block, width = records.shape
    bins = width // 2
    slots = pairs.shape[0]
    half = block // 2
    wide = 2 * CHANS
    chunks = half // wide
    here = lax.axis_index("chan")
    mine = here % QUAD
    quad = here // QUAD
    chip = mine // 2
    core = (mine % 2).reshape(1).astype(jnp.int32)
    basis = jnp.asarray(make_basis(width, bins))
    hann = jnp.asarray(make_hann(width))
    lagmap = jnp.asarray(make_lagmap(width, bins, LAGS))
    live = dead[None, :] * glitch
    live_wire = live.astype(jnp.bfloat16)[..., None]

    def cut(at, count):
        raw = lax.dynamic_slice_in_dim(records, at, count, 1)
        return raw * lax.dynamic_slice_in_dim(live_wire, at, count, 1)

    there = (1 - chip) * half
    notes = jnp.concatenate([live.reshape(-1), pairs.reshape(-1)]).astype(jnp.float32)
    send, at = lax.optimization_barrier((cut(there, wide), chip * half))
    got = [to_quad_peer(send, 2)]
    own, there = lax.optimization_barrier((cut(at, half), there))
    own_peer = to_quad_peer(own, 1)
    notes, there = lax.optimization_barrier((notes, there))
    send, there = lax.optimization_barrier((cut(there + wide, wide), there))
    got.append(to_quad_peer(send, 2))
    notes = jnp.stack([notes, to_quad_peer(notes, 2)])
    got.append(to_quad_peer(cut(there + 2 * wide, half - 2 * wide), 2))
    got_peer = [to_quad_peer(got[0], 1)]
    notes = jnp.concatenate([notes, to_quad_peer(notes, 1)])

    white = []
    for c in range(3):
        if c:
            got_peer.append(to_quad_peer(after(got[c], white[-1]), 1))
        white += whiten(c * wide, core, own, got[c], own_peer, got_peer[c], hann, basis)
    near = [(swap_quads(w, 0), w, swap_quads(w, 1)) for w in white]

    flags = notes[:, : windows * block]
    sent = after(flags, got_peer[1])
    flags = jnp.stack([swap_quads(sent, 0), flags, swap_quads(sent, 1)])
    flags = flags.reshape(3 * QUAD, windows, 2, chunks, 2, CHANS)
    flags = lax.dynamic_index_in_dim(flags, chip, 2, False)
    flags = lax.dynamic_index_in_dim(flags, core[0], 3, False)
    flags = jnp.broadcast_to(
        flags.transpose(2, 0, 1, 3)[..., None], (chunks, 3 * QUAD, windows, CHANS, 128)
    )

    listed = notes[:, windows * block :].astype(jnp.int32).reshape(2, 2, slots, 2)
    listed = listed.swapaxes(0, 1)[::-1].reshape(-1, 2)
    filled = (listed[..., 0] >= 0) & (listed[..., 1] >= 0)
    inside = (listed % QUAD) ^ mine
    side = jnp.where(quad % 2 == 0, 1, -1)
    place = (1 - (listed // QUAD - quad) * side) * QUAD + (inside % 2) * 2 + inside // 2
    place = jnp.where(filled[..., None], jnp.clip(place, 0, 3 * QUAD - 1), 0)
    filled = filled.astype(jnp.int32)
    slot = jnp.stack([mine ^ m for m in MASKS]).astype(jnp.int32)
    shape = (slots, 2, half, LAGS)

    def cross(sides, c, spot, depth, place, held=()):
        return cross_stack(
            sides, c, spot, depth, place, filled, near[c], flags, lagmap, tuple(held)
        )

    def returned(home, away):
        return (home, away, to_quad_peer(home, 1), to_quad_peer(away, 1))

    place = after(place, *white)
    both = cross((0, 1), 0, 0, 2, place)
    away, home = cross((0, 1), 1, 1, 2, place, both)
    parts = returned(home, to_quad_peer(away, 2))
    away, home = cross((0, 1), 2, 0, 1, after(place, home))
    away = to_quad_peer(away, 2)
    held = place_stacks(0, slot, parts, None, shape)
    parts = returned(home, away)
    (away,) = cross((0,), 3, 0, 1, after(place, home, held))
    away = to_quad_peer(away, 2)
    held = place_stacks(2, slot, parts, held, shape)
    (home,) = cross((1,), 3, 0, 1, after(place, held))
    held = place_stacks(3, slot, returned(home, away), held, shape)
    return held.reshape(slots, block, LAGS)


def solution(mesh):
    placed = (
        P(None, ("group", "chan"), None),
        P(("group", "chan")),
        P(None, ("group", "chan")),
        P(("group", "chan"), None),
    )
    return jax.shard_map(
        body,
        mesh=mesh,
        in_specs=placed,
        out_specs=P(("group", "chan"), None, None),
        check_vma=False,
    )
```

time: 492 us -> 120 us (0.24)
  waiting for transfers between devices: 217 us -> 21.1 us
  other arithmetic: 161 us -> 7.7 us
  Pallas kernels: 0 us -> 49.5 us
  loops' own time: 39.6 us -> 0 us
  matrix products: 14.9 us -> 0 us
  local copies, waits for them, and re-layouts: 19.7 us -> 8.02 us
    ppermute x12 -> x28, waiting for transfers between devices: 217 us -> 21.1 us  [the longest x18 20.8 us: to_quad_peer(): return lax.ppermute(value, 'chan', [(s, s ^ mask) for s in range(count)])]
    convert_element_type x17 -> x4, other arithmetic: 52.8 us -> 0.72 us  [the longest x1 0.69 us: body(): live_wire = live.astype(jnp.bfloat16)[..., None]]
    pallas_call x0 -> x11, Pallas kernels: none -> 49.5 us  [the longest x5 32.2 us: cross_stack(): pl.pallas_call(functools.partial(cross_kernel, sides, chunk, spot, window...]
    another operation x2 -> x4, other arithmetic: 44.4 us -> 0.11 us  [the longest x1 0.08 us: body(): slot = jnp.stack([mine ^ m for m in MASKS]).astype(jnp.int32)]
    another operation x1 -> x0, loops' own time: 39.6 us -> none  [body(): crosses = lax.map(one_slot, pairs)]
    concatenate x8 -> x1, other arithmetic: 29.2 us -> 0.01 us  [body(): notes = jnp.concatenate([notes, to_quad_peer(notes, 1)])]
    reduce_sum x33 -> x0, other arithmetic: 19 us -> none  [the longest x16 17.7 us: cross_pair(): cross_re = jnp.sum(a_re * b_re + a_im * b_im, axis=0)]
    dynamic_update_slice x16 -> x0, other arithmetic: 15.5 us -> none  [body(): crosses = lax.map(one_slot, pairs)]
  transfers between devices with their start and end apart: 12 -> 28, of which waited for: 7 -> 7; matrix products, arithmetic and copies ran while one was open for 6% -> 6% of each run, Pallas kernels for 0% -> 33%
where the time goes in v2:
time: 120 us; the launch traced here: 119 us
  Pallas kernels  49.5 us (41%)
  starting transfers between devices  31.7 us (26%)
  waiting for transfers between devices  21.1 us (18%)
  local copies, waits for them, and re-layouts  8.02 us (7%)
  other arithmetic  7.7 us (6%)
    pallas_call x5, Pallas kernels, cross_stack(): pl.pallas_call(functools.partial(cross_kernel, sides, chunk, spot, window...  32.2 us
    ppermute x18, waiting for transfers between devices, to_quad_peer(): return lax.ppermute(value, 'chan', [(s, s ^ mask) for s in range(count)])  20.8 us
    ppermute x18, starting transfers between devices, to_quad_peer(): return lax.ppermute(value, 'chan', [(s, s ^ mask) for s in range(count)])  17.7 us
    ppermute x10, starting transfers between devices, swap_quads(): return lax.ppermute(value, 'chan', pairs)  14.1 us
    pallas_call x3, Pallas kernels, whiten(): pl.pallas_call(functools.partial(whiten_kernel, chunks, first), out_shape...  10.1 us
    pallas_call x3, Pallas kernels, place_stacks(): pl.pallas_call(place_kernel, out_shape=jax.ShapeDtypeStruct(shape, jnp.fl...  7.25 us
    mul x4, other arithmetic, cut(): return raw * lax.dynamic_slice_in_dim(live_wire, at, count, 1)  6.78 us
    unnamed x13, local copies, waits for them, and re-layouts  4.27 us
  transfers between devices with their start and end apart: 28, of which 7 were waited for; matrix products, arithmetic and copies ran while one was open for 6% of the time, Pallas kernels for 33%

profile of v2, /device:TPU:11, one launch (start us, length us, event | category | flops | bytes accessed | tf_op | source)
XLA Modules:
  0.0 118.5 jit_solution(6486214337787820391)
XLA Ops:
  0.0 0.7 multiply_convert_fusion
  0.8 1.1 dynamic-slice_multiply_fusion.3
  1.9 0.8 copy.25
  2.8 1.7 %dynamic-slice_multiply_fusion.own = bf16[4,64,2048]{2,1,0:T(8,128)(2,1)S(1)} fusion(bf16[4,128,2048]{2,1,0:T(8,128)(2,1)} %param.7, s32[]{:T(128)S(6)} %select_n.79, bf16[4,64]{1,0:T(4,128)(2,1)S(1)} %constant_dynamic-slice_fusion.3), kind=kLoop, calls=%fused_computation | loop fusion | flops 2097152 | bytes 2097668 | tf_op jit(solution)/shard_map/mul | solution.py:327
  4.5 1.3 %collective-permute-start = (f32[544]{0:T(1024)S(1)}, f32[544]{0:T(1024)S(1)}, u32[]{:S(2)}, u32[]{:S(2)}) collective-permute-start(f32[544]{0:T(1024)S(1)} %add_convert_fusion), channel_id=1, source_target_pairs={{0,2},{1,3},{2,0},{3,1},{4,6},{5,7},{6,4},{7,5},{8,10},{9,11},{10,... | collective-permute-start | bytes 6536 | tf_op jit(solution)/shard_map/ppermute | solution.py:51
  6.1 1.2 %collective-permute-start.3 = (bf16[4,64,2048]{2,1,0:T(8,128)(2,1)S(1)}, bf16[4,64,2048]{2,1,0:T(8,128)(2,1)S(1)}, u32[]{:S(2)}, u32[]{:S(2)}) collective-permute-start(bf16[4,64,2048]{2,1,0:T(8,128)(2,1)S(1)} %dynamic-slice_multiply_fusion.own), channel_id=1, source_target_pairs={{0,1},{1,0},{2,3},{3,2},{4,5},{5,4},{6,7},{7,6},{8,9},{9,8},{10,11... | collective-permute-start | bytes 3145736 | tf_op jit(solution)/shard_map/ppermute | solution.py:51
  7.4 1.8 %dynamic-slice_multiply_fusion.2 = bf16[4,16,2048]{2,1,0:T(8,128)(2,1)} fusion(bf16[4,128,2048]{2,1,0:T(8,128)(2,1)} %param.7, s32[]{:T(128)S(6)} %select_n.89, bf16[4,16]{1,0:T(4,128)(2,1)S(1)} %constant_dynamic-slice_fusion.2), kind=kLoop, calls=%fused_computation.2 | loop fusion | flops 524288 | bytes 524420 | tf_op jit(solution)/shard_map/mul | solution.py:327
  9.2 1.2 %collective-permute-start.5 = (bf16[4,16,2048]{2,1,0:T(8,128)(2,1)}, bf16[4,16,2048]{2,1,0:T(8,128)(2,1)S(1)}, u32[]{:S(2)}, u32[]{:S(2)}) collective-permute-start(bf16[4,16,2048]{2,1,0:T(8,128)(2,1)} %dynamic-slice_multiply_fusion.2), channel_id=1, source_target_pairs={{0,2},{1,3},{2,0},{3,1},{4,6},{5,7},{6,4},{7,5},{8,10},{9,11},{10,... | collective-permute-start | bytes 786440 | tf_op jit(solution)/shard_map/ppermute | solution.py:51
  10.5 2.2 %collective-permute-done.2.got = bf16[4,16,2048]{2,1,0:T(8,128)(2,1)S(1)} collective-permute-done((bf16[4,16,2048]{2,1,0:T(8,128)(2,1)S(1)}, bf16[4,16,2048]{2,1,0:T(8,128)(2,1)S(1)}, u32[]{:S(2)}, u32[]{:S(2)}) %collective-permute-start.2) | collective-permute-done | bytes 262176 | tf_op jit(solution)/shard_map/ppermute | solution.py:51
  12.7 3.3 %collective-permute-start.4 = (bf16[4,16,2048]{2,1,0:T(8,128)(2,1)S(1)}, bf16[4,16,2048]{2,1,0:T(8,128)(2,1)S(1)}, u32[]{:S(2)}, u32[]{:S(2)}) collective-permute-start(bf16[4,16,2048]{2,1,0:T(8,128)(2,1)S(1)} %collective-permute-done.2.got), channel_id=1, source_target_pairs={{0,1},{1,0},{2,3},{3,2},{4,5},{5,4},{6,7},{7,6},{8,9},{9,8},{10,11... | collective-permute-start | bytes 786440 | tf_op jit(solution)/shard_map/ppermute | solution.py:51
  16.0 2.1 %dynamic-slice_multiply_fusion.1 = bf16[4,32,2048]{2,1,0:T(8,128)(2,1)} fusion(bf16[4,128,2048]{2,1,0:T(8,128)(2,1)} %param.7, s32[]{:T(128)S(6)} %select_n.90, bf16[4,32]{1,0:T(4,128)(2,1)S(1)} %constant_dynamic-slice_fusion.1), kind=kLoop, calls=%fused_computation.1 | loop fusion | flops 1048576 | bytes 1048836 | tf_op jit(solution)/shard_map/mul | solution.py:327
  18.2 3.2 %whiten.3.refs_1_ = bf16[128,2048]{1,0:T(8,128)(2,1)S(1)} custom-call(s32[1]{0:T(128)} %bitcast.7.core, bf16[4,64,2048]{2,1,0:T(8,128)(2,1)S(1)} %dynamic-slice_multiply_fusion.own, bf16[4,16,2048]{2,1,0:T(8,128)(2,1)S(1)} %collective-permute-done.2.got, bf16[4,64,2048]{2,1,0:T(8,128)(2,1)S(1)} %collective-permute-done.3.own_peer, ...), custom_call_target="tpu_custom_call" | custom-call | flops 1024 | bytes 1024 | tf_op jit(solution)/shard_map/whiten/pallas_call | solution.py:143
  22.0 1.0 collective-permute-done.1
  23.3 0.7 copy-done.3
  24.0 3.2 %collective-permute-start.12 = (f32[4,512]{1,0:T(4,128)S(1)}, f32[4,512]{1,0:T(4,128)S(1)}, u32[]{:S(2)}, u32[]{:S(2)}) collective-permute-start(f32[4,512]{1,0:T(4,128)S(1)} %pad_maximum_fusion.1), channel_id=1, source_target_pairs={{4,8},{5,9},{6,10},{7,11},{8,4},{9,5},{10,6},{11,7},{20,24},{21,25... | collective-permute-start | bytes 24584 | tf_op jit(solution)/shard_map/ppermute | solution.py:62
  27.4 1.5 %collective-permute-start.13 = (bf16[128,2048]{1,0:T(8,128)(2,1)S(1)}, bf16[128,2048]{1,0:T(8,128)(2,1)}, u32[]{:S(2)}, u32[]{:S(2)}) collective-permute-start(bf16[128,2048]{1,0:T(8,128)(2,1)S(1)} %whiten.3.refs_1_), channel_id=1, source_target_pairs={{0,4},{1,5},{2,6},{3,7},{4,0},{5,1},{6,2},{7,3},{8,12},{9,13},{10,... | collective-permute-start | bytes 1572872 | tf_op jit(solution)/shard_map/ppermute | solution.py:62
  28.9 2.1 %collective-permute-start.14 = (bf16[128,2048]{1,0:T(8,128)(2,1)S(1)}, bf16[128,2048]{1,0:T(8,128)(2,1)}, u32[]{:S(2)}, u32[]{:S(2)}) collective-permute-start(bf16[128,2048]{1,0:T(8,128)(2,1)S(1)} %whiten.3.refs_1_), channel_id=1, source_target_pairs={{4,8},{5,9},{6,10},{7,11},{8,4},{9,5},{10,6},{11,7},{20,24},{21,25... | collective-permute-start | bytes 1572872 | tf_op jit(solution)/shard_map/ppermute | solution.py:62
  31.0 0.9 copy-done.4
  31.9 2.9 %whiten.4.refs_1_ = bf16[128,2048]{1,0:T(8,128)(2,1)S(1)} custom-call(s32[1]{0:T(128)} %bitcast.7.core, bf16[4,64,2048]{2,1,0:T(8,128)(2,1)S(1)} %dynamic-slice_multiply_fusion.own, bf16[4,16,2048]{2,1,0:T(8,128)(2,1)S(1)} %collective-permute-done.5.got, bf16[4,64,2048]{2,1,0:T(8,128)(2,1)S(1)} %collective-permute-done.3.own_peer, ...), custom_call_target="tpu_custom_call" | custom-call | flops 1024 | bytes 1024 | tf_op jit(solution)/shard_map/whiten/pallas_call | solution.py:143
  34.9 3.2 %collective-permute-start.10 = (bf16[128,2048]{1,0:T(8,128)(2,1)S(1)}, bf16[128,2048]{1,0:T(8,128)(2,1)}, u32[]{:S(2)}, u32[]{:S(2)}) collective-permute-start(bf16[128,2048]{1,0:T(8,128)(2,1)S(1)} %whiten.4.refs_1_), channel_id=1, source_target_pairs={{4,8},{5,9},{6,10},{7,11},{8,4},{9,5},{10,6},{11,7},{20,24},{21,25... | collective-permute-start | bytes 1572872 | tf_op jit(solution)/shard_map/ppermute | solution.py:62
  38.1 1.7 %collective-permute-start.8 = (bf16[4,32,2048]{2,1,0:T(8,128)(2,1)}, bf16[4,32,2048]{2,1,0:T(8,128)(2,1)S(1)}, u32[]{:S(2)}, u32[]{:S(2)}) collective-permute-start(bf16[4,32,2048]{2,1,0:T(8,128)(2,1)} %collective-permute-done.7.got), channel_id=1, source_target_pairs={{0,1},{1,0},{2,3},{3,2},{4,5},{5,4},{6,7},{7,6},{8,9},{9,8},{10,11... | collective-permute-start | bytes 1572872 | tf_op jit(solution)/shard_map/ppermute | solution.py:51
  40.0 1.4 %reshape.81 = f32[12,4,2,4,2,8]{5,4,3,2,1,0:T(2,128)} reshape(f32[3,4,512]{2,1,0:T(4,128)S(1)} %pad_maximum_fusion) | data formatting | bytes 49152 | tf_op jit(solution)/shard_map/reshape | solution.py:353
  41.3 1.0 constant_dynamic-slice_fusion
  42.7 0.8 copy-done.1
  43.5 1.0 copy-done.2
  44.6 4.0 %whiten.5 = (bf16[128,2048]{1,0:T(8,128)(2,1)S(1)}, bf16[128,2048]{1,0:T(8,128)(2,1)S(1)}) custom-call(s32[1]{0:T(128)} %bitcast.7.core, bf16[4,64,2048]{2,1,0:T(8,128)(2,1)S(1)} %dynamic-slice_multiply_fusion.own, bf16[4,32,2048]{2,1,0:T(8,128)(2,1)} %collective-permute-done.7.got, bf16[4,64,2048]{2,1,0:T(8,128)(2,1)} %copy-done, ...), custom_call_target="tpu_custom_call" | custom-call | flops 1024 | bytes 1024 | tf_op jit(solution)/shard_map/whiten/pallas_call | solution.py:143
  48.9 8.3 %cross_stack.5 = (bf16[2,256,512]{2,1,0:T(8,128)(2,1)S(1)}, bf16[2,256,512]{2,1,0:T(8,128)(2,1)}) custom-call(s32[64,2]{1,0:T(8,128)S(1)} %fusion.7.place, s32[64]{0:T(128)S(1)} %get-tuple-element.51.filled, bf16[128,2048]{1,0:T(8,128)(2,1)} %collective-permute-done.13.refs_0_, bf16[128,2048]{1,0:T(8,128)(2,1)S(1)} %whiten.3.refs_1_, ...), custom_call_target="tpu_custom_call" | custom-call | flops 1024 | bytes 1024 | tf_op jit(solution)/shard_map/cross_stack/pallas_call | solution.py:247
  57.3 8.3 %cross_stack.6 = (bf16[2,256,512]{2,1,0:T(8,128)(2,1)S(1)}, bf16[2,256,512]{2,1,0:T(8,128)(2,1)}) custom-call(s32[64,2]{1,0:T(8,128)S(1)} %fusion.7.place, s32[64]{0:T(128)S(1)} %get-tuple-element.51.filled, bf16[128,2048]{1,0:T(8,128)(2,1)S(1)} %collective-permute-done.9.refs_0_, ...), custom_call_target="tpu_custom_call", output_to_operand_aliasing={{0}: (7, {}), {1}: (8, {})} | custom-call | flops 1024 | bytes 1024 | tf_op jit(solution)/shard_map/cross_stack/pallas_call | solution.py:247
  65.5 1.6 %collective-permute-start.20 = (bf16[2,256,512]{2,1,0:T(8,128)(2,1)S(1)}, bf16[2,256,512]{2,1,0:T(8,128)(2,1)S(1)}, u32[]{:S(2)}, u32[]{:S(2)}) collective-permute-start(bf16[2,256,512]{2,1,0:T(8,128)(2,1)S(1)} %get-tuple-element.48), channel_id=1, source_target_pairs={{0,2},{1,3},{2,0},{3,1},{4,6},{5,7},{6,4},{7,5},{8,10},{9,11},{10,... | collective-permute-start | bytes 1572872 | tf_op jit(solution)/shard_map/ppermute | solution.py:51
  67.1 1.9 %collective-permute-start.16 = (bf16[128,2048]{1,0:T(8,128)(2,1)S(1)}, bf16[128,2048]{1,0:T(8,128)(2,1)S(1)}, u32[]{:S(2)}, u32[]{:S(2)}) collective-permute-start(bf16[128,2048]{1,0:T(8,128)(2,1)S(1)} %get-tuple-element.38.refs_1_), channel_id=1, source_target_pairs={{4,8},{5,9},{6,10},{7,11},{8,4},{9,5},{10,6},{11,7},{20,24},{21,25... | collective-permute-start | bytes 1572872 | tf_op jit(solution)/shard_map/ppermute | solution.py:62
  69.0 0.4 collective-permute-start.21
  69.4 9.9 %collective-permute-done.20 = bf16[2,256,512]{2,1,0:T(8,128)(2,1)S(1)} collective-permute-done((bf16[2,256,512]{2,1,0:T(8,128)(2,1)S(1)}, bf16[2,256,512]{2,1,0:T(8,128)(2,1)S(1)}, u32[]{:S(2)}, u32[]{:S(2)}) %collective-permute-start.20) | collective-permute-done | bytes 524320 | tf_op jit(solution)/shard_map/ppermute | solution.py:51
  79.2 0.7 collective-permute-start.22
  80.3 2.1 %collective-permute-start.24 = (bf16[128,2048]{1,0:T(8,128)(2,1)S(1)}, bf16[128,2048]{1,0:T(8,128)(2,1)S(1)}, u32[]{:S(2)}, u32[]{:S(2)}) collective-permute-start(bf16[128,2048]{1,0:T(8,128)(2,1)S(1)} %get-tuple-element.39.refs_1_), channel_id=1, source_target_pairs={{4,8},{5,9},{6,10},{7,11},{8,4},{9,5},{10,6},{11,7},{20,24},{21,25... | collective-permute-start | bytes 1572872 | tf_op jit(solution)/shard_map/ppermute | solution.py:62
  82.4 6.9 %cross_stack.7 = (bf16[1,256,512]{2,1,0:T(8,128)(2,1)}, bf16[1,256,512]{2,1,0:T(8,128)(2,1)S(1)}) custom-call(s32[64,2]{1,0:T(8,128)S(1)} %fusion.7.place, s32[64]{0:T(128)S(1)} %get-tuple-element.51.filled, bf16[128,2048]{1,0:T(8,128)(2,1)S(1)} %collective-permute-done.15.refs_0_, bf16[128,2048]{1,0:T(8,128)(2,1)S(1)} %get-tuple-element.38.refs_1_, ...), custom_call_target="tpu_custom_call" | custom-call | flops 1024 | bytes 1024 | tf_op jit(solution)/shard_map/cross_stack/pallas_call | solution.py:247
  89.4 1.2 %collective-permute-start.17 = (bf16[1,256,512]{2,1,0:T(8,128)(2,1)}, bf16[1,256,512]{2,1,0:T(8,128)(2,1)S(1)}, u32[]{:S(2)}, u32[]{:S(2)}) collective-permute-start(bf16[1,256,512]{2,1,0:T(8,128)(2,1)} %get-tuple-element.47), channel_id=1, source_target_pairs={{0,2},{1,3},{2,0},{3,1},{4,6},{5,7},{6,4},{7,5},{8,10},{9,11},{10,... | collective-permute-start | bytes 786440 | tf_op jit(solution)/shard_map/ppermute | solution.py:51
  90.7 0.4 collective-permute-start.18
  91.0 5.5 %collective-permute-done.17 = bf16[1,256,512]{2,1,0:T(8,128)(2,1)S(1)} collective-permute-done((bf16[1,256,512]{2,1,0:T(8,128)(2,1)}, bf16[1,256,512]{2,1,0:T(8,128)(2,1)S(1)}, u32[]{:S(2)}, u32[]{:S(2)}) %collective-permute-start.17) | collective-permute-done | bytes 262176 | tf_op jit(solution)/shard_map/ppermute | solution.py:51
  96.5 1.8 %collective-permute-start.19 = (bf16[1,256,512]{2,1,0:T(8,128)(2,1)S(1)}, bf16[1,256,512]{2,1,0:T(8,128)(2,1)S(1)}, u32[]{:S(2)}, u32[]{:S(2)}) collective-permute-start(bf16[1,256,512]{2,1,0:T(8,128)(2,1)S(1)} %collective-permute-done.17), channel_id=1, source_target_pairs={{0,1},{1,0},{2,3},{3,2},{4,5},{5,4},{6,7},{7,6},{8,9},{9,8},{10,11... | collective-permute-start | bytes 786440 | tf_op jit(solution)/shard_map/ppermute | solution.py:51
  98.4 4.1 %place_stacks.3.refs_0_ = f32[16,2,64,512]{3,2,1,0:T(8,128)} custom-call(s32[4]{0:T(128)S(1)} %pad_add_fusion.slot, bf16[2,2,128,512]{3,2,1,0:T(8,128)(2,1)} %bitcast.17.r0, bf16[2,2,128,512]{3,2,1,0:T(8,128)(2,1)S(1)} %bitcast.34, bf16[2,2,128,512]{3,2,1,0:T(8,128)(2,1)} %bitcast.19.r2, bf16[2,2,128,512]{3,2,1,0:T(8,128)(2,1)} %bitcast.20.r3), custom_call_target="tpu_custom_call" | custom-call | flops 1024 | bytes 1024 | tf_op jit(solution)/shard_map/place_stacks/pallas_call | solution.py:289
  102.5 4.5 %cross_stack.9 = bf16[1,256,512]{2,1,0:T(8,128)(2,1)S(1)} custom-call(s32[64,2]{1,0:T(8,128)S(1)} %fusion.7.place, s32[64]{0:T(128)S(1)} %get-tuple-element.51.filled, bf16[128,2048]{1,0:T(8,128)(2,1)S(1)} %collective-permute-done.23.refs_0_, bf16[128,2048]{1,0:T(8,128)(2,1)S(1)} %get-tuple-element.39.refs_1_, ...), custom_call_target="tpu_custom_call" | custom-call | flops 1024 | bytes 1024 | tf_op jit(solution)/shard_map/cross_stack/pallas_call | solution.py:247
  107.0 0.8 collective-permute-start.25
  107.8 1.6 %place_stacks.4.refs_0_ = f32[16,2,64,512]{3,2,1,0:T(8,128)} custom-call(s32[4]{0:T(128)S(1)} %pad_add_fusion.slot, bf16[1,2,128,512]{3,2,1,0:T(8,128)(2,1)S(1)} %bitcast.35, bf16[1,2,128,512]{3,2,1,0:T(8,128)(2,1)S(1)} %bitcast.36, bf16[1,2,128,512]{3,2,1,0:T(8,128)(2,1)S(1)} %bitcast.38, ...), custom_call_target="tpu_custom_call", output_to_operand_aliasing={{}: (5, {})} | custom-call | flops 1024 | bytes 1024 | tf_op jit(solution)/shard_map/place_stacks/pallas_call | solution.py:289
  109.4 4.2 %cross_stack.8 = bf16[1,256,512]{2,1,0:T(8,128)(2,1)S(1)} custom-call(s32[64,2]{1,0:T(8,128)S(1)} %fusion.7.place, s32[64]{0:T(128)S(1)} %get-tuple-element.51.filled, bf16[128,2048]{1,0:T(8,128)(2,1)S(1)} %collective-permute-done.23.refs_0_, bf16[128,2048]{1,0:T(8,128)(2,1)S(1)} %get-tuple-element.39.refs_1_, ...), custom_call_target="tpu_custom_call" | custom-call | flops 1024 | bytes 1024 | tf_op jit(solution)/shard_map/cross_stack/pallas_call | solution.py:247
  113.9 1.0 collective-permute-done.25
  115.0 0.8 collective-permute-start.27
  115.8 1.2 collective-permute-done.27
  116.9 1.6 %place_stacks.5 = f32[16,2,64,512]{3,2,1,0:T(8,128)} custom-call(s32[4]{0:T(128)S(1)} %pad_add_fusion.slot, bf16[1,2,128,512]{3,2,1,0:T(8,128)(2,1)S(1)} %bitcast.33, bf16[1,2,128,512]{3,2,1,0:T(8,128)(2,1)S(1)} %bitcast.37, bf16[1,2,128,512]{3,2,1,0:T(8,128)(2,1)S(1)} %bitcast.40, ...), custom_call_target="tpu_custom_call", output_to_operand_aliasing={{}: (5, {})} | custom-call | flops 1024 | bytes 1024 | tf_op jit(solution)/shard_map/place_stacks/pallas_call | solution.py:289
  (63 shorter events, 3.4 us)
Async XLA Ops:
  0.8 17.4 %copy-start.5 = (f32[2,1024]{1,0:T(2,128)S(1)}, f32[2,1024]{1,0:T(2,128)}, u32[]{:S(2)}) copy-start(f32[2,1024]{1,0:T(2,128)} %constant.144.clone.curve) | copy-start | bytes 24580
  4.5 13.6 %collective-permute-start = (f32[544]{0:T(1024)S(1)}, f32[544]{0:T(1024)S(1)}, u32[]{:S(2)}, u32[]{:S(2)}) collective-permute-start(f32[544]{0:T(1024)S(1)} %add_convert_fusion), channel_id=1, source_target_pairs={{0,2},{1,3},{2,0},{3,1},{4,6},{5,7},{6,4},{7,5},{8,10},{9,11},{10,... | collective-permute-start | bytes 6536 | tf_op jit(solution)/shard_map/ppermute | solution.py:51
  5.8 6.9 %collective-permute-start.2 = (bf16[4,16,2048]{2,1,0:T(8,128)(2,1)S(1)}, bf16[4,16,2048]{2,1,0:T(8,128)(2,1)S(1)}, u32[]{:S(2)}, u32[]{:S(2)}) collective-permute-start(bf16[4,16,2048]{2,1,0:T(8,128)(2,1)S(1)} %dynamic-slice_multiply_fusion.3), channel_id=1, source_target_pairs={{0,2},{1,3},{2,0},{3,1},{4,6},{5,7},{6,4},{7,5},{8,10},{9,11},{10,... | collective-permute-start | bytes 786440 | tf_op jit(solution)/shard_map/ppermute | solution.py:51
  6.1 12.1 %collective-permute-start.3 = (bf16[4,64,2048]{2,1,0:T(8,128)(2,1)S(1)}, bf16[4,64,2048]{2,1,0:T(8,128)(2,1)S(1)}, u32[]{:S(2)}, u32[]{:S(2)}) collective-permute-start(bf16[4,64,2048]{2,1,0:T(8,128)(2,1)S(1)} %dynamic-slice_multiply_fusion.own), channel_id=1, source_target_pairs={{0,1},{1,0},{2,3},{3,2},{4,5},{5,4},{6,7},{7,6},{8,9},{9,8},{10,11... | collective-permute-start | bytes 3145736 | tf_op jit(solution)/shard_map/ppermute | solution.py:51
  9.2 12.2 %collective-permute-start.5 = (bf16[4,16,2048]{2,1,0:T(8,128)(2,1)}, bf16[4,16,2048]{2,1,0:T(8,128)(2,1)S(1)}, u32[]{:S(2)}, u32[]{:S(2)}) collective-permute-start(bf16[4,16,2048]{2,1,0:T(8,128)(2,1)} %dynamic-slice_multiply_fusion.2), channel_id=1, source_target_pairs={{0,2},{1,3},{2,0},{3,1},{4,6},{5,7},{6,4},{7,5},{8,10},{9,11},{10,... | collective-permute-start | bytes 786440 | tf_op jit(solution)/shard_map/ppermute | solution.py:51
  12.7 5.5 %collective-permute-start.4 = (bf16[4,16,2048]{2,1,0:T(8,128)(2,1)S(1)}, bf16[4,16,2048]{2,1,0:T(8,128)(2,1)S(1)}, u32[]{:S(2)}, u32[]{:S(2)}) collective-permute-start(bf16[4,16,2048]{2,1,0:T(8,128)(2,1)S(1)} %collective-permute-done.2.got), channel_id=1, source_target_pairs={{0,1},{1,0},{2,3},{3,2},{4,5},{5,4},{6,7},{7,6},{8,9},{9,8},{10,11... | collective-permute-start | bytes 786440 | tf_op jit(solution)/shard_map/ppermute | solution.py:51
  18.1 16.7 %collective-permute-start.7 = (bf16[4,32,2048]{2,1,0:T(8,128)(2,1)}, bf16[4,32,2048]{2,1,0:T(8,128)(2,1)}, u32[]{:S(2)}, u32[]{:S(2)}) collective-permute-start(bf16[4,32,2048]{2,1,0:T(8,128)(2,1)} %dynamic-slice_multiply_fusion.1), channel_id=1, source_target_pairs={{0,2},{1,3},{2,0},{3,1},{4,6},{5,7},{6,4},{7,5},{8,10},{9,11},{10,... | collective-permute-start | bytes 1572872 | tf_op jit(solution)/shard_map/ppermute | solution.py:51
  18.2 12.8 %copy-start = (bf16[4,64,2048]{2,1,0:T(8,128)(2,1)}, bf16[4,64,2048]{2,1,0:T(8,128)(2,1)S(1)}, u32[]{:S(2)}) copy-start(bf16[4,64,2048]{2,1,0:T(8,128)(2,1)S(1)} %collective-permute-done.3.own_peer) | copy-start | bytes 3145732
  21.4 1.9 %collective-permute-start.6 = (bf16[4,16,2048]{2,1,0:T(8,128)(2,1)S(1)}, bf16[4,16,2048]{2,1,0:T(8,128)(2,1)S(1)}, u32[]{:S(2)}, u32[]{:S(2)}) collective-permute-start(bf16[4,16,2048]{2,1,0:T(8,128)(2,1)S(1)} %collective-permute-done.5.got), channel_id=1, source_target_pairs={{0,1},{1,0},{2,3},{3,2},{4,5},{5,4},{6,7},{7,6},{8,9},{9,8},{10,11... | collective-permute-start | bytes 786440 | tf_op jit(solution)/shard_map/ppermute | solution.py:51
  21.7 1.3 %collective-permute-start.1 = (f32[2,544]{1,0:T(2,128)S(1)}, f32[2,544]{1,0:T(2,128)S(1)}, u32[]{:S(2)}, u32[]{:S(2)}) collective-permute-start(f32[2,544]{1,0:T(2,128)S(1)} %pad_maximum_fusion.3), channel_id=1, source_target_pairs={{0,1},{1,0},{2,3},{3,2},{4,5},{5,4},{6,7},{7,6},{8,9},{9,8},{10,11... | collective-permute-start | bytes 13064 | tf_op jit(solution)/shard_map/ppermute | solution.py:51
  23.3 0.7 copy-start.3
  24.0 10.9 %collective-permute-start.12 = (f32[4,512]{1,0:T(4,128)S(1)}, f32[4,512]{1,0:T(4,128)S(1)}, u32[]{:S(2)}, u32[]{:S(2)}) collective-permute-start(f32[4,512]{1,0:T(4,128)S(1)} %pad_maximum_fusion.1), channel_id=1, source_target_pairs={{4,8},{5,9},{6,10},{7,11},{8,4},{9,5},{10,6},{11,7},{20,24},{21,25... | collective-permute-start | bytes 24584 | tf_op jit(solution)/shard_map/ppermute | solution.py:62
  27.2 10.9 %collective-permute-start.11 = (f32[4,512]{1,0:T(4,128)S(1)}, f32[4,512]{1,0:T(4,128)S(1)}, u32[]{:S(2)}, u32[]{:S(2)}) collective-permute-start(f32[4,512]{1,0:T(4,128)S(1)} %pad_maximum_fusion.1), channel_id=1, source_target_pairs={{0,4},{1,5},{2,6},{3,7},{4,0},{5,1},{6,2},{7,3},{8,12},{9,13},{10,... | collective-permute-start | bytes 24584 | tf_op jit(solution)/shard_map/ppermute | solution.py:62
  27.4 21.2 %collective-permute-start.13 = (bf16[128,2048]{1,0:T(8,128)(2,1)S(1)}, bf16[128,2048]{1,0:T(8,128)(2,1)}, u32[]{:S(2)}, u32[]{:S(2)}) collective-permute-start(bf16[128,2048]{1,0:T(8,128)(2,1)S(1)} %whiten.3.refs_1_), channel_id=1, source_target_pairs={{0,4},{1,5},{2,6},{3,7},{4,0},{5,1},{6,2},{7,3},{8,12},{9,13},{10,... | collective-permute-start | bytes 1572872 | tf_op jit(solution)/shard_map/ppermute | solution.py:62
  28.9 19.7 %collective-permute-start.14 = (bf16[128,2048]{1,0:T(8,128)(2,1)S(1)}, bf16[128,2048]{1,0:T(8,128)(2,1)}, u32[]{:S(2)}, u32[]{:S(2)}) collective-permute-start(bf16[128,2048]{1,0:T(8,128)(2,1)S(1)} %whiten.3.refs_1_), channel_id=1, source_target_pairs={{4,8},{5,9},{6,10},{7,11},{8,4},{9,5},{10,6},{11,7},{20,24},{21,25... | collective-permute-start | bytes 1572872 | tf_op jit(solution)/shard_map/ppermute | solution.py:62
  31.0 1.0 copy-start.4
  34.8 22.4 %collective-permute-start.9 = (bf16[128,2048]{1,0:T(8,128)(2,1)S(1)}, bf16[128,2048]{1,0:T(8,128)(2,1)S(1)}, u32[]{:S(2)}, u32[]{:S(2)}) collective-permute-start(bf16[128,2048]{1,0:T(8,128)(2,1)S(1)} %whiten.4.refs_1_), channel_id=1, source_target_pairs={{0,4},{1,5},{2,6},{3,7},{4,0},{5,1},{6,2},{7,3},{8,12},{9,13},{10,... | collective-permute-start | bytes 1572872 | tf_op jit(solution)/shard_map/ppermute | solution.py:62
  34.9 22.3 %collective-permute-start.10 = (bf16[128,2048]{1,0:T(8,128)(2,1)S(1)}, bf16[128,2048]{1,0:T(8,128)(2,1)}, u32[]{:S(2)}, u32[]{:S(2)}) collective-permute-start(bf16[128,2048]{1,0:T(8,128)(2,1)S(1)} %whiten.4.refs_1_), channel_id=1, source_target_pairs={{4,8},{5,9},{6,10},{7,11},{8,4},{9,5},{10,6},{11,7},{20,24},{21,25... | collective-permute-start | bytes 1572872 | tf_op jit(solution)/shard_map/ppermute | solution.py:62
  38.1 4.6 %collective-permute-start.8 = (bf16[4,32,2048]{2,1,0:T(8,128)(2,1)}, bf16[4,32,2048]{2,1,0:T(8,128)(2,1)S(1)}, u32[]{:S(2)}, u32[]{:S(2)}) collective-permute-start(bf16[4,32,2048]{2,1,0:T(8,128)(2,1)} %collective-permute-done.7.got), channel_id=1, source_target_pairs={{0,1},{1,0},{2,3},{3,2},{4,5},{5,4},{6,7},{7,6},{8,9},{9,8},{10,11... | collective-permute-start | bytes 1572872 | tf_op jit(solution)/shard_map/ppermute | solution.py:51
  42.7 0.8 copy-start.1
  43.5 1.0 copy-start.2
  65.5 13.7 %collective-permute-start.20 = (bf16[2,256,512]{2,1,0:T(8,128)(2,1)S(1)}, bf16[2,256,512]{2,1,0:T(8,128)(2,1)S(1)}, u32[]{:S(2)}, u32[]{:S(2)}) collective-permute-start(bf16[2,256,512]{2,1,0:T(8,128)(2,1)S(1)} %get-tuple-element.48), channel_id=1, source_target_pairs={{0,2},{1,3},{2,0},{3,1},{4,6},{5,7},{6,4},{7,5},{8,10},{9,11},{10,... | collective-permute-start | bytes 1572872 | tf_op jit(solution)/shard_map/ppermute | solution.py:51
  67.1 13.2 %collective-permute-start.15 = (bf16[128,2048]{1,0:T(8,128)(2,1)S(1)}, bf16[128,2048]{1,0:T(8,128)(2,1)S(1)}, u32[]{:S(2)}, u32[]{:S(2)}) collective-permute-start(bf16[128,2048]{1,0:T(8,128)(2,1)S(1)} %get-tuple-element.38.refs_1_), channel_id=1, source_target_pairs={{0,4},{1,5},{2,6},{3,7},{4,0},{5,1},{6,2},{7,3},{8,12},{9,13},{10,... | collective-permute-start | bytes 1572872 | tf_op jit(solution)/shard_map/ppermute | solution.py:62
  67.1 15.3 %collective-permute-start.16 = (bf16[128,2048]{1,0:T(8,128)(2,1)S(1)}, bf16[128,2048]{1,0:T(8,128)(2,1)S(1)}, u32[]{:S(2)}, u32[]{:S(2)}) collective-permute-start(bf16[128,2048]{1,0:T(8,128)(2,1)S(1)} %get-tuple-element.38.refs_1_), channel_id=1, source_target_pairs={{4,8},{5,9},{6,10},{7,11},{8,4},{9,5},{10,6},{11,7},{20,24},{21,25... | collective-permute-start | bytes 1572872 | tf_op jit(solution)/shard_map/ppermute | solution.py:62
  69.0 21.6 %collective-permute-start.21 = (bf16[2,256,512]{2,1,0:T(8,128)(2,1)}, bf16[2,256,512]{2,1,0:T(8,128)(2,1)}, u32[]{:S(2)}, u32[]{:S(2)}) collective-permute-start(bf16[2,256,512]{2,1,0:T(8,128)(2,1)} %get-tuple-element.44), channel_id=1, source_target_pairs={{0,1},{1,0},{2,3},{3,2},{4,5},{5,4},{6,7},{7,6},{8,9},{9,8},{10,11... | collective-permute-start | bytes 1572872 | tf_op jit(solution)/shard_map/ppermute | solution.py:51
  79.2 19.1 %collective-permute-start.22 = (bf16[2,256,512]{2,1,0:T(8,128)(2,1)S(1)}, bf16[2,256,512]{2,1,0:T(8,128)(2,1)}, u32[]{:S(2)}, u32[]{:S(2)}) collective-permute-start(bf16[2,256,512]{2,1,0:T(8,128)(2,1)S(1)} %collective-permute-done.20), channel_id=1, source_target_pairs={{0,1},{1,0},{2,3},{3,2},{4,5},{5,4},{6,7},{7,6},{8,9},{9,8},{10,11... | collective-permute-start | bytes 1572872 | tf_op jit(solution)/shard_map/ppermute | solution.py:51
  80.0 22.5 %collective-permute-start.23 = (bf16[128,2048]{1,0:T(8,128)(2,1)S(1)}, bf16[128,2048]{1,0:T(8,128)(2,1)S(1)}, u32[]{:S(2)}, u32[]{:S(2)}) collective-permute-start(bf16[128,2048]{1,0:T(8,128)(2,1)S(1)} %get-tuple-element.39.refs_1_), channel_id=1, source_target_pairs={{0,4},{1,5},{2,6},{3,7},{4,0},{5,1},{6,2},{7,3},{8,12},{9,13},{10,... | collective-permute-start | bytes 1572872 | tf_op jit(solution)/shard_map/ppermute | solution.py:62
  80.3 22.1 %collective-permute-start.24 = (bf16[128,2048]{1,0:T(8,128)(2,1)S(1)}, bf16[128,2048]{1,0:T(8,128)(2,1)S(1)}, u32[]{:S(2)}, u32[]{:S(2)}) collective-permute-start(bf16[128,2048]{1,0:T(8,128)(2,1)S(1)} %get-tuple-element.39.refs_1_), channel_id=1, source_target_pairs={{4,8},{5,9},{6,10},{7,11},{8,4},{9,5},{10,6},{11,7},{20,24},{21,25... | collective-permute-start | bytes 1572872 | tf_op jit(solution)/shard_map/ppermute | solution.py:62
  89.4 7.2 %collective-permute-start.17 = (bf16[1,256,512]{2,1,0:T(8,128)(2,1)}, bf16[1,256,512]{2,1,0:T(8,128)(2,1)S(1)}, u32[]{:S(2)}, u32[]{:S(2)}) collective-permute-start(bf16[1,256,512]{2,1,0:T(8,128)(2,1)} %get-tuple-element.47), channel_id=1, source_target_pairs={{0,2},{1,3},{2,0},{3,1},{4,6},{5,7},{6,4},{7,5},{8,10},{9,11},{10,... | collective-permute-start | bytes 786440 | tf_op jit(solution)/shard_map/ppermute | solution.py:51
  90.7 17.2 %collective-permute-start.18 = (bf16[1,256,512]{2,1,0:T(8,128)(2,1)S(1)}, bf16[1,256,512]{2,1,0:T(8,128)(2,1)S(1)}, u32[]{:S(2)}, u32[]{:S(2)}) collective-permute-start(bf16[1,256,512]{2,1,0:T(8,128)(2,1)S(1)} %get-tuple-element.46), channel_id=1, source_target_pairs={{0,1},{1,0},{2,3},{3,2},{4,5},{5,4},{6,7},{7,6},{8,9},{9,8},{10,11... | collective-permute-start | bytes 786440 | tf_op jit(solution)/shard_map/ppermute | solution.py:51
  96.5 11.3 %collective-permute-start.19 = (bf16[1,256,512]{2,1,0:T(8,128)(2,1)S(1)}, bf16[1,256,512]{2,1,0:T(8,128)(2,1)S(1)}, u32[]{:S(2)}, u32[]{:S(2)}) collective-permute-start(bf16[1,256,512]{2,1,0:T(8,128)(2,1)S(1)} %collective-permute-done.17), channel_id=1, source_target_pairs={{0,1},{1,0},{2,3},{3,2},{4,5},{5,4},{6,7},{7,6},{8,9},{9,8},{10,11... | collective-permute-start | bytes 786440 | tf_op jit(solution)/shard_map/ppermute | solution.py:51
  107.0 8.0 %collective-permute-start.25 = (bf16[1,256,512]{2,1,0:T(8,128)(2,1)S(1)}, bf16[1,256,512]{2,1,0:T(8,128)(2,1)S(1)}, u32[]{:S(2)}, u32[]{:S(2)}) collective-permute-start(bf16[1,256,512]{2,1,0:T(8,128)(2,1)S(1)} %cross_stack.9), channel_id=1, source_target_pairs={{0,2},{1,3},{2,0},{3,1},{4,6},{5,7},{6,4},{7,5},{8,10},{9,11},{10,... | collective-permute-start | bytes 786440 | tf_op jit(solution)/shard_map/ppermute | solution.py:51
  113.6 2.2 %collective-permute-start.26 = (bf16[1,256,512]{2,1,0:T(8,128)(2,1)S(1)}, bf16[1,256,512]{2,1,0:T(8,128)(2,1)S(1)}, u32[]{:S(2)}, u32[]{:S(2)}) collective-permute-start(bf16[1,256,512]{2,1,0:T(8,128)(2,1)S(1)} %cross_stack.8), channel_id=1, source_target_pairs={{0,1},{1,0},{2,3},{3,2},{4,5},{5,4},{6,7},{7,6},{8,9},{9,8},{10,11... | collective-permute-start | bytes 786440 | tf_op jit(solution)/shard_map/ppermute | solution.py:51
  115.0 1.9 %collective-permute-start.27 = (bf16[1,256,512]{2,1,0:T(8,128)(2,1)S(1)}, bf16[1,256,512]{2,1,0:T(8,128)(2,1)S(1)}, u32[]{:S(2)}, u32[]{:S(2)}) collective-permute-start(bf16[1,256,512]{2,1,0:T(8,128)(2,1)S(1)} %collective-permute-done.25), channel_id=1, source_target_pairs={{0,1},{1,0},{2,3},{3,2},{4,5},{5,4},{6,7},{7,6},{8,9},{9,8},{10,11... | collective-permute-start | bytes 786440 | tf_op jit(solution)/shard_map/ppermute | solution.py:51

commit v3 on v2

--- a/solution.py
+++ b/solution.py
@@ -13,11 +13,16 @@
 QUAD = 4
 CHANS = 8
 STEP = 256
+WHITEN_US, CROSS_US, PLACE_US = 2, 3.2, 1.5
 VMEM_BYTES = 50 << 20
 MASKS = (0, 2, 1, 3)
 
 SMEM = pl.BlockSpec(memory_space=pltpu.SMEM)
 ANY = pl.BlockSpec(memory_space=pl.ANY)
+
+
+def cost(us):
+    return pl.CostEstimate(flops=int(us * 1e9), bytes_accessed=1024, transcendentals=0)
 
 
 def bin_order(bins):
@@ -46,12 +51,13 @@
     return table.astype(np.float32).astype(jnp.bfloat16)
 
 
-def to_quad_peer(value, mask):
+def to_quad_peer(value, mask, name):
     count = lax.axis_size("chan")
-    return lax.ppermute(value, "chan", [(s, s ^ mask) for s in range(count)])
-
-
-def swap_quads(value, odd):
+    with jax.named_scope(name):
+        return lax.ppermute(value, "chan", [(s, s ^ mask) for s in range(count)])
+
+
+def swap_quads(value, odd, name):
     count = lax.axis_size("chan")
     pairs = []
     for s in range(count):
@@ -59,25 +65,27 @@
         other = s + QUAD if quad % 2 == odd else s - QUAD
         if 0 <= other < count:
             pairs.append((s, other))
-    return lax.ppermute(value, "chan", pairs)
+    with jax.named_scope(name):
+        return lax.ppermute(value, "chan", pairs)
 
 
 def after(value, *others):
     return lax.optimization_barrier((value,) + others)[0]
 
 
-def whiten_kernel(chunks, first, core, own, got, own_peer, got_peer, curve, basis, *refs):
+def whiten_kernel(chunks, first, meta, own, got, own_peer, got_peer, curve, basis, *refs):
     outs = refs[:chunks]
-    raw, table, hann, re_s, im_s, amp_s, result, sems, out_sem = refs[chunks:]
+    raw, raw_got, table, hann, re_s, im_s, amp_s, result, sems, out_sem = refs[chunks:]
     windows, both = raw.shape[1:3]
     half = raw.shape[3] // 2
     steps = basis.shape[0]
     bins = steps * STEP
+    here = pl.ds(pl.multiple_of(meta[1] + first, 16), both)
     copies = [
-        pltpu.make_async_copy(own.at[:, pl.ds(first, both)], raw.at[0], sems.at[0]),
-        pltpu.make_async_copy(got, raw.at[1], sems.at[1]),
-        pltpu.make_async_copy(own_peer.at[:, pl.ds(first, both)], raw.at[2], sems.at[2]),
-        pltpu.make_async_copy(got_peer, raw.at[3], sems.at[3]),
+        pltpu.make_async_copy(own.at[:, here], raw.at[0], sems.at[0]),
+        pltpu.make_async_copy(got.at[pl.ds(0, windows * both)], raw_got.at[0], sems.at[1]),
+        pltpu.make_async_copy(own_peer.at[:, here], raw.at[1], sems.at[2]),
+        pltpu.make_async_copy(got_peer.at[pl.ds(0, windows * both)], raw_got.at[1], sems.at[3]),
         pltpu.make_async_copy(curve, hann, sems.at[4]),
     ]
     tables = [
@@ -88,15 +96,18 @@
         copy.start()
     for copy in copies:
         copy.wait()
-    low = core[0] == 0
+    low = meta[0] == 0
     sums, gaps = [], []
     for c in range(chunks):
         low_at = slice(2 * c * CHANS, (2 * c + 1) * CHANS)
         high_at = slice((2 * c + 1) * CHANS, (2 * c + 2) * CHANS)
         for r in range(QUAD):
             for w in range(windows):
-                left = raw[r, w, :, 0:half].astype(jnp.float32)
-                right = raw[r, w, :, half:].astype(jnp.float32)
+                if r % 2:
+                    whole = raw_got[r // 2, pl.ds(w * both, both), :].astype(jnp.float32)
+                else:
+                    whole = raw[r // 2, w].astype(jnp.float32)
+                left, right = whole[:, :half], whole[:, half:]
                 left = jnp.where(low, left[low_at], left[high_at]) * hann[0:1, :]
                 right = jnp.where(low, right[low_at], right[high_at]) * hann[1:2, :]
                 sums.append(left + right)
@@ -134,9 +145,9 @@
         write.wait()
 
 
-def whiten(first, core, own, got, own_peer, got_peer, hann, basis):
-    windows, both, width = got.shape
-    chunks = both // (2 * CHANS)
+def whiten(first, chunks, meta, own, got, own_peer, got_peer, hann, basis):
+    windows, _, width = own.shape
+    both = chunks * 2 * CHANS
     rows = QUAD * windows * CHANS
     total = chunks * rows
     bins = width // 2
@@ -146,7 +157,8 @@
         in_specs=[SMEM] + [ANY] * 6,
         out_specs=[ANY] * chunks,
         scratch_shapes=[
-            pltpu.VMEM((QUAD, windows, both, width), jnp.bfloat16),
+            pltpu.VMEM((2, windows, both, width), jnp.bfloat16),
+            pltpu.VMEM((2, windows * both, width), jnp.bfloat16),
             pltpu.VMEM(basis.shape, jnp.bfloat16),
             pltpu.VMEM(hann.shape, jnp.float32),
             pltpu.VMEM((total, bins), jnp.float32),
@@ -157,31 +169,49 @@
             pltpu.SemaphoreType.DMA((chunks,)),
         ],
         compiler_params=pltpu.CompilerParams(vmem_limit_bytes=VMEM_BYTES),
-        cost_estimate=pl.CostEstimate(flops=1024, bytes_accessed=1024, transcendentals=0),
+        cost_estimate=cost(WHITEN_US * chunks),
         name="whiten",
-    )(core, own, got, own_peer, got_peer, hann, basis)
-
-
-def cross_kernel(sides, chunk, spot, windows, place, filled, *refs):
+    )(meta, own, got, own_peer, got_peer, hann, basis)
+
+
+def cross_kernel(sides, chunk, windows, meta, place, filled, *refs):
     count = len(sides)
     blocks, flags, lagmap = refs[:3], refs[3], refs[4]
-    outs = refs[-count - 8 : -8]
-    raw, live, near, cross, table, result, sems, out_sems = refs[-8:]
+    outs = refs[-count - 9 : -9]
+    raw, held, live, near, cross, table, result, sems, out_sems = refs[-9:]
     width = near.shape[-1]
     bins = width // 2
     pairs = place.shape[0] // 2
     copies = [pltpu.make_async_copy(b, raw.at[i], sems.at[i]) for i, b in enumerate(blocks)]
-    copies.append(pltpu.make_async_copy(flags.at[chunk], live, sems.at[3]))
+    copies.insert(0, pltpu.make_async_copy(flags, held, sems.at[3]))
     load = pltpu.make_async_copy(lagmap, table, sems.at[4])
     for copy in copies:
         copy.start()
     load.start()
     for i, copy in enumerate(copies):
         copy.wait()
-        if i < 3:
-            near[pl.ds(i * QUAD, QUAD)] = (
-                raw[i].astype(jnp.float32).reshape(QUAD, windows, CHANS, width)
+        if i == 0:
+            shape = (CHANS, held.shape[1])
+            first = meta[1] + meta[0] * CHANS + chunk * 2 * CHANS
+            pick = lax.broadcasted_iota(jnp.int32, shape, 1) == first + lax.broadcasted_iota(
+                jnp.int32, shape, 0
             )
+            picked = lax.dot_general(
+                jnp.where(pick, 1.0, 0.0).astype(jnp.bfloat16),
+                held[...],
+                (((1,), (1,)), ((), ())),
+                preferred_element_type=jnp.float32,
+            )
+            for k in range(held.shape[0]):
+                live[k // windows, k % windows] = jnp.broadcast_to(
+                    picked[:, k : k + 1], (CHANS, 128)
+                )
+            continue
+        wide = raw[i - 1].astype(jnp.float32).reshape(QUAD, windows, CHANS, width)
+        for r in range(QUAD):
+            for w in range(windows):
+                flag = live[(i - 1) * QUAD + r, w][:, 0:1]
+                near[(i - 1) * QUAD + r, w] = wide[r, w] * flag
 
     def one(p):
         a, b = near.at[place[p, 0]], near.at[place[p, 1]]
@@ -232,27 +262,26 @@
             table[...],
             preferred_element_type=jnp.float32,
         ).astype(jnp.bfloat16)
-        write = pltpu.make_async_copy(result.at[n], outs[n].at[spot], out_sems.at[n])
+        write = pltpu.make_async_copy(result.at[n], outs[n].at[0], out_sems.at[n])
         write.start()
         writes.append(write)
     for write in writes:
         write.wait()
 
 
-def cross_stack(sides, chunk, spot, depth, place, filled, blocks, flags, lagmap, held):
+def cross_stack(sides, chunk, windows, meta, place, filled, blocks, flags, lagmap):
     count = len(sides)
     pairs = place.shape[0] // 2
     rows, width = blocks[0].shape
-    windows = flags.shape[2]
     return pl.pallas_call(
-        functools.partial(cross_kernel, sides, chunk, spot, windows),
-        out_shape=[jax.ShapeDtypeStruct((depth, pairs * CHANS, LAGS), jnp.bfloat16)] * count,
-        in_specs=[SMEM, SMEM] + [ANY] * (5 + len(held)),
+        functools.partial(cross_kernel, sides, chunk, windows),
+        out_shape=[jax.ShapeDtypeStruct((1, pairs * CHANS, LAGS), jnp.bfloat16)] * count,
+        in_specs=[SMEM] * 3 + [ANY] * 5,
         out_specs=[ANY] * count,
-        input_output_aliases={7 + n: n for n in range(len(held))},
         scratch_shapes=[
             pltpu.VMEM((3, rows, width), jnp.bfloat16),
-            pltpu.VMEM(flags.shape[1:], jnp.float32),
+            pltpu.VMEM(flags.shape, jnp.bfloat16),
+            pltpu.VMEM((3 * QUAD, windows, CHANS, 128), jnp.float32),
             pltpu.VMEM((3 * QUAD, windows, CHANS, width), jnp.float32),
             pltpu.VMEM((pairs * CHANS // 16, 16, width), jnp.bfloat16),
             pltpu.VMEM((width, LAGS), jnp.bfloat16),
@@ -261,9 +290,9 @@
             pltpu.SemaphoreType.DMA((count,)),
         ],
         compiler_params=pltpu.CompilerParams(vmem_limit_bytes=VMEM_BYTES),
-        cost_estimate=pl.CostEstimate(flops=1024, bytes_accessed=1024, transcendentals=0),
+        cost_estimate=cost(CROSS_US * count),
         name="cross_stack",
-    )(place, filled, *blocks, flags, lagmap, *held)
+    )(meta, place, filled, *blocks, flags, lagmap)
 
 
 def place_kernel(slot, r0, r1, r2, r3, *refs):
@@ -299,7 +328,7 @@
         ),
         input_output_aliases={5: 0} if extra else {},
         compiler_params=pltpu.CompilerParams(vmem_limit_bytes=VMEM_BYTES),
-        cost_estimate=pl.CostEstimate(flops=1024, bytes_accessed=1024, transcendentals=0),
+        cost_estimate=cost(PLACE_US * depth),
         name="place_stacks",
     )(slot, *parts, *extra)
 
@@ -315,49 +344,43 @@
     mine = here % QUAD
     quad = here // QUAD
     chip = mine // 2
-    core = (mine % 2).reshape(1).astype(jnp.int32)
+    meta = jnp.stack([mine % 2, chip * half]).astype(jnp.int32)
     basis = jnp.asarray(make_basis(width, bins))
     hann = jnp.asarray(make_hann(width))
     lagmap = jnp.asarray(make_lagmap(width, bins, LAGS))
-    live = dead[None, :] * glitch
-    live_wire = live.astype(jnp.bfloat16)[..., None]
-
     def cut(at, count):
-        raw = lax.dynamic_slice_in_dim(records, at, count, 1)
-        return raw * lax.dynamic_slice_in_dim(live_wire, at, count, 1)
+        return lax.dynamic_slice_in_dim(records, at, count, 1).reshape(-1, width)
 
     there = (1 - chip) * half
-    notes = jnp.concatenate([live.reshape(-1), pairs.reshape(-1)]).astype(jnp.float32)
-    send, at = lax.optimization_barrier((cut(there, wide), chip * half))
-    got = [to_quad_peer(send, 2)]
-    own, there = lax.optimization_barrier((cut(at, half), there))
-    own_peer = to_quad_peer(own, 1)
-    notes, there = lax.optimization_barrier((notes, there))
-    send, there = lax.optimization_barrier((cut(there + wide, wide), there))
-    got.append(to_quad_peer(send, 2))
-    notes = jnp.stack([notes, to_quad_peer(notes, 2)])
-    got.append(to_quad_peer(cut(there + 2 * wide, half - 2 * wide), 2))
-    got_peer = [to_quad_peer(got[0], 1)]
-    notes = jnp.concatenate([notes, to_quad_peer(notes, 1)])
-
-    white = []
-    for c in range(3):
-        if c:
-            got_peer.append(to_quad_peer(after(got[c], white[-1]), 1))
-        white += whiten(c * wide, core, own, got[c], own_peer, got_peer[c], hann, basis)
-    near = [(swap_quads(w, 0), w, swap_quads(w, 1)) for w in white]
-
-    flags = notes[:, : windows * block]
-    sent = after(flags, got_peer[1])
-    flags = jnp.stack([swap_quads(sent, 0), flags, swap_quads(sent, 1)])
-    flags = flags.reshape(3 * QUAD, windows, 2, chunks, 2, CHANS)
-    flags = lax.dynamic_index_in_dim(flags, chip, 2, False)
-    flags = lax.dynamic_index_in_dim(flags, core[0], 3, False)
-    flags = jnp.broadcast_to(
-        flags.transpose(2, 0, 1, 3)[..., None], (chunks, 3 * QUAD, windows, CHANS, 128)
-    )
-
-    listed = notes[:, windows * block :].astype(jnp.int32).reshape(2, 2, slots, 2)
+    send, there = lax.optimization_barrier((cut(there, wide), there))
+    got = [to_quad_peer(send, 2, "Y0_")]
+    own_peer = to_quad_peer(records, 1, "CA_")
+    live = after((dead[None, :] * glitch).astype(jnp.bfloat16).reshape(-1), send)
+    notes = jnp.concatenate([swap_quads(live, 0, "NE_"), live, swap_quads(live, 1, "NO_")])
+    notes = jnp.concatenate([notes, pairs.reshape(-1).astype(jnp.bfloat16)])
+    size = notes.shape[0]
+    page = jnp.pad(notes, (0, 16 * width - size)).reshape(16, width)
+    got.append(to_quad_peer(jnp.concatenate([cut(there + wide, wide), page]), 2, "Y1_"))
+    got.append(to_quad_peer(cut(there + 2 * wide, half - 2 * wide), 2, "Y2_"))
+    white, near, got_peer = [], [], []
+
+    def whiten_next(c, count, *earlier):
+        got_peer.append(to_quad_peer(after(got[c], *earlier), 1, f"CB{c}_"))
+        for w in whiten(c * wide, count, meta, records, got[c], own_peer, got_peer[c], hann, basis):
+            n = len(white)
+            near.append((swap_quads(w, 0, f"Z{n}E_"), w, swap_quads(w, 1, f"Z{n}O_")))
+            white.append(w)
+
+    whiten_next(0, 1)
+    whiten_next(1, 1, white[0])
+    notes_peer = to_quad_peer(after(notes, white[1]), 1, "NC_")
+    whiten_next(2, chunks - 2, white[1])
+    notes = [notes, got[1][-16:].reshape(-1)[:size], notes_peer, got_peer[1][-16:].reshape(-1)[:size]]
+    notes = jnp.stack(notes)
+    flags = notes[:, : 3 * windows * block].reshape(QUAD, 3, windows, block).swapaxes(0, 1)
+    flags = flags.reshape(-1, block)
+
+    listed = notes[:, 3 * windows * block :].astype(jnp.int32).reshape(2, 2, slots, 2)
     listed = listed.swapaxes(0, 1)[::-1].reshape(-1, 2)
     filled = (listed[..., 0] >= 0) & (listed[..., 1] >= 0)
     inside = (listed % QUAD) ^ mine
@@ -368,27 +391,31 @@
     slot = jnp.stack([mine ^ m for m in MASKS]).astype(jnp.int32)
     shape = (slots, 2, half, LAGS)
 
-    def cross(sides, c, spot, depth, place, held=()):
-        return cross_stack(
-            sides, c, spot, depth, place, filled, near[c], flags, lagmap, tuple(held)
+    def cross(sides, c, place):
+        return cross_stack(sides, c, windows, meta, place, filled, near[c], flags, lagmap)
+
+    def returned(home, away, name):
+        return (
+            home,
+            away,
+            to_quad_peer(home, 1, "H" + name),
+            to_quad_peer(away, 1, "F" + name),
         )
 
-    def returned(home, away):
-        return (home, away, to_quad_peer(home, 1), to_quad_peer(away, 1))
-
+    held, sent = None, None
     place = after(place, *white)
-    both = cross((0, 1), 0, 0, 2, place)
-    away, home = cross((0, 1), 1, 1, 2, place, both)
-    parts = returned(home, to_quad_peer(away, 2))
-    away, home = cross((0, 1), 2, 0, 1, after(place, home))
-    away = to_quad_peer(away, 2)
-    held = place_stacks(0, slot, parts, None, shape)
-    parts = returned(home, away)
-    (away,) = cross((0,), 3, 0, 1, after(place, home, held))
-    away = to_quad_peer(away, 2)
-    held = place_stacks(2, slot, parts, held, shape)
-    (home,) = cross((1,), 3, 0, 1, after(place, held))
-    held = place_stacks(3, slot, returned(home, away), held, shape)
+    for c in range(chunks - 1):
+        away, home = cross((0, 1), c, place)
+        if sent:
+            held = place_stacks(c - 1, slot, returned(*after(sent, home), str(c - 1) + "_"), held, shape)
+        place = after(place, home if held is None else held)
+        sent = (home, to_quad_peer(away, 2, f"R{c}_"))
+    c = chunks - 1
+    (away,) = cross((0,), c, place)
+    held = place_stacks(c - 1, slot, returned(*after(sent, away), str(c - 1) + "_"), held, shape)
+    away = to_quad_peer(away, 2, f"R{c}_")
+    (home,) = cross((1,), c, after(place, held))
+    held = place_stacks(c, slot, returned(home, away, str(c) + "_"), held, shape)
     return held.reshape(slots, block, LAGS)
 
 

time: 120 us -> 109 us (0.908)
  waiting for transfers between devices: 21.1 us -> 13 us
  other arithmetic: 7.7 us -> 2.41 us
  starting transfers between devices: 31.7 us -> 27.9 us
  local copies, waits for them, and re-layouts: 8.02 us -> 11.1 us
  Pallas kernels: 49.5 us -> 51.7 us
    ppermute x18 -> x20, waiting for transfers between devices: 20.8 us -> 13 us  [to_quad_peer(): return lax.ppermute(value, 'chan', [(s, s ^ mask) for s in range(count)])]
    mul x4 -> x0, other arithmetic: 6.78 us -> none  [cut(): return raw * lax.dynamic_slice_in_dim(live_wire, at, count, 1)]
    ppermute x18 -> x20, starting transfers between devices: 17.7 us -> 11.9 us  [to_quad_peer(): return lax.ppermute(value, 'chan', [(s, s ^ mask) for s in range(count)])]
    unnamed x13 -> x27, local copies, waits for them, and re-layouts: 4.27 us -> 7.25 us
    ppermute x10, starting transfers between devices: 14.1 us -> 16 us  [swap_quads(): return lax.ppermute(value, 'chan', pairs)]
    dynamic_slice x2 -> x3, local copies, waits for them, and re-layouts: 1.2 us -> 2.98 us  [cut(): return lax.dynamic_slice_in_dim(records, at, count, 1).reshape(-1, width)]
    pallas_call x3, Pallas kernels: 10.1 us -> 11.7 us  [whiten(): pl.pallas_call(functools.partial(whiten_kernel, chunks, first), out_shape...]
    reshape x3, local copies, waits for them, and re-layouts: 1.55 us -> 0.06 us  [the longest x1 0.03 us: body(): page = jnp.pad(notes, (0, 16 * width - size)).reshape(16, width)]
  transfers between devices with their start and end apart: 28 -> 30, of which waited for: 7 -> 11; matrix products, arithmetic and copies ran while one was open for 6% -> 7% of each run, Pallas kernels for 33% -> 47%
where the time goes in v3:
time: 109 us; the launch traced here: 107 us
  Pallas kernels  51.7 us (47%)
  starting transfers between devices  27.9 us (26%)
  waiting for transfers between devices  13 us (12%)
  local copies, waits for them, and re-layouts  11.1 us (10%)
  other arithmetic  2.41 us (2%)
    pallas_call x5, Pallas kernels, cross_stack(): pl.pallas_call(functools.partial(cross_kernel, sides, chunk, windows), ou...  32.8 us
    ppermute x10, starting transfers between devices, swap_quads(): return lax.ppermute(value, 'chan', pairs)  16 us
    ppermute x20, waiting for transfers between devices, to_quad_peer(): return lax.ppermute(value, 'chan', [(s, s ^ mask) for s in range(count)])  13 us
    ppermute x20, starting transfers between devices, to_quad_peer(): return lax.ppermute(value, 'chan', [(s, s ^ mask) for s in range(count)])  11.9 us
    pallas_call x3, Pallas kernels, whiten(): pl.pallas_call(functools.partial(whiten_kernel, chunks, first), out_shape...  11.7 us
    unnamed x27, local copies, waits for them, and re-layouts  7.25 us
    pallas_call x4, Pallas kernels, place_stacks(): pl.pallas_call(place_kernel, out_shape=jax.ShapeDtypeStruct(shape, jnp.fl...  7.16 us
    dynamic_slice x3, local copies, waits for them, and re-layouts, cut(): return lax.dynamic_slice_in_dim(records, at, count, 1).reshape(-1, width)  2.98 us
  transfers between devices with their start and end apart: 30, of which 11 were waited for; matrix products, arithmetic and copies ran while one was open for 7% of the time, Pallas kernels for 47%

profile of v3, /device:TPU:11, one launch (start us, length us, event | category | flops | bytes accessed | tf_op | source)
XLA Modules:
  0.0 106.5 jit_solution(238076726680521490)
XLA Ops:
  0.0 0.7 collective-permute-start.3
  0.7 1.0 constant_dynamic-slice_fusion.2
  1.6 1.3 %collective-permute-start.4 = (bf16[64,2048]{1,0:T(8,128)(2,1)S(1)}, bf16[64,2048]{1,0:T(8,128)(2,1)S(1)}, u32[]{:S(2)}, u32[]{:S(2)}) collective-permute-start(bf16[64,2048]{1,0:T(8,128)(2,1)S(1)} %bitcast.64), channel_id=1, source_target_pairs={{0,2},{1,3},{2,0},{3,1},{4,6},{5,7},{6,4},{7,5},{8,10},{9,11},{10,... | collective-permute-start | bytes 786440 | tf_op jit(solution)/shard_map/Y0_/ppermute | solution.py:57
  3.0 0.7 fusion.16
  3.8 4.3 %collective-permute-start.1 = (bf16[512]{0:T(512)(128)(2,1)S(1)}, bf16[512]{0:T(512)(128)(2,1)S(1)}, u32[]{:S(2)}, u32[]{:S(2)}) collective-permute-start(bf16[512]{0:T(512)(128)(2,1)S(1)} %fusion.16), channel_id=1, source_target_pairs={{4,8},{5,9},{6,10},{7,11},{8,4},{9,5},{10,6},{11,7},{20,24},{21,25... | collective-permute-start | bytes 3080 | tf_op jit(solution)/shard_map/NO_/ppermute | solution.py:69
  8.1 1.1 %constant_dynamic-slice_fusion.1 = bf16[4,16,2048]{2,1,0:T(8,128)(2,1)S(1)} fusion(bf16[4,128,2048]{2,1,0:T(8,128)(2,1)} %own.5, s32[]{:T(128)S(6)} %select_n.61), kind=kLoop, calls=%fused_computation.39 | loop fusion | bytes 524292 | tf_op jit(solution)/shard_map/dynamic_slice | solution.py:352
  9.2 0.7 convert_element_type.16
  11.1 0.9 collective-permute-start.5
  12.0 0.7 pad_maximum_fusion
  13.1 1.6 %copy-done = bf16[4,128,2048]{2,1,0:T(8,128)(2,1)S(1)} copy-done((bf16[4,128,2048]{2,1,0:T(8,128)(2,1)S(1)}, bf16[4,128,2048]{2,1,0:T(8,128)(2,1)}, u32[]{:S(2)}) %copy-start) | copy-done | bytes 2097176
  14.7 0.7 copy-done.4
  15.4 3.5 %whiten.3.refs_1_ = bf16[128,2048]{1,0:T(8,128)(2,1)S(1)} custom-call(s32[2]{0:T(128)S(1)} %pad_add_fusion.1.meta, bf16[4,128,2048]{2,1,0:T(8,128)(2,1)S(1)} %copy-done, bf16[64,2048]{1,0:T(8,128)(2,1)S(1)} %collective-permute-done.4.got, bf16[4,128,2048]{2,1,0:T(8,128)(2,1)} %collective-permute-done.3.own_peer, ...), custom_call_target="tpu_custom_call" | custom-call | flops 2000000000 | bytes 1024 | tf_op jit(solution)/shard_map/whiten/pallas_call | solution.py:154
  19.0 3.3 %collective-permute-done.2.got = bf16[80,2048]{1,0:T(8,128)(2,1)S(1)} collective-permute-done((bf16[80,2048]{1,0:T(8,128)(2,1)}, bf16[80,2048]{1,0:T(8,128)(2,1)S(1)}, u32[]{:S(2)}, u32[]{:S(2)}) %collective-permute-start.2) | collective-permute-done | bytes 327712 | tf_op jit(solution)/shard_map/Y1_/ppermute | solution.py:57
  22.3 0.8 collective-permute-start.6
  23.1 0.9 constant_dynamic-slice_fusion
  24.4 4.0 %collective-permute-start.11 = (bf16[128,2048]{1,0:T(8,128)(2,1)S(1)}, bf16[128,2048]{1,0:T(8,128)(2,1)}, u32[]{:S(2)}, u32[]{:S(2)}) collective-permute-start(bf16[128,2048]{1,0:T(8,128)(2,1)S(1)} %whiten.3.refs_1_), channel_id=1, source_target_pairs={{4,8},{5,9},{6,10},{7,11},{8,4},{9,5},{10,6},{11,7},{20,24},{21,25... | collective-permute-start | bytes 1572872 | tf_op jit(solution)/shard_map/Z0O_/ppermute | solution.py:69
  28.3 0.7 copy-done.2
  29.1 1.0 copy-done.3
  30.0 3.5 %whiten.4.refs_1_ = bf16[128,2048]{1,0:T(8,128)(2,1)S(1)} custom-call(s32[2]{0:T(128)S(1)} %pad_add_fusion.1.meta, bf16[4,128,2048]{2,1,0:T(8,128)(2,1)S(1)} %copy-done.1, bf16[80,2048]{1,0:T(8,128)(2,1)S(1)} %collective-permute-done.2.got, bf16[4,128,2048]{2,1,0:T(8,128)(2,1)} %collective-permute-done.3.own_peer, bf16[80,2048]{1,0:T(8,128)(2,1)S(1)} %copy-done.3, ...), custom_call_target="tpu_custom_call" | custom-call | flops 2000000000 | bytes 1024 | tf_op jit(solution)/shard_map/whiten/pallas_call | solution.py:154
  33.6 0.9 collective-permute-start.7
  34.6 3.3 %collective-permute-done.8.got = bf16[128,2048]{1,0:T(8,128)(2,1)} collective-permute-done((bf16[128,2048]{1,0:T(8,128)(2,1)}, bf16[128,2048]{1,0:T(8,128)(2,1)}, u32[]{:S(2)}, u32[]{:S(2)}) %collective-permute-start.8) | collective-permute-done | bytes 524320 | tf_op jit(solution)/shard_map/Y2_/ppermute | solution.py:57
  37.9 2.7 %collective-permute-start.14 = (bf16[128,2048]{1,0:T(8,128)(2,1)S(1)}, bf16[128,2048]{1,0:T(8,128)(2,1)}, u32[]{:S(2)}, u32[]{:S(2)}) collective-permute-start(bf16[128,2048]{1,0:T(8,128)(2,1)S(1)} %whiten.4.refs_1_), channel_id=1, source_target_pairs={{4,8},{5,9},{6,10},{7,11},{8,4},{9,5},{10,6},{11,7},{20,24},{21,25... | collective-permute-start | bytes 1572872 | tf_op jit(solution)/shard_map/Z1O_/ppermute | solution.py:69
  40.5 1.1 %collective-permute-start.9 = (bf16[128,2048]{1,0:T(8,128)(2,1)}, bf16[128,2048]{1,0:T(8,128)(2,1)S(1)}, u32[]{:S(2)}, u32[]{:S(2)}) collective-permute-start(bf16[128,2048]{1,0:T(8,128)(2,1)} %collective-permute-done.8.got), channel_id=1, source_target_pairs={{0,1},{1,0},{2,3},{3,2},{4,5},{5,4},{6,7},{7,6},{8,9},{9,8},{10,11... | collective-permute-start | bytes 1572872 | tf_op jit(solution)/shard_map/CB2_/ppermute | solution.py:57
  42.3 1.2 %collective-permute-done.9.got_peer = bf16[128,2048]{1,0:T(8,128)(2,1)S(1)} collective-permute-done((bf16[128,2048]{1,0:T(8,128)(2,1)}, bf16[128,2048]{1,0:T(8,128)(2,1)S(1)}, u32[]{:S(2)}, u32[]{:S(2)}) %collective-permute-start.9) | collective-permute-done | bytes 524320 | tf_op jit(solution)/shard_map/CB2_/ppermute | solution.py:57
  43.4 0.8 copy-done.6
  44.2 1.0 copy-done.7
  45.3 4.7 %whiten.5 = (bf16[128,2048]{1,0:T(8,128)(2,1)S(1)}, bf16[128,2048]{1,0:T(8,128)(2,1)S(1)}) custom-call(s32[2]{0:T(128)S(1)} %pad_add_fusion.1.meta, bf16[4,128,2048]{2,1,0:T(8,128)(2,1)} %own.5, bf16[128,2048]{1,0:T(8,128)(2,1)} %collective-permute-done.8.got, bf16[4,128,2048]{2,1,0:T(8,128)(2,1)} %collective-permute-done.3.own_peer, ...), custom_call_target="tpu_custom_call" | custom-call | flops 4000000000 | bytes 1024 | tf_op jit(solution)/shard_map/whiten/pallas_call | solution.py:154
  50.1 2.6 %collective-permute-start.19 = (bf16[128,2048]{1,0:T(8,128)(2,1)S(1)}, bf16[128,2048]{1,0:T(8,128)(2,1)}, u32[]{:S(2)}, u32[]{:S(2)}) collective-permute-start(bf16[128,2048]{1,0:T(8,128)(2,1)S(1)} %get-tuple-element.36.refs_1_), channel_id=1, source_target_pairs={{4,8},{5,9},{6,10},{7,11},{8,4},{9,5},{10,6},{11,7},{20,24},{21,25... | collective-permute-start | bytes 1572872 | tf_op jit(solution)/shard_map/Z2O_/ppermute | solution.py:69
  52.7 7.9 %cross_stack.5 = (bf16[1,256,512]{2,1,0:T(8,128)(2,1)S(1)}, bf16[1,256,512]{2,1,0:T(8,128)(2,1)S(1)}) custom-call(s32[2]{0:T(128)S(1)} %pad_add_fusion.1.meta, s32[64,2]{1,0:T(8,128)S(1)} %fusion.7.place, s32[64]{0:T(128)S(1)} %get-tuple-element.55.filled, bf16[128,2048]{1,0:T(8,128)(2,1)} %collective-permute-done.10.refs_0_, ...), custom_call_target="tpu_custom_call" | custom-call | flops 6400000000 | bytes 1024 | tf_op jit(solution)/shard_map/cross_stack/pallas_call | solution.py:276
  60.9 7.7 %cross_stack.6 = (bf16[1,256,512]{2,1,0:T(8,128)(2,1)S(1)}, bf16[1,256,512]{2,1,0:T(8,128)(2,1)S(1)}) custom-call(s32[2]{0:T(128)S(1)} %pad_add_fusion.1.meta, s32[64,2]{1,0:T(8,128)S(1)} %fusion.7.place, s32[64]{0:T(128)S(1)} %get-tuple-element.55.filled, bf16[128,2048]{1,0:T(8,128)(2,1)S(1)} %collective-permute-done.13.refs_0_, ...), custom_call_target="tpu_custom_call" | custom-call | flops 6400000000 | bytes 1024 | tf_op jit(solution)/shard_map/cross_stack/pallas_call | solution.py:276
  68.5 0.7 copy-done.8
  69.3 1.0 collective-permute-start.15
  70.3 1.4 %collective-permute-done.15 = bf16[1,256,512]{2,1,0:T(8,128)(2,1)S(1)} collective-permute-done((bf16[1,256,512]{2,1,0:T(8,128)(2,1)S(1)}, bf16[1,256,512]{2,1,0:T(8,128)(2,1)S(1)}, u32[]{:S(2)}, u32[]{:S(2)}) %collective-permute-start.15) | collective-permute-done | bytes 262176 | tf_op jit(solution)/shard_map/H0_/ppermute | solution.py:57
  71.7 2.1 %collective-permute-start.24 = (bf16[128,2048]{1,0:T(8,128)(2,1)S(1)}, bf16[128,2048]{1,0:T(8,128)(2,1)S(1)}, u32[]{:S(2)}, u32[]{:S(2)}) collective-permute-start(bf16[128,2048]{1,0:T(8,128)(2,1)S(1)} %get-tuple-element.37.refs_1_), channel_id=1, source_target_pairs={{4,8},{5,9},{6,10},{7,11},{8,4},{9,5},{10,6},{11,7},{20,24},{21,25... | collective-permute-start | bytes 1572872 | tf_op jit(solution)/shard_map/Z3O_/ppermute | solution.py:69
  73.8 1.3 %collective-permute-start.17 = (bf16[1,256,512]{2,1,0:T(8,128)(2,1)}, bf16[1,256,512]{2,1,0:T(8,128)(2,1)S(1)}, u32[]{:S(2)}, u32[]{:S(2)}) collective-permute-start(bf16[1,256,512]{2,1,0:T(8,128)(2,1)} %copy-done.8), channel_id=1, source_target_pairs={{0,2},{1,3},{2,0},{3,1},{4,6},{5,7},{6,4},{7,5},{8,10},{9,11},{10,... | collective-permute-start | bytes 786440 | tf_op jit(solution)/shard_map/R1_/ppermute | solution.py:57
  75.1 2.4 %place_stacks.4.refs_0_ = f32[16,2,64,512]{3,2,1,0:T(8,128)} custom-call(s32[4]{0:T(128)S(1)} %pad_add_fusion.slot, bf16[1,2,128,512]{3,2,1,0:T(8,128)(2,1)S(1)} %bitcast.60, bf16[1,2,128,512]{3,2,1,0:T(8,128)(2,1)} %bitcast.16.r1, bf16[1,2,128,512]{3,2,1,0:T(8,128)(2,1)S(1)} %bitcast.61, bf16[1,2,128,512]{3,2,1,0:T(8,128)(2,1)S(1)} %bitcast.62), custom_call_target="tpu_custom_call" | custom-call | flops 1500000000 | bytes 1024 | tf_op jit(solution)/shard_map/place_stacks/pallas_call | solution.py:318
  77.5 7.9 %cross_stack.7 = (bf16[1,256,512]{2,1,0:T(8,128)(2,1)S(1)}, bf16[1,256,512]{2,1,0:T(8,128)(2,1)S(1)}) custom-call(s32[2]{0:T(128)S(1)} %pad_add_fusion.1.meta, s32[64,2]{1,0:T(8,128)S(1)} %fusion.7.place, s32[64]{0:T(128)S(1)} %get-tuple-element.55.filled, bf16[128,2048]{1,0:T(8,128)(2,1)} %collective-permute-done.18.refs_0_, ...), custom_call_target="tpu_custom_call" | custom-call | flops 6400000000 | bytes 1024 | tf_op jit(solution)/shard_map/cross_stack/pallas_call | solution.py:276
  85.4 0.8 collective-permute-start.20
  86.5 0.9 collective-permute-done.20
  87.8 1.6 %place_stacks.5.refs_0_ = f32[16,2,64,512]{3,2,1,0:T(8,128)} custom-call(s32[4]{0:T(128)S(1)} %pad_add_fusion.slot, bf16[1,2,128,512]{3,2,1,0:T(8,128)(2,1)S(1)} %bitcast.43, bf16[1,2,128,512]{3,2,1,0:T(8,128)(2,1)S(1)} %bitcast.46, bf16[1,2,128,512]{3,2,1,0:T(8,128)(2,1)S(1)} %bitcast.49, ...), custom_call_target="tpu_custom_call", output_to_operand_aliasing={{}: (5, {})} | custom-call | flops 1500000000 | bytes 1024 | tf_op jit(solution)/shard_map/place_stacks/pallas_call | solution.py:318
  89.4 4.7 %cross_stack.8 = bf16[1,256,512]{2,1,0:T(8,128)(2,1)S(1)} custom-call(s32[2]{0:T(128)S(1)} %pad_add_fusion.1.meta, s32[64,2]{1,0:T(8,128)S(1)} %fusion.7.place, s32[64]{0:T(128)S(1)} %get-tuple-element.55.filled, bf16[128,2048]{1,0:T(8,128)(2,1)S(1)} %collective-permute-done.23.refs_0_, bf16[128,2048]{1,0:T(8,128)(2,1)S(1)} %get-tuple-element.37.refs_1_, ...), custom_call_target="tpu_custom_call" | custom-call | flops 3200000000 | bytes 1024 | tf_op jit(solution)/shard_map/cross_stack/pallas_call | solution.py:276
  94.0 1.0 collective-permute-start.25
  95.3 0.9 collective-permute-done.25
  96.6 1.6 %place_stacks.6.refs_0_ = f32[16,2,64,512]{3,2,1,0:T(8,128)} custom-call(s32[4]{0:T(128)S(1)} %pad_add_fusion.slot, bf16[1,2,128,512]{3,2,1,0:T(8,128)(2,1)S(1)} %bitcast.44, bf16[1,2,128,512]{3,2,1,0:T(8,128)(2,1)S(1)} %bitcast.45, bf16[1,2,128,512]{3,2,1,0:T(8,128)(2,1)S(1)} %bitcast.51, ...), custom_call_target="tpu_custom_call", output_to_operand_aliasing={{}: (5, {})} | custom-call | flops 1500000000 | bytes 1024 | tf_op jit(solution)/shard_map/place_stacks/pallas_call | solution.py:318
  98.2 4.8 %cross_stack.9 = bf16[1,256,512]{2,1,0:T(8,128)(2,1)S(1)} custom-call(s32[2]{0:T(128)S(1)} %pad_add_fusion.1.meta, s32[64,2]{1,0:T(8,128)S(1)} %fusion.7.place, s32[64]{0:T(128)S(1)} %get-tuple-element.55.filled, bf16[128,2048]{1,0:T(8,128)(2,1)S(1)} %collective-permute-done.23.refs_0_, bf16[128,2048]{1,0:T(8,128)(2,1)S(1)} %get-tuple-element.37.refs_1_, ...), custom_call_target="tpu_custom_call" | custom-call | flops 3200000000 | bytes 1024 | tf_op jit(solution)/shard_map/cross_stack/pallas_call | solution.py:276
  102.9 0.4 collective-permute-start.28
  103.8 0.8 collective-permute-done.28
  104.9 1.6 %place_stacks.7 = f32[16,2,64,512]{3,2,1,0:T(8,128)} custom-call(s32[4]{0:T(128)S(1)} %pad_add_fusion.slot, bf16[1,2,128,512]{3,2,1,0:T(8,128)(2,1)S(1)} %bitcast.48, bf16[1,2,128,512]{3,2,1,0:T(8,128)(2,1)S(1)} %bitcast.47, bf16[1,2,128,512]{3,2,1,0:T(8,128)(2,1)S(1)} %bitcast.50, ...), custom_call_target="tpu_custom_call", output_to_operand_aliasing={{}: (5, {})} | custom-call | flops 1500000000 | bytes 1024 | tf_op jit(solution)/shard_map/place_stacks/pallas_call | solution.py:318
  (82 shorter events, 5.2 us)
Async XLA Ops:
  0.0 13.1 %collective-permute-start.3 = (bf16[4,128,2048]{2,1,0:T(8,128)(2,1)}, bf16[4,128,2048]{2,1,0:T(8,128)(2,1)}, u32[]{:S(2)}, u32[]{:S(2)}) collective-permute-start(bf16[4,128,2048]{2,1,0:T(8,128)(2,1)} %own.5), channel_id=1, source_target_pairs={{0,1},{1,0},{2,3},{3,2},{4,5},{5,4},{6,7},{7,6},{8,9},{9,8},{10,11... | collective-permute-start | bytes 6291464 | tf_op jit(solution)/shard_map/CA_/ppermute | solution.py:57
  1.6 9.4 %collective-permute-start.4 = (bf16[64,2048]{1,0:T(8,128)(2,1)S(1)}, bf16[64,2048]{1,0:T(8,128)(2,1)S(1)}, u32[]{:S(2)}, u32[]{:S(2)}) collective-permute-start(bf16[64,2048]{1,0:T(8,128)(2,1)S(1)} %bitcast.64), channel_id=1, source_target_pairs={{0,2},{1,3},{2,0},{3,1},{4,6},{5,7},{6,4},{7,5},{8,10},{9,11},{10,... | collective-permute-start | bytes 786440 | tf_op jit(solution)/shard_map/Y0_/ppermute | solution.py:57
  3.6 6.5 %collective-permute-start = (bf16[512]{0:T(512)(128)(2,1)S(1)}, bf16[512]{0:T(512)(128)(2,1)S(1)}, u32[]{:S(2)}, u32[]{:S(2)}) collective-permute-start(bf16[512]{0:T(512)(128)(2,1)S(1)} %fusion.16), channel_id=1, source_target_pairs={{0,4},{1,5},{2,6},{3,7},{4,0},{5,1},{6,2},{7,3},{8,12},{9,13},{10,... | collective-permute-start | bytes 3080 | tf_op jit(solution)/shard_map/NE_/ppermute | solution.py:69
  3.8 6.8 %collective-permute-start.1 = (bf16[512]{0:T(512)(128)(2,1)S(1)}, bf16[512]{0:T(512)(128)(2,1)S(1)}, u32[]{:S(2)}, u32[]{:S(2)}) collective-permute-start(bf16[512]{0:T(512)(128)(2,1)S(1)} %fusion.16), channel_id=1, source_target_pairs={{4,8},{5,9},{6,10},{7,11},{8,4},{9,5},{10,6},{11,7},{20,24},{21,25... | collective-permute-start | bytes 3080 | tf_op jit(solution)/shard_map/NO_/ppermute | solution.py:69
  11.1 2.1 %collective-permute-start.5 = (bf16[64,2048]{1,0:T(8,128)(2,1)S(1)}, bf16[64,2048]{1,0:T(8,128)(2,1)S(1)}, u32[]{:S(2)}, u32[]{:S(2)}) collective-permute-start(bf16[64,2048]{1,0:T(8,128)(2,1)S(1)} %collective-permute-done.4.got), channel_id=1, source_target_pairs={{0,1},{1,0},{2,3},{3,2},{4,5},{5,4},{6,7},{7,6},{8,9},{9,8},{10,11... | collective-permute-start | bytes 786440 | tf_op jit(solution)/shard_map/CB0_/ppermute | solution.py:57
  12.7 9.5 %collective-permute-start.2 = (bf16[80,2048]{1,0:T(8,128)(2,1)}, bf16[80,2048]{1,0:T(8,128)(2,1)S(1)}, u32[]{:S(2)}, u32[]{:S(2)}) collective-permute-start(bf16[80,2048]{1,0:T(8,128)(2,1)} %pad_maximum_fusion), channel_id=1, source_target_pairs={{0,2},{1,3},{2,0},{3,1},{4,6},{5,7},{6,4},{7,5},{8,10},{9,11},{10,... | collective-permute-start | bytes 983048 | tf_op jit(solution)/shard_map/Y1_/ppermute | solution.py:57
  13.1 1.6 %copy-start = (bf16[4,128,2048]{2,1,0:T(8,128)(2,1)S(1)}, bf16[4,128,2048]{2,1,0:T(8,128)(2,1)}, u32[]{:S(2)}) copy-start(bf16[4,128,2048]{2,1,0:T(8,128)(2,1)} %own.5) | copy-start | bytes 6291460
  14.7 0.7 copy-start.4
  15.4 13.6 %copy-start.1 = (bf16[4,128,2048]{2,1,0:T(8,128)(2,1)S(1)}, bf16[4,128,2048]{2,1,0:T(8,128)(2,1)}, u32[]{:S(2)}) copy-start(bf16[4,128,2048]{2,1,0:T(8,128)(2,1)} %own.5) | copy-start | bytes 6291460
  15.4 13.6 %copy-start.5 = (f32[2,1024]{1,0:T(2,128)S(1)}, f32[2,1024]{1,0:T(2,128)}, u32[]{:S(2)}) copy-start(f32[2,1024]{1,0:T(2,128)} %constant.110.clone.curve) | copy-start | bytes 24580
  22.3 6.1 %collective-permute-start.6 = (bf16[80,2048]{1,0:T(8,128)(2,1)S(1)}, bf16[80,2048]{1,0:T(8,128)(2,1)S(1)}, u32[]{:S(2)}, u32[]{:S(2)}) collective-permute-start(bf16[80,2048]{1,0:T(8,128)(2,1)S(1)} %collective-permute-done.2.got), channel_id=1, source_target_pairs={{0,1},{1,0},{2,3},{3,2},{4,5},{5,4},{6,7},{7,6},{8,9},{9,8},{10,11... | collective-permute-start | bytes 983048 | tf_op jit(solution)/shard_map/CB1_/ppermute | solution.py:57
  24.0 13.9 %collective-permute-start.8 = (bf16[128,2048]{1,0:T(8,128)(2,1)}, bf16[128,2048]{1,0:T(8,128)(2,1)}, u32[]{:S(2)}, u32[]{:S(2)}) collective-permute-start(bf16[128,2048]{1,0:T(8,128)(2,1)} %bitcast.11), channel_id=1, source_target_pairs={{0,2},{1,3},{2,0},{3,1},{4,6},{5,7},{6,4},{7,5},{8,10},{9,11},{10,... | collective-permute-start | bytes 1572872 | tf_op jit(solution)/shard_map/Y2_/ppermute | solution.py:57
  24.3 25.8 %collective-permute-start.10 = (bf16[128,2048]{1,0:T(8,128)(2,1)S(1)}, bf16[128,2048]{1,0:T(8,128)(2,1)}, u32[]{:S(2)}, u32[]{:S(2)}) collective-permute-start(bf16[128,2048]{1,0:T(8,128)(2,1)S(1)} %whiten.3.refs_1_), channel_id=1, source_target_pairs={{0,4},{1,5},{2,6},{3,7},{4,0},{5,1},{6,2},{7,3},{8,12},{9,13},{10,... | collective-permute-start | bytes 1572872 | tf_op jit(solution)/shard_map/Z0E_/ppermute | solution.py:69
  24.4 28.3 %collective-permute-start.11 = (bf16[128,2048]{1,0:T(8,128)(2,1)S(1)}, bf16[128,2048]{1,0:T(8,128)(2,1)}, u32[]{:S(2)}, u32[]{:S(2)}) collective-permute-start(bf16[128,2048]{1,0:T(8,128)(2,1)S(1)} %whiten.3.refs_1_), channel_id=1, source_target_pairs={{4,8},{5,9},{6,10},{7,11},{8,4},{9,5},{10,6},{11,7},{20,24},{21,25... | collective-permute-start | bytes 1572872 | tf_op jit(solution)/shard_map/Z0O_/ppermute | solution.py:69
  28.3 0.7 copy-start.2
  29.1 1.0 copy-start.3
  33.5 27.3 %collective-permute-start.13 = (bf16[128,2048]{1,0:T(8,128)(2,1)S(1)}, bf16[128,2048]{1,0:T(8,128)(2,1)S(1)}, u32[]{:S(2)}, u32[]{:S(2)}) collective-permute-start(bf16[128,2048]{1,0:T(8,128)(2,1)S(1)} %whiten.4.refs_1_), channel_id=1, source_target_pairs={{0,4},{1,5},{2,6},{3,7},{4,0},{5,1},{6,2},{7,3},{8,12},{9,13},{10,... | collective-permute-start | bytes 1572872 | tf_op jit(solution)/shard_map/Z1E_/ppermute | solution.py:69
  33.6 6.9 %collective-permute-start.7 = (bf16[1568]{0:T(1024)(128)(2,1)S(1)}, bf16[1568]{0:T(1024)(128)(2,1)S(1)}, u32[]{:S(2)}, u32[]{:S(2)}) collective-permute-start(bf16[1568]{0:T(1024)(128)(2,1)S(1)} %dynamic-update-slice.3), channel_id=1, source_target_pairs={{0,1},{1,0},{2,3},{3,2},{4,5},{5,4},{6,7},{7,6},{8,9},{9,8},{10,11... | collective-permute-start | bytes 9416 | tf_op jit(solution)/shard_map/NC_/ppermute | solution.py:57
  37.9 23.0 %collective-permute-start.14 = (bf16[128,2048]{1,0:T(8,128)(2,1)S(1)}, bf16[128,2048]{1,0:T(8,128)(2,1)}, u32[]{:S(2)}, u32[]{:S(2)}) collective-permute-start(bf16[128,2048]{1,0:T(8,128)(2,1)S(1)} %whiten.4.refs_1_), channel_id=1, source_target_pairs={{4,8},{5,9},{6,10},{7,11},{8,4},{9,5},{10,6},{11,7},{20,24},{21,25... | collective-permute-start | bytes 1572872 | tf_op jit(solution)/shard_map/Z1O_/ppermute | solution.py:69
  40.5 2.9 %collective-permute-start.9 = (bf16[128,2048]{1,0:T(8,128)(2,1)}, bf16[128,2048]{1,0:T(8,128)(2,1)S(1)}, u32[]{:S(2)}, u32[]{:S(2)}) collective-permute-start(bf16[128,2048]{1,0:T(8,128)(2,1)} %collective-permute-done.8.got), channel_id=1, source_target_pairs={{0,1},{1,0},{2,3},{3,2},{4,5},{5,4},{6,7},{7,6},{8,9},{9,8},{10,11... | collective-permute-start | bytes 1572872 | tf_op jit(solution)/shard_map/CB2_/ppermute | solution.py:57
  43.4 0.8 copy-start.6
  44.2 1.0 copy-start.7
  50.0 27.5 %collective-permute-start.18 = (bf16[128,2048]{1,0:T(8,128)(2,1)S(1)}, bf16[128,2048]{1,0:T(8,128)(2,1)}, u32[]{:S(2)}, u32[]{:S(2)}) collective-permute-start(bf16[128,2048]{1,0:T(8,128)(2,1)S(1)} %get-tuple-element.36.refs_1_), channel_id=1, source_target_pairs={{0,4},{1,5},{2,6},{3,7},{4,0},{5,1},{6,2},{7,3},{8,12},{9,13},{10,... | collective-permute-start | bytes 1572872 | tf_op jit(solution)/shard_map/Z2E_/ppermute | solution.py:69
  50.1 27.4 %collective-permute-start.19 = (bf16[128,2048]{1,0:T(8,128)(2,1)S(1)}, bf16[128,2048]{1,0:T(8,128)(2,1)}, u32[]{:S(2)}, u32[]{:S(2)}) collective-permute-start(bf16[128,2048]{1,0:T(8,128)(2,1)S(1)} %get-tuple-element.36.refs_1_), channel_id=1, source_target_pairs={{4,8},{5,9},{6,10},{7,11},{8,4},{9,5},{10,6},{11,7},{20,24},{21,25... | collective-permute-start | bytes 1572872 | tf_op jit(solution)/shard_map/Z2O_/ppermute | solution.py:69
  60.6 8.7 %collective-permute-start.12 = (bf16[1,256,512]{2,1,0:T(8,128)(2,1)S(1)}, bf16[1,256,512]{2,1,0:T(8,128)(2,1)}, u32[]{:S(2)}, u32[]{:S(2)}) collective-permute-start(bf16[1,256,512]{2,1,0:T(8,128)(2,1)S(1)} %get-tuple-element.41), channel_id=1, source_target_pairs={{0,2},{1,3},{2,0},{3,1},{4,6},{5,7},{6,4},{7,5},{8,10},{9,11},{10,... | collective-permute-start | bytes 786440 | tf_op jit(solution)/shard_map/R0_/ppermute | solution.py:57
  68.5 0.7 copy-start.8
  69.3 2.5 %collective-permute-start.15 = (bf16[1,256,512]{2,1,0:T(8,128)(2,1)S(1)}, bf16[1,256,512]{2,1,0:T(8,128)(2,1)S(1)}, u32[]{:S(2)}, u32[]{:S(2)}) collective-permute-start(bf16[1,256,512]{2,1,0:T(8,128)(2,1)S(1)} %get-tuple-element.43), channel_id=1, source_target_pairs={{0,1},{1,0},{2,3},{3,2},{4,5},{5,4},{6,7},{7,6},{8,9},{9,8},{10,11... | collective-permute-start | bytes 786440 | tf_op jit(solution)/shard_map/H0_/ppermute | solution.py:57
  70.2 3.6 %collective-permute-start.16 = (bf16[1,256,512]{2,1,0:T(8,128)(2,1)}, bf16[1,256,512]{2,1,0:T(8,128)(2,1)S(1)}, u32[]{:S(2)}, u32[]{:S(2)}) collective-permute-start(bf16[1,256,512]{2,1,0:T(8,128)(2,1)} %collective-permute-done.12), channel_id=1, source_target_pairs={{0,1},{1,0},{2,3},{3,2},{4,5},{5,4},{6,7},{7,6},{8,9},{9,8},{10,11... | collective-permute-start | bytes 786440 | tf_op jit(solution)/shard_map/F0_/ppermute | solution.py:57
  70.3 19.1 %collective-permute-start.23 = (bf16[128,2048]{1,0:T(8,128)(2,1)S(1)}, bf16[128,2048]{1,0:T(8,128)(2,1)S(1)}, u32[]{:S(2)}, u32[]{:S(2)}) collective-permute-start(bf16[128,2048]{1,0:T(8,128)(2,1)S(1)} %get-tuple-element.37.refs_1_), channel_id=1, source_target_pairs={{0,4},{1,5},{2,6},{3,7},{4,0},{5,1},{6,2},{7,3},{8,12},{9,13},{10,... | collective-permute-start | bytes 1572872 | tf_op jit(solution)/shard_map/Z3E_/ppermute | solution.py:69
  71.7 17.6 %collective-permute-start.24 = (bf16[128,2048]{1,0:T(8,128)(2,1)S(1)}, bf16[128,2048]{1,0:T(8,128)(2,1)S(1)}, u32[]{:S(2)}, u32[]{:S(2)}) collective-permute-start(bf16[128,2048]{1,0:T(8,128)(2,1)S(1)} %get-tuple-element.37.refs_1_), channel_id=1, source_target_pairs={{4,8},{5,9},{6,10},{7,11},{8,4},{9,5},{10,6},{11,7},{20,24},{21,25... | collective-permute-start | bytes 1572872 | tf_op jit(solution)/shard_map/Z3O_/ppermute | solution.py:69
  73.8 11.5 %collective-permute-start.17 = (bf16[1,256,512]{2,1,0:T(8,128)(2,1)}, bf16[1,256,512]{2,1,0:T(8,128)(2,1)S(1)}, u32[]{:S(2)}, u32[]{:S(2)}) collective-permute-start(bf16[1,256,512]{2,1,0:T(8,128)(2,1)} %copy-done.8), channel_id=1, source_target_pairs={{0,2},{1,3},{2,0},{3,1},{4,6},{5,7},{6,4},{7,5},{8,10},{9,11},{10,... | collective-permute-start | bytes 786440 | tf_op jit(solution)/shard_map/R1_/ppermute | solution.py:57
  85.4 2.0 %collective-permute-start.20 = (bf16[1,256,512]{2,1,0:T(8,128)(2,1)S(1)}, bf16[1,256,512]{2,1,0:T(8,128)(2,1)S(1)}, u32[]{:S(2)}, u32[]{:S(2)}) collective-permute-start(bf16[1,256,512]{2,1,0:T(8,128)(2,1)S(1)} %get-tuple-element.48), channel_id=1, source_target_pairs={{0,1},{1,0},{2,3},{3,2},{4,5},{5,4},{6,7},{7,6},{8,9},{9,8},{10,11... | collective-permute-start | bytes 786440 | tf_op jit(solution)/shard_map/H1_/ppermute | solution.py:57
  86.2 1.5 %collective-permute-start.21 = (bf16[1,256,512]{2,1,0:T(8,128)(2,1)S(1)}, bf16[1,256,512]{2,1,0:T(8,128)(2,1)S(1)}, u32[]{:S(2)}, u32[]{:S(2)}) collective-permute-start(bf16[1,256,512]{2,1,0:T(8,128)(2,1)S(1)} %collective-permute-done.17), channel_id=1, source_target_pairs={{0,1},{1,0},{2,3},{3,2},{4,5},{5,4},{6,7},{7,6},{8,9},{9,8},{10,11... | collective-permute-start | bytes 786440 | tf_op jit(solution)/shard_map/F1_/ppermute | solution.py:57
  86.3 7.7 %collective-permute-start.22 = (bf16[1,256,512]{2,1,0:T(8,128)(2,1)S(1)}, bf16[1,256,512]{2,1,0:T(8,128)(2,1)S(1)}, u32[]{:S(2)}, u32[]{:S(2)}) collective-permute-start(bf16[1,256,512]{2,1,0:T(8,128)(2,1)S(1)} %get-tuple-element.51), channel_id=1, source_target_pairs={{0,2},{1,3},{2,0},{3,1},{4,6},{5,7},{6,4},{7,5},{8,10},{9,11},{10,... | collective-permute-start | bytes 786440 | tf_op jit(solution)/shard_map/R2_/ppermute | solution.py:57
  87.8 1.6 %copy-start.9 = (bf16[2048,512]{1,0:T(8,128)(2,1)S(1)}, bf16[2048,512]{1,0:T(8,128)(2,1)}, u32[]{:S(2)}) copy-start(bf16[2048,512]{1,0:T(8,128)(2,1)} %constant.111.clone.refs_4_) | copy-start | bytes 6291460
  94.0 2.2 %collective-permute-start.25 = (bf16[1,256,512]{2,1,0:T(8,128)(2,1)S(1)}, bf16[1,256,512]{2,1,0:T(8,128)(2,1)S(1)}, u32[]{:S(2)}, u32[]{:S(2)}) collective-permute-start(bf16[1,256,512]{2,1,0:T(8,128)(2,1)S(1)} %get-tuple-element.52), channel_id=1, source_target_pairs={{0,1},{1,0},{2,3},{3,2},{4,5},{5,4},{6,7},{7,6},{8,9},{9,8},{10,11... | collective-permute-start | bytes 786440 | tf_op jit(solution)/shard_map/H2_/ppermute | solution.py:57
  95.0 1.5 %collective-permute-start.26 = (bf16[1,256,512]{2,1,0:T(8,128)(2,1)S(1)}, bf16[1,256,512]{2,1,0:T(8,128)(2,1)S(1)}, u32[]{:S(2)}, u32[]{:S(2)}) collective-permute-start(bf16[1,256,512]{2,1,0:T(8,128)(2,1)S(1)} %collective-permute-done.22), channel_id=1, source_target_pairs={{0,1},{1,0},{2,3},{3,2},{4,5},{5,4},{6,7},{7,6},{8,9},{9,8},{10,11... | collective-permute-start | bytes 786440 | tf_op jit(solution)/shard_map/F2_/ppermute | solution.py:57
  95.0 8.4 %collective-permute-start.27 = (bf16[1,256,512]{2,1,0:T(8,128)(2,1)S(1)}, bf16[1,256,512]{2,1,0:T(8,128)(2,1)S(1)}, u32[]{:S(2)}, u32[]{:S(2)}) collective-permute-start(bf16[1,256,512]{2,1,0:T(8,128)(2,1)S(1)} %cross_stack.8), channel_id=1, source_target_pairs={{0,2},{1,3},{2,0},{3,1},{4,6},{5,7},{6,4},{7,5},{8,10},{9,11},{10,... | collective-permute-start | bytes 786440 | tf_op jit(solution)/shard_map/R3_/ppermute | solution.py:57
  102.9 1.6 %collective-permute-start.28 = (bf16[1,256,512]{2,1,0:T(8,128)(2,1)S(1)}, bf16[1,256,512]{2,1,0:T(8,128)(2,1)S(1)}, u32[]{:S(2)}, u32[]{:S(2)}) collective-permute-start(bf16[1,256,512]{2,1,0:T(8,128)(2,1)S(1)} %cross_stack.9), channel_id=1, source_target_pairs={{0,1},{1,0},{2,3},{3,2},{4,5},{5,4},{6,7},{7,6},{8,9},{9,8},{10,11... | collective-permute-start | bytes 786440 | tf_op jit(solution)/shard_map/H3_/ppermute | solution.py:57
  103.4 1.5 %collective-permute-start.29 = (bf16[1,256,512]{2,1,0:T(8,128)(2,1)S(1)}, bf16[1,256,512]{2,1,0:T(8,128)(2,1)S(1)}, u32[]{:S(2)}, u32[]{:S(2)}) collective-permute-start(bf16[1,256,512]{2,1,0:T(8,128)(2,1)S(1)} %collective-permute-done.27), channel_id=1, source_target_pairs={{0,1},{1,0},{2,3},{3,2},{4,5},{5,4},{6,7},{7,6},{8,9},{9,8},{10,11... | collective-permute-start | bytes 786440 | tf_op jit(solution)/shard_map/F3_/ppermute | solution.py:57

commit v4 on v3

--- a/solution.py
+++ b/solution.py
@@ -80,12 +80,13 @@
     half = raw.shape[3] // 2
     steps = basis.shape[0]
     bins = steps * STEP
+    part = both // 2
     here = pl.ds(pl.multiple_of(meta[1] + first, 16), both)
     copies = [
         pltpu.make_async_copy(own.at[:, here], raw.at[0], sems.at[0]),
-        pltpu.make_async_copy(got.at[pl.ds(0, windows * both)], raw_got.at[0], sems.at[1]),
+        pltpu.make_async_copy(got.at[pl.ds(0, windows * part)], raw_got.at[0], sems.at[1]),
         pltpu.make_async_copy(own_peer.at[:, here], raw.at[1], sems.at[2]),
-        pltpu.make_async_copy(got_peer.at[pl.ds(0, windows * both)], raw_got.at[1], sems.at[3]),
+        pltpu.make_async_copy(got_peer.at[pl.ds(0, windows * part)], raw_got.at[1], sems.at[3]),
         pltpu.make_async_copy(curve, hann, sems.at[4]),
     ]
     tables = [
@@ -98,18 +99,19 @@
         copy.wait()
     low = meta[0] == 0
     sums, gaps = [], []
+    wide = [x.astype(jnp.float32) for x in (raw_got[0], raw_got[1])]
     for c in range(chunks):
-        low_at = slice(2 * c * CHANS, (2 * c + 1) * CHANS)
-        high_at = slice((2 * c + 1) * CHANS, (2 * c + 2) * CHANS)
         for r in range(QUAD):
             for w in range(windows):
                 if r % 2:
-                    whole = raw_got[r // 2, pl.ds(w * both, both), :].astype(jnp.float32)
+                    at = (w * chunks + c) * CHANS
+                    rows = wide[r // 2][at : at + CHANS]
                 else:
-                    whole = raw[r // 2, w].astype(jnp.float32)
-                left, right = whole[:, :half], whole[:, half:]
-                left = jnp.where(low, left[low_at], left[high_at]) * hann[0:1, :]
-                right = jnp.where(low, right[low_at], right[high_at]) * hann[1:2, :]
+                    rows = raw[r // 2, w].astype(jnp.float32)
+                    at = 2 * c * CHANS
+                    rows = jnp.where(low, rows[at : at + CHANS], rows[at + CHANS : at + 2 * CHANS])
+                left = rows[:, :half] * hann[0:1, :]
+                right = rows[:, half:] * hann[1:2, :]
                 sums.append(left + right)
                 gaps.append(left - right)
     folded = [jnp.concatenate(x, 0).astype(jnp.bfloat16) for x in (sums, gaps)]
@@ -158,7 +160,7 @@
         out_specs=[ANY] * chunks,
         scratch_shapes=[
             pltpu.VMEM((2, windows, both, width), jnp.bfloat16),
-            pltpu.VMEM((2, windows * both, width), jnp.bfloat16),
+            pltpu.VMEM((2, windows * both // 2, width), jnp.bfloat16),
             pltpu.VMEM(basis.shape, jnp.bfloat16),
             pltpu.VMEM(hann.shape, jnp.float32),
             pltpu.VMEM((total, bins), jnp.float32),
@@ -348,35 +350,50 @@
     basis = jnp.asarray(make_basis(width, bins))
     hann = jnp.asarray(make_hann(width))
     lagmap = jnp.asarray(make_lagmap(width, bins, LAGS))
-    def cut(at, count):
-        return lax.dynamic_slice_in_dim(records, at, count, 1).reshape(-1, width)
-
-    there = (1 - chip) * half
-    send, there = lax.optimization_barrier((cut(there, wide), there))
-    got = [to_quad_peer(send, 2, "Y0_")]
+    core = mine % 2
+    split = records.reshape(windows, 2, chunks, 2, CHANS, width)
+
+    def cut(c, count, core):
+        start = (0, 1 - chip, c, core, 0, 0)
+        sizes = (windows, 1, count, 1, CHANS, width)
+        return lax.dynamic_slice(split, start, sizes).reshape(-1, width)
+
+    def exchange(c, count, core, *pages):
+        near_core = jnp.concatenate([cut(c, count, core), *pages])
+        far_core = jnp.concatenate([cut(c, count, 1 - core), *pages])
+        near_core, far_core = lax.optimization_barrier((near_core, far_core))
+        n = len(got)
+        got.append(
+            (to_quad_peer(near_core, 2, f"Y{n}A_"), to_quad_peer(far_core, 3, f"Y{n}B_"))
+        )
+        return near_core
+
+    got = []
+    sent = exchange(0, 1, core)
+    core = after(core, sent)
     own_peer = to_quad_peer(records, 1, "CA_")
-    live = after((dead[None, :] * glitch).astype(jnp.bfloat16).reshape(-1), send)
+    live = after((dead[None, :] * glitch).astype(jnp.bfloat16).reshape(-1), sent)
     notes = jnp.concatenate([swap_quads(live, 0, "NE_"), live, swap_quads(live, 1, "NO_")])
     notes = jnp.concatenate([notes, pairs.reshape(-1).astype(jnp.bfloat16)])
     size = notes.shape[0]
     page = jnp.pad(notes, (0, 16 * width - size)).reshape(16, width)
-    got.append(to_quad_peer(jnp.concatenate([cut(there + wide, wide), page]), 2, "Y1_"))
-    got.append(to_quad_peer(cut(there + 2 * wide, half - 2 * wide), 2, "Y2_"))
-    white, near, got_peer = [], [], []
+    exchange(1, 1, core, page)
+    white, near = [], []
 
     def whiten_next(c, count, *earlier):
-        got_peer.append(to_quad_peer(after(got[c], *earlier), 1, f"CB{c}_"))
-        for w in whiten(c * wide, count, meta, records, got[c], own_peer, got_peer[c], hann, basis):
+        mate = after(meta, *earlier)
+        for w in whiten(c * wide, count, mate, records, got[c][0], own_peer, got[c][1], hann, basis):
             n = len(white)
             near.append((swap_quads(w, 0, f"Z{n}E_"), w, swap_quads(w, 1, f"Z{n}O_")))
             white.append(w)
 
     whiten_next(0, 1)
-    whiten_next(1, 1, white[0])
-    notes_peer = to_quad_peer(after(notes, white[1]), 1, "NC_")
+    exchange(2, chunks - 2, after(core, white[0]))
+    notes_peer = to_quad_peer(after(notes, white[0]), 1, "NC_")
+    whiten_next(1, 1, notes_peer)
     whiten_next(2, chunks - 2, white[1])
-    notes = [notes, got[1][-16:].reshape(-1)[:size], notes_peer, got_peer[1][-16:].reshape(-1)[:size]]
-    notes = jnp.stack(notes)
+    pages = [after(part, white[1])[-16:].reshape(-1)[:size] for part in got[1]]
+    notes = jnp.stack([notes, pages[0], notes_peer, pages[1]])
     flags = notes[:, : 3 * windows * block].reshape(QUAD, 3, windows, block).swapaxes(0, 1)
     flags = flags.reshape(-1, block)
 

time: 109 us -> 99.1 us (0.909); the launches traced: 107 us -> 98.8 us
  local copies, waits for them, and re-layouts: 11.1 us -> 5.63 us
  waiting for transfers between devices: 13 us -> 8.02 us
  starting transfers between devices: 27.9 us -> 31.1 us
    unnamed x27 -> x19, local copies, waits for them, and re-layouts: 7.25 us -> 0.73 us
    ppermute x20, waiting for transfers between devices: 13 us -> 8 us  [to_quad_peer(): return lax.ppermute(value, 'chan', [(s, s ^ mask) for s in range(count)])]
    reshape x0 -> x2, local copies, waits for them, and re-layouts: none -> 2.62 us  [cut(): return lax.dynamic_slice(split, start, sizes).reshape(-1, width)]
    ppermute x20, starting transfers between devices: 11.9 us -> 14.3 us  [to_quad_peer(): return lax.ppermute(value, 'chan', [(s, s ^ mask) for s in range(count)])]
    dynamic_slice x3 -> x1, local copies, waits for them, and re-layouts: 2.98 us -> 0.84 us  [cut(): return lax.dynamic_slice(split, start, sizes).reshape(-1, width)]
  transfers between devices with their start and end apart: 30 -> 30, of which waited for: 11 -> 9; matrix products, arithmetic and copies ran while one was open for 7% -> 8% of each run, Pallas kernels for 47% -> 50%
where the time goes in v4:
time: 99.1 us; the launch traced here: 98.8 us
  Pallas kernels  51.3 us (52%)
  starting transfers between devices  31.1 us (31%)
  waiting for transfers between devices  8.02 us (8%)
  local copies, waits for them, and re-layouts  5.63 us (6%)
  other arithmetic  2.39 us (2%)
    pallas_call x5, Pallas kernels, cross_stack(): pl.pallas_call(functools.partial(cross_kernel, sides, chunk, windows), ou...  32.2 us
    ppermute x10, starting transfers between devices, swap_quads(): return lax.ppermute(value, 'chan', pairs)  16.8 us
    ppermute x20, starting transfers between devices, to_quad_peer(): return lax.ppermute(value, 'chan', [(s, s ^ mask) for s in range(count)])  14.3 us
    pallas_call x3, Pallas kernels, whiten(): pl.pallas_call(functools.partial(whiten_kernel, chunks, first), out_shape...  12.7 us
    ppermute x20, waiting for transfers between devices, to_quad_peer(): return lax.ppermute(value, 'chan', [(s, s ^ mask) for s in range(count)])  8 us
    pallas_call x4, Pallas kernels, place_stacks(): pl.pallas_call(place_kernel, out_shape=jax.ShapeDtypeStruct(shape, jnp.fl...  6.35 us
    reshape x2, local copies, waits for them, and re-layouts, cut(): return lax.dynamic_slice(split, start, sizes).reshape(-1, width)  2.62 us
  transfers between devices with their start and end apart: 30, of which 9 were waited for; matrix products, arithmetic and copies ran while one was open for 8% of the time, Pallas kernels for 50%

profile of v4, /device:TPU:11, one launch (start us, length us, event | category | flops | bytes accessed | tf_op | source)
XLA Modules:
  0.0 98.8 jit_solution(14109179813558411989)
XLA Ops:
  0.0 0.7 collective-permute-start.4
  0.7 1.6 %dynamic-slice_bitcast_fusion.2 = (bf16[32,2048]{1,0:T(8,128)(2,1)S(1)}, bf16[32,2048]{1,0:T(8,128)(2,1)}) fusion(bf16[4,2,4,2,8,2048]{5,4,3,2,1,0:T(8,128)(2,1)} %bitcast.63, s32[]{:T(128)S(6)} %select_n.79, s32[]{:T(128)S(6)} %select_n.81, s32[]{:T(128)S(6)} %select_n.80), kind=kLoop, calls=%fused_computation.4 | loop fusion | bytes 524300 | tf_op jit(solution)/shard_map/reshape | solution.py:359
  2.3 1.2 %collective-permute-start.3 = (bf16[32,2048]{1,0:T(8,128)(2,1)}, bf16[32,2048]{1,0:T(8,128)(2,1)S(1)}, u32[]{:S(2)}, u32[]{:S(2)}) collective-permute-start(bf16[32,2048]{1,0:T(8,128)(2,1)} %get-tuple-element.38), channel_id=1, source_target_pairs={{0,2},{1,3},{2,0},{3,1},{4,6},{5,7},{6,4},{7,5},{8,10},{9,11},{10,... | collective-permute-start | bytes 393224 | tf_op jit(solution)/shard_map/Y0A_/ppermute | solution.py:57
  3.6 0.7 fusion.16
  4.4 4.3 %collective-permute-start.1 = (bf16[512]{0:T(512)(128)(2,1)S(1)}, bf16[512]{0:T(512)(128)(2,1)S(1)}, u32[]{:S(2)}, u32[]{:S(2)}) collective-permute-start(bf16[512]{0:T(512)(128)(2,1)S(1)} %fusion.16), channel_id=1, source_target_pairs={{4,8},{5,9},{6,10},{7,11},{8,4},{9,5},{10,6},{11,7},{20,24},{21,25... | collective-permute-start | bytes 3080 | tf_op jit(solution)/shard_map/NO_/ppermute | solution.py:69
  8.7 1.2 %collective-permute-start.5 = (bf16[32,2048]{1,0:T(8,128)(2,1)S(1)}, bf16[32,2048]{1,0:T(8,128)(2,1)S(1)}, u32[]{:S(2)}, u32[]{:S(2)}) collective-permute-start(bf16[32,2048]{1,0:T(8,128)(2,1)S(1)} %get-tuple-element.42), channel_id=1, source_target_pairs={{0,3},{1,2},{2,1},{3,0},{4,7},{5,6},{6,5},{7,4},{8,11},{9,10},{10,... | collective-permute-start | bytes 393224 | tf_op jit(solution)/shard_map/Y0B_/ppermute | solution.py:57
  10.1 1.0 dynamic-slice_bitcast_fusion
  11.1 0.7 convert_element_type.16
  12.8 0.6 stack.47
  13.5 0.7 pad_maximum_fusion
  14.2 1.2 %collective-permute-start.2 = (bf16[48,2048]{1,0:T(8,128)(2,1)}, bf16[48,2048]{1,0:T(8,128)(2,1)S(1)}, u32[]{:S(2)}, u32[]{:S(2)}) collective-permute-start(bf16[48,2048]{1,0:T(8,128)(2,1)} %get-tuple-element.41), channel_id=1, source_target_pairs={{0,2},{1,3},{2,0},{3,1},{4,6},{5,7},{6,4},{7,5},{8,10},{9,11},{10,... | collective-permute-start | bytes 589832 | tf_op jit(solution)/shard_map/Y1A_/ppermute | solution.py:57
  15.4 0.3 collective-permute-start.7
  15.8 3.7 %whiten.3.refs_1_ = bf16[128,2048]{1,0:T(8,128)(2,1)S(1)} custom-call(s32[2]{0:T(128)S(1)} %pad_add_fusion.1.meta, bf16[4,128,2048]{2,1,0:T(8,128)(2,1)S(1)} %copy-done, bf16[32,2048]{1,0:T(8,128)(2,1)S(1)} %collective-permute-done.3.got, bf16[4,128,2048]{2,1,0:T(8,128)(2,1)} %collective-permute-done.4.own_peer, ...), custom_call_target="tpu_custom_call" | custom-call | flops 2000000000 | bytes 1024 | tf_op jit(solution)/shard_map/whiten/pallas_call | solution.py:156
  19.6 2.6 %collective-permute-start.11 = (bf16[128,2048]{1,0:T(8,128)(2,1)S(1)}, bf16[128,2048]{1,0:T(8,128)(2,1)}, u32[]{:S(2)}, u32[]{:S(2)}) collective-permute-start(bf16[128,2048]{1,0:T(8,128)(2,1)S(1)} %whiten.3.refs_1_), channel_id=1, source_target_pairs={{4,8},{5,9},{6,10},{7,11},{8,4},{9,5},{10,6},{11,7},{20,24},{21,25... | collective-permute-start | bytes 1572872 | tf_op jit(solution)/shard_map/Z0O_/ppermute | solution.py:69
  22.3 0.8 constant_dynamic-slice_fusion
  23.4 0.6 collective-permute-start.8
  24.0 1.3 %collective-permute-start.9 = (bf16[64,2048]{1,0:T(8,128)(2,1)}, bf16[64,2048]{1,0:T(8,128)(2,1)}, u32[]{:S(2)}, u32[]{:S(2)}) collective-permute-start(bf16[64,2048]{1,0:T(8,128)(2,1)} %bitcast.15), channel_id=1, source_target_pairs={{0,3},{1,2},{2,1},{3,0},{4,7},{5,6},{6,5},{7,4},{8,11},{9,10},{10,... | collective-permute-start | bytes 786440 | tf_op jit(solution)/shard_map/Y2B_/ppermute | solution.py:57
  25.2 0.4 collective-permute-done.7.got_peer
  25.6 3.7 %whiten.4.refs_1_ = bf16[128,2048]{1,0:T(8,128)(2,1)S(1)} custom-call(s32[2]{0:T(128)S(1)} %pad_add_fusion.1.meta, bf16[4,128,2048]{2,1,0:T(8,128)(2,1)S(1)} %copy-done, bf16[48,2048]{1,0:T(8,128)(2,1)S(1)} %collective-permute-done.2.got, bf16[4,128,2048]{2,1,0:T(8,128)(2,1)} %collective-permute-done.4.own_peer, ...), custom_call_target="tpu_custom_call" | custom-call | flops 2000000000 | bytes 1024 | tf_op jit(solution)/shard_map/whiten/pallas_call | solution.py:156
  30.4 1.1 %collective-permute-done.8.got = bf16[64,2048]{1,0:T(8,128)(2,1)} collective-permute-done((bf16[64,2048]{1,0:T(8,128)(2,1)}, bf16[64,2048]{1,0:T(8,128)(2,1)}, u32[]{:S(2)}, u32[]{:S(2)}) %collective-permute-start.8) | collective-permute-done | bytes 262176 | tf_op jit(solution)/shard_map/Y2A_/ppermute | solution.py:57
  31.5 2.8 %collective-permute-start.14 = (bf16[128,2048]{1,0:T(8,128)(2,1)S(1)}, bf16[128,2048]{1,0:T(8,128)(2,1)S(1)}, u32[]{:S(2)}, u32[]{:S(2)}) collective-permute-start(bf16[128,2048]{1,0:T(8,128)(2,1)S(1)} %whiten.4.refs_1_), channel_id=1, source_target_pairs={{4,8},{5,9},{6,10},{7,11},{8,4},{9,5},{10,6},{11,7},{20,24},{21,25... | collective-permute-start | bytes 1572872 | tf_op jit(solution)/shard_map/Z1O_/ppermute | solution.py:69
  34.3 3.4 %collective-permute-done.9.got_peer = bf16[64,2048]{1,0:T(8,128)(2,1)} collective-permute-done((bf16[64,2048]{1,0:T(8,128)(2,1)}, bf16[64,2048]{1,0:T(8,128)(2,1)}, u32[]{:S(2)}, u32[]{:S(2)}) %collective-permute-start.9) | collective-permute-done | bytes 262176 | tf_op jit(solution)/shard_map/Y2B_/ppermute | solution.py:57
  37.7 5.3 %whiten.5 = (bf16[128,2048]{1,0:T(8,128)(2,1)}, bf16[128,2048]{1,0:T(8,128)(2,1)S(1)}) custom-call(s32[2]{0:T(128)S(1)} %pad_add_fusion.1.meta, bf16[4,128,2048]{2,1,0:T(8,128)(2,1)S(1)} %copy-done, bf16[64,2048]{1,0:T(8,128)(2,1)} %collective-permute-done.8.got, bf16[4,128,2048]{2,1,0:T(8,128)(2,1)} %collective-permute-done.4.own_peer, ...), custom_call_target="tpu_custom_call" | custom-call | flops 4000000000 | bytes 1024 | tf_op jit(solution)/shard_map/whiten/pallas_call | solution.py:156
  43.0 0.6 collective-permute-start.18
  43.6 2.5 %collective-permute-start.19 = (bf16[128,2048]{1,0:T(8,128)(2,1)}, bf16[128,2048]{1,0:T(8,128)(2,1)}, u32[]{:S(2)}, u32[]{:S(2)}) collective-permute-start(bf16[128,2048]{1,0:T(8,128)(2,1)} %get-tuple-element.52.refs_1_), channel_id=1, source_target_pairs={{4,8},{5,9},{6,10},{7,11},{8,4},{9,5},{10,6},{11,7},{20,24},{21,25... | collective-permute-start | bytes 1572872 | tf_op jit(solution)/shard_map/Z2O_/ppermute | solution.py:69
  46.1 7.6 %cross_stack.5 = (bf16[1,256,512]{2,1,0:T(8,128)(2,1)S(1)}, bf16[1,256,512]{2,1,0:T(8,128)(2,1)S(1)}) custom-call(s32[2]{0:T(128)S(1)} %pad_add_fusion.1.meta, s32[64,2]{1,0:T(8,128)S(1)} %fusion.7.place, s32[64]{0:T(128)S(1)} %get-tuple-element.71.filled, bf16[128,2048]{1,0:T(8,128)(2,1)} %collective-permute-done.10.refs_0_, ...), custom_call_target="tpu_custom_call" | custom-call | flops 6400000000 | bytes 1024 | tf_op jit(solution)/shard_map/cross_stack/pallas_call | solution.py:278
  53.7 1.3 %collective-permute-start.12 = (bf16[1,256,512]{2,1,0:T(8,128)(2,1)S(1)}, bf16[1,256,512]{2,1,0:T(8,128)(2,1)S(1)}, u32[]{:S(2)}, u32[]{:S(2)}) collective-permute-start(bf16[1,256,512]{2,1,0:T(8,128)(2,1)S(1)} %get-tuple-element.57), channel_id=1, source_target_pairs={{0,2},{1,3},{2,0},{3,1},{4,6},{5,7},{6,4},{7,5},{8,10},{9,11},{10,... | collective-permute-start | bytes 786440 | tf_op jit(solution)/shard_map/R0_/ppermute | solution.py:57
  55.0 7.6 %cross_stack.6 = (bf16[1,256,512]{2,1,0:T(8,128)(2,1)S(1)}, bf16[1,256,512]{2,1,0:T(8,128)(2,1)S(1)}) custom-call(s32[2]{0:T(128)S(1)} %pad_add_fusion.1.meta, s32[64,2]{1,0:T(8,128)S(1)} %fusion.7.place, s32[64]{0:T(128)S(1)} %get-tuple-element.71.filled, bf16[128,2048]{1,0:T(8,128)(2,1)} %collective-permute-done.13.refs_0_, ...), custom_call_target="tpu_custom_call" | custom-call | flops 6400000000 | bytes 1024 | tf_op jit(solution)/shard_map/cross_stack/pallas_call | solution.py:278
  63.0 0.3 collective-permute-start.16
  63.4 0.9 collective-permute-done.15
  64.3 3.5 %collective-permute-start.24 = (bf16[128,2048]{1,0:T(8,128)(2,1)S(1)}, bf16[128,2048]{1,0:T(8,128)(2,1)S(1)}, u32[]{:S(2)}, u32[]{:S(2)}) collective-permute-start(bf16[128,2048]{1,0:T(8,128)(2,1)S(1)} %copy-done.3), channel_id=1, source_target_pairs={{4,8},{5,9},{6,10},{7,11},{8,4},{9,5},{10,6},{11,7},{20,24},{21,25... | collective-permute-start | bytes 1572872 | tf_op jit(solution)/shard_map/Z3O_/ppermute | solution.py:69
  67.8 0.4 collective-permute-start.17
  68.2 1.6 %place_stacks.4.refs_0_ = f32[16,2,64,512]{3,2,1,0:T(8,128)} custom-call(s32[4]{0:T(128)S(1)} %pad_add_fusion.slot, bf16[1,2,128,512]{3,2,1,0:T(8,128)(2,1)S(1)} %bitcast.83, bf16[1,2,128,512]{3,2,1,0:T(8,128)(2,1)S(1)} %bitcast.84, bf16[1,2,128,512]{3,2,1,0:T(8,128)(2,1)S(1)} %bitcast.85, bf16[1,2,128,512]{3,2,1,0:T(8,128)(2,1)S(1)} %bitcast.86), custom_call_target="tpu_custom_call" | custom-call | flops 1500000000 | bytes 1024 | tf_op jit(solution)/shard_map/place_stacks/pallas_call | solution.py:320
  69.8 7.7 %cross_stack.7 = (bf16[1,256,512]{2,1,0:T(8,128)(2,1)S(1)}, bf16[1,256,512]{2,1,0:T(8,128)(2,1)S(1)}) custom-call(s32[2]{0:T(128)S(1)} %pad_add_fusion.1.meta, s32[64,2]{1,0:T(8,128)S(1)} %fusion.7.place, s32[64]{0:T(128)S(1)} %get-tuple-element.71.filled, bf16[128,2048]{1,0:T(8,128)(2,1)} %collective-permute-done.18.refs_0_, ...), custom_call_target="tpu_custom_call" | custom-call | flops 6400000000 | bytes 1024 | tf_op jit(solution)/shard_map/cross_stack/pallas_call | solution.py:278
  77.5 1.0 %collective-permute-start.20 = (bf16[1,256,512]{2,1,0:T(8,128)(2,1)S(1)}, bf16[1,256,512]{2,1,0:T(8,128)(2,1)S(1)}, u32[]{:S(2)}, u32[]{:S(2)}) collective-permute-start(bf16[1,256,512]{2,1,0:T(8,128)(2,1)S(1)} %get-tuple-element.64), channel_id=1, source_target_pairs={{0,1},{1,0},{2,3},{3,2},{4,5},{5,4},{6,7},{7,6},{8,9},{9,8},{10,11... | collective-permute-start | bytes 786440 | tf_op jit(solution)/shard_map/H1_/ppermute | solution.py:57
  78.6 1.2 %collective-permute-start.22 = (bf16[1,256,512]{2,1,0:T(8,128)(2,1)S(1)}, bf16[1,256,512]{2,1,0:T(8,128)(2,1)S(1)}, u32[]{:S(2)}, u32[]{:S(2)}) collective-permute-start(bf16[1,256,512]{2,1,0:T(8,128)(2,1)S(1)} %get-tuple-element.67), channel_id=1, source_target_pairs={{0,2},{1,3},{2,0},{3,1},{4,6},{5,7},{6,4},{7,5},{8,10},{9,11},{10,... | collective-permute-start | bytes 786440 | tf_op jit(solution)/shard_map/R2_/ppermute | solution.py:57
  80.0 1.6 %place_stacks.5.refs_0_ = f32[16,2,64,512]{3,2,1,0:T(8,128)} custom-call(s32[4]{0:T(128)S(1)} %pad_add_fusion.slot, bf16[1,2,128,512]{3,2,1,0:T(8,128)(2,1)S(1)} %bitcast.66, bf16[1,2,128,512]{3,2,1,0:T(8,128)(2,1)S(1)} %bitcast.69, bf16[1,2,128,512]{3,2,1,0:T(8,128)(2,1)S(1)} %bitcast.72, ...), custom_call_target="tpu_custom_call", output_to_operand_aliasing={{}: (5, {})} | custom-call | flops 1500000000 | bytes 1024 | tf_op jit(solution)/shard_map/place_stacks/pallas_call | solution.py:320
  81.6 4.4 %cross_stack.8 = bf16[1,256,512]{2,1,0:T(8,128)(2,1)S(1)} custom-call(s32[2]{0:T(128)S(1)} %pad_add_fusion.1.meta, s32[64,2]{1,0:T(8,128)S(1)} %fusion.7.place, s32[64]{0:T(128)S(1)} %get-tuple-element.71.filled, bf16[128,2048]{1,0:T(8,128)(2,1)S(1)} %collective-permute-done.23.refs_0_, bf16[128,2048]{1,0:T(8,128)(2,1)S(1)} %copy-done.3, ...), custom_call_target="tpu_custom_call" | custom-call | flops 3200000000 | bytes 1024 | tf_op jit(solution)/shard_map/cross_stack/pallas_call | solution.py:278
  86.1 1.2 %collective-permute-start.25 = (bf16[1,256,512]{2,1,0:T(8,128)(2,1)S(1)}, bf16[1,256,512]{2,1,0:T(8,128)(2,1)S(1)}, u32[]{:S(2)}, u32[]{:S(2)}) collective-permute-start(bf16[1,256,512]{2,1,0:T(8,128)(2,1)S(1)} %get-tuple-element.68), channel_id=1, source_target_pairs={{0,1},{1,0},{2,3},{3,2},{4,5},{5,4},{6,7},{7,6},{8,9},{9,8},{10,11... | collective-permute-start | bytes 786440 | tf_op jit(solution)/shard_map/H2_/ppermute | solution.py:57
  87.3 1.2 %collective-permute-start.27 = (bf16[1,256,512]{2,1,0:T(8,128)(2,1)S(1)}, bf16[1,256,512]{2,1,0:T(8,128)(2,1)S(1)}, u32[]{:S(2)}, u32[]{:S(2)}) collective-permute-start(bf16[1,256,512]{2,1,0:T(8,128)(2,1)S(1)} %cross_stack.8), channel_id=1, source_target_pairs={{0,2},{1,3},{2,0},{3,1},{4,6},{5,7},{6,4},{7,5},{8,10},{9,11},{10,... | collective-permute-start | bytes 786440 | tf_op jit(solution)/shard_map/R3_/ppermute | solution.py:57
  88.5 0.3 collective-permute-done.26
  88.8 1.6 %place_stacks.6.refs_0_ = f32[16,2,64,512]{3,2,1,0:T(8,128)} custom-call(s32[4]{0:T(128)S(1)} %pad_add_fusion.slot, bf16[1,2,128,512]{3,2,1,0:T(8,128)(2,1)S(1)} %bitcast.67, bf16[1,2,128,512]{3,2,1,0:T(8,128)(2,1)S(1)} %bitcast.68, bf16[1,2,128,512]{3,2,1,0:T(8,128)(2,1)S(1)} %bitcast.74, ...), custom_call_target="tpu_custom_call", output_to_operand_aliasing={{}: (5, {})} | custom-call | flops 1500000000 | bytes 1024 | tf_op jit(solution)/shard_map/place_stacks/pallas_call | solution.py:320
  90.4 4.8 %cross_stack.9 = bf16[1,256,512]{2,1,0:T(8,128)(2,1)S(1)} custom-call(s32[2]{0:T(128)S(1)} %pad_add_fusion.1.meta, s32[64,2]{1,0:T(8,128)S(1)} %fusion.7.place, s32[64]{0:T(128)S(1)} %get-tuple-element.71.filled, bf16[128,2048]{1,0:T(8,128)(2,1)S(1)} %collective-permute-done.23.refs_0_, bf16[128,2048]{1,0:T(8,128)(2,1)S(1)} %copy-done.3, ...), custom_call_target="tpu_custom_call" | custom-call | flops 3200000000 | bytes 1024 | tf_op jit(solution)/shard_map/cross_stack/pallas_call | solution.py:278
  95.2 0.5 collective-permute-start.28
  95.7 0.3 collective-permute-start.29
  96.0 0.9 collective-permute-done.28
  96.9 0.4 collective-permute-done.29
  97.2 1.6 %place_stacks.7 = f32[16,2,64,512]{3,2,1,0:T(8,128)} custom-call(s32[4]{0:T(128)S(1)} %pad_add_fusion.slot, bf16[1,2,128,512]{3,2,1,0:T(8,128)(2,1)S(1)} %bitcast.71, bf16[1,2,128,512]{3,2,1,0:T(8,128)(2,1)S(1)} %bitcast.70, bf16[1,2,128,512]{3,2,1,0:T(8,128)(2,1)S(1)} %bitcast.73, ...), custom_call_target="tpu_custom_call", output_to_operand_aliasing={{}: (5, {})} | custom-call | flops 1500000000 | bytes 1024 | tf_op jit(solution)/shard_map/place_stacks/pallas_call | solution.py:320
  (74 shorter events, 3.5 us)
Async XLA Ops:
  0.0 15.8 %copy-start.1 = (f32[2,1024]{1,0:T(2,128)S(1)}, f32[2,1024]{1,0:T(2,128)}, u32[]{:S(2)}) copy-start(f32[2,1024]{1,0:T(2,128)} %constant.106.clone.curve) | copy-start | bytes 24580
  0.0 15.8 %copy-start = (bf16[4,128,2048]{2,1,0:T(8,128)(2,1)S(1)}, bf16[4,128,2048]{2,1,0:T(8,128)(2,1)}, u32[]{:S(2)}) copy-start(bf16[4,128,2048]{2,1,0:T(8,128)(2,1)} %own.5) | copy-start | bytes 6291460
  0.0 15.8 %collective-permute-start.4 = (bf16[4,128,2048]{2,1,0:T(8,128)(2,1)}, bf16[4,128,2048]{2,1,0:T(8,128)(2,1)}, u32[]{:S(2)}, u32[]{:S(2)}) collective-permute-start(bf16[4,128,2048]{2,1,0:T(8,128)(2,1)} %own.5), channel_id=1, source_target_pairs={{0,1},{1,0},{2,3},{3,2},{4,5},{5,4},{6,7},{7,6},{8,9},{9,8},{10,11... | collective-permute-start | bytes 6291464 | tf_op jit(solution)/shard_map/CA_/ppermute | solution.py:57
  2.3 13.4 %collective-permute-start.3 = (bf16[32,2048]{1,0:T(8,128)(2,1)}, bf16[32,2048]{1,0:T(8,128)(2,1)S(1)}, u32[]{:S(2)}, u32[]{:S(2)}) collective-permute-start(bf16[32,2048]{1,0:T(8,128)(2,1)} %get-tuple-element.38), channel_id=1, source_target_pairs={{0,2},{1,3},{2,0},{3,1},{4,6},{5,7},{6,4},{7,5},{8,10},{9,11},{10,... | collective-permute-start | bytes 393224 | tf_op jit(solution)/shard_map/Y0A_/ppermute | solution.py:57
  4.2 7.7 %collective-permute-start = (bf16[512]{0:T(512)(128)(2,1)S(1)}, bf16[512]{0:T(512)(128)(2,1)S(1)}, u32[]{:S(2)}, u32[]{:S(2)}) collective-permute-start(bf16[512]{0:T(512)(128)(2,1)S(1)} %fusion.16), channel_id=1, source_target_pairs={{0,4},{1,5},{2,6},{3,7},{4,0},{5,1},{6,2},{7,3},{8,12},{9,13},{10,... | collective-permute-start | bytes 3080 | tf_op jit(solution)/shard_map/NE_/ppermute | solution.py:69
  4.4 8.0 %collective-permute-start.1 = (bf16[512]{0:T(512)(128)(2,1)S(1)}, bf16[512]{0:T(512)(128)(2,1)S(1)}, u32[]{:S(2)}, u32[]{:S(2)}) collective-permute-start(bf16[512]{0:T(512)(128)(2,1)S(1)} %fusion.16), channel_id=1, source_target_pairs={{4,8},{5,9},{6,10},{7,11},{8,4},{9,5},{10,6},{11,7},{20,24},{21,25... | collective-permute-start | bytes 3080 | tf_op jit(solution)/shard_map/NO_/ppermute | solution.py:69
  8.7 7.0 %collective-permute-start.5 = (bf16[32,2048]{1,0:T(8,128)(2,1)S(1)}, bf16[32,2048]{1,0:T(8,128)(2,1)S(1)}, u32[]{:S(2)}, u32[]{:S(2)}) collective-permute-start(bf16[32,2048]{1,0:T(8,128)(2,1)S(1)} %get-tuple-element.42), channel_id=1, source_target_pairs={{0,3},{1,2},{2,1},{3,0},{4,7},{5,6},{6,5},{7,4},{8,11},{9,10},{10,... | collective-permute-start | bytes 393224 | tf_op jit(solution)/shard_map/Y0B_/ppermute | solution.py:57
  14.2 9.8 %collective-permute-start.2 = (bf16[48,2048]{1,0:T(8,128)(2,1)}, bf16[48,2048]{1,0:T(8,128)(2,1)S(1)}, u32[]{:S(2)}, u32[]{:S(2)}) collective-permute-start(bf16[48,2048]{1,0:T(8,128)(2,1)} %get-tuple-element.41), channel_id=1, source_target_pairs={{0,2},{1,3},{2,0},{3,1},{4,6},{5,7},{6,4},{7,5},{8,10},{9,11},{10,... | collective-permute-start | bytes 589832 | tf_op jit(solution)/shard_map/Y1A_/ppermute | solution.py:57
  15.4 10.2 %collective-permute-start.7 = (bf16[48,2048]{1,0:T(8,128)(2,1)S(1)}, bf16[48,2048]{1,0:T(8,128)(2,1)S(1)}, u32[]{:S(2)}, u32[]{:S(2)}) collective-permute-start(bf16[48,2048]{1,0:T(8,128)(2,1)S(1)} %get-tuple-element.45), channel_id=1, source_target_pairs={{0,3},{1,2},{2,1},{3,0},{4,7},{5,6},{6,5},{7,4},{8,11},{9,10},{10,... | collective-permute-start | bytes 589832 | tf_op jit(solution)/shard_map/Y1B_/ppermute | solution.py:57
  19.5 24.0 %collective-permute-start.10 = (bf16[128,2048]{1,0:T(8,128)(2,1)S(1)}, bf16[128,2048]{1,0:T(8,128)(2,1)}, u32[]{:S(2)}, u32[]{:S(2)}) collective-permute-start(bf16[128,2048]{1,0:T(8,128)(2,1)S(1)} %whiten.3.refs_1_), channel_id=1, source_target_pairs={{0,4},{1,5},{2,6},{3,7},{4,0},{5,1},{6,2},{7,3},{8,12},{9,13},{10,... | collective-permute-start | bytes 1572872 | tf_op jit(solution)/shard_map/Z0E_/ppermute | solution.py:69
  19.6 26.4 %collective-permute-start.11 = (bf16[128,2048]{1,0:T(8,128)(2,1)S(1)}, bf16[128,2048]{1,0:T(8,128)(2,1)}, u32[]{:S(2)}, u32[]{:S(2)}) collective-permute-start(bf16[128,2048]{1,0:T(8,128)(2,1)S(1)} %whiten.3.refs_1_), channel_id=1, source_target_pairs={{4,8},{5,9},{6,10},{7,11},{8,4},{9,5},{10,6},{11,7},{20,24},{21,25... | collective-permute-start | bytes 1572872 | tf_op jit(solution)/shard_map/Z0O_/ppermute | solution.py:69
  22.2 1.2 %collective-permute-start.6 = (bf16[1568]{0:T(1024)(128)(2,1)S(1)}, bf16[1568]{0:T(1024)(128)(2,1)S(1)}, u32[]{:S(2)}, u32[]{:S(2)}) collective-permute-start(bf16[1568]{0:T(1024)(128)(2,1)S(1)} %dynamic-update-slice.3), channel_id=1, source_target_pairs={{0,1},{1,0},{2,3},{3,2},{4,5},{5,4},{6,7},{7,6},{8,9},{9,8},{10,11... | collective-permute-start | bytes 9416 | tf_op jit(solution)/shard_map/NC_/ppermute | solution.py:57
  23.1 6.4 %copy-start.5 = (bf16[1,1568]{1,0:T(2,128)(2,1)S(1)}, bf16[1,1568]{1,0:T(2,128)(2,1)}, u32[]{:S(2)}) copy-start(bf16[1,1568]{1,0:T(2,128)(2,1)} %stack.47) | copy-start | bytes 9412
  23.4 8.0 %collective-permute-start.8 = (bf16[64,2048]{1,0:T(8,128)(2,1)}, bf16[64,2048]{1,0:T(8,128)(2,1)}, u32[]{:S(2)}, u32[]{:S(2)}) collective-permute-start(bf16[64,2048]{1,0:T(8,128)(2,1)} %bitcast.14), channel_id=1, source_target_pairs={{0,2},{1,3},{2,0},{3,1},{4,6},{5,7},{6,4},{7,5},{8,10},{9,11},{10,... | collective-permute-start | bytes 786440 | tf_op jit(solution)/shard_map/Y2A_/ppermute | solution.py:57
  24.0 13.7 %collective-permute-start.9 = (bf16[64,2048]{1,0:T(8,128)(2,1)}, bf16[64,2048]{1,0:T(8,128)(2,1)}, u32[]{:S(2)}, u32[]{:S(2)}) collective-permute-start(bf16[64,2048]{1,0:T(8,128)(2,1)} %bitcast.15), channel_id=1, source_target_pairs={{0,3},{1,2},{2,1},{3,0},{4,7},{5,6},{6,5},{7,4},{8,11},{9,10},{10,... | collective-permute-start | bytes 786440 | tf_op jit(solution)/shard_map/Y2B_/ppermute | solution.py:57
  30.0 25.1 %collective-permute-start.13 = (bf16[128,2048]{1,0:T(8,128)(2,1)S(1)}, bf16[128,2048]{1,0:T(8,128)(2,1)}, u32[]{:S(2)}, u32[]{:S(2)}) collective-permute-start(bf16[128,2048]{1,0:T(8,128)(2,1)S(1)} %whiten.4.refs_1_), channel_id=1, source_target_pairs={{0,4},{1,5},{2,6},{3,7},{4,0},{5,1},{6,2},{7,3},{8,12},{9,13},{10,... | collective-permute-start | bytes 1572872 | tf_op jit(solution)/shard_map/Z1E_/ppermute | solution.py:69
  31.5 23.6 %collective-permute-start.14 = (bf16[128,2048]{1,0:T(8,128)(2,1)S(1)}, bf16[128,2048]{1,0:T(8,128)(2,1)S(1)}, u32[]{:S(2)}, u32[]{:S(2)}) collective-permute-start(bf16[128,2048]{1,0:T(8,128)(2,1)S(1)} %whiten.4.refs_1_), channel_id=1, source_target_pairs={{4,8},{5,9},{6,10},{7,11},{8,4},{9,5},{10,6},{11,7},{20,24},{21,25... | collective-permute-start | bytes 1572872 | tf_op jit(solution)/shard_map/Z1O_/ppermute | solution.py:69
  43.0 10.7 %copy-start.2 = (bf16[128,2048]{1,0:T(8,128)(2,1)}, bf16[128,2048]{1,0:T(8,128)(2,1)S(1)}, u32[]{:S(2)}) copy-start(bf16[128,2048]{1,0:T(8,128)(2,1)S(1)} %get-tuple-element.53.refs_1_) | copy-start | bytes 1572868
  43.0 26.8 %collective-permute-start.18 = (bf16[128,2048]{1,0:T(8,128)(2,1)}, bf16[128,2048]{1,0:T(8,128)(2,1)}, u32[]{:S(2)}, u32[]{:S(2)}) collective-permute-start(bf16[128,2048]{1,0:T(8,128)(2,1)} %get-tuple-element.52.refs_1_), channel_id=1, source_target_pairs={{0,4},{1,5},{2,6},{3,7},{4,0},{5,1},{6,2},{7,3},{8,12},{9,13},{10,... | collective-permute-start | bytes 1572872 | tf_op jit(solution)/shard_map/Z2E_/ppermute | solution.py:69
  43.6 26.2 %collective-permute-start.19 = (bf16[128,2048]{1,0:T(8,128)(2,1)}, bf16[128,2048]{1,0:T(8,128)(2,1)}, u32[]{:S(2)}, u32[]{:S(2)}) collective-permute-start(bf16[128,2048]{1,0:T(8,128)(2,1)} %get-tuple-element.52.refs_1_), channel_id=1, source_target_pairs={{4,8},{5,9},{6,10},{7,11},{8,4},{9,5},{10,6},{11,7},{20,24},{21,25... | collective-permute-start | bytes 1572872 | tf_op jit(solution)/shard_map/Z2O_/ppermute | solution.py:69
  53.7 9.6 %copy-start.3 = (bf16[128,2048]{1,0:T(8,128)(2,1)S(1)}, bf16[128,2048]{1,0:T(8,128)(2,1)}, u32[]{:S(2)}) copy-start(bf16[128,2048]{1,0:T(8,128)(2,1)} %copy-done.2) | copy-start | bytes 1572868
  53.7 9.0 %collective-permute-start.12 = (bf16[1,256,512]{2,1,0:T(8,128)(2,1)S(1)}, bf16[1,256,512]{2,1,0:T(8,128)(2,1)S(1)}, u32[]{:S(2)}, u32[]{:S(2)}) collective-permute-start(bf16[1,256,512]{2,1,0:T(8,128)(2,1)S(1)} %get-tuple-element.57), channel_id=1, source_target_pairs={{0,2},{1,3},{2,0},{3,1},{4,6},{5,7},{6,4},{7,5},{8,10},{9,11},{10,... | collective-permute-start | bytes 786440 | tf_op jit(solution)/shard_map/R0_/ppermute | solution.py:57
  62.7 1.6 %collective-permute-start.15 = (bf16[1,256,512]{2,1,0:T(8,128)(2,1)S(1)}, bf16[1,256,512]{2,1,0:T(8,128)(2,1)S(1)}, u32[]{:S(2)}, u32[]{:S(2)}) collective-permute-start(bf16[1,256,512]{2,1,0:T(8,128)(2,1)S(1)} %get-tuple-element.59), channel_id=1, source_target_pairs={{0,1},{1,0},{2,3},{3,2},{4,5},{5,4},{6,7},{7,6},{8,9},{9,8},{10,11... | collective-permute-start | bytes 786440 | tf_op jit(solution)/shard_map/H0_/ppermute | solution.py:57
  63.0 4.9 %collective-permute-start.16 = (bf16[1,256,512]{2,1,0:T(8,128)(2,1)S(1)}, bf16[1,256,512]{2,1,0:T(8,128)(2,1)S(1)}, u32[]{:S(2)}, u32[]{:S(2)}) collective-permute-start(bf16[1,256,512]{2,1,0:T(8,128)(2,1)S(1)} %collective-permute-done.12), channel_id=1, source_target_pairs={{0,1},{1,0},{2,3},{3,2},{4,5},{5,4},{6,7},{7,6},{8,9},{9,8},{10,11... | collective-permute-start | bytes 786440 | tf_op jit(solution)/shard_map/F0_/ppermute | solution.py:57
  63.3 18.3 %collective-permute-start.23 = (bf16[128,2048]{1,0:T(8,128)(2,1)S(1)}, bf16[128,2048]{1,0:T(8,128)(2,1)S(1)}, u32[]{:S(2)}, u32[]{:S(2)}) collective-permute-start(bf16[128,2048]{1,0:T(8,128)(2,1)S(1)} %copy-done.3), channel_id=1, source_target_pairs={{0,4},{1,5},{2,6},{3,7},{4,0},{5,1},{6,2},{7,3},{8,12},{9,13},{10,... | collective-permute-start | bytes 1572872 | tf_op jit(solution)/shard_map/Z3E_/ppermute | solution.py:69
  64.3 17.3 %collective-permute-start.24 = (bf16[128,2048]{1,0:T(8,128)(2,1)S(1)}, bf16[128,2048]{1,0:T(8,128)(2,1)S(1)}, u32[]{:S(2)}, u32[]{:S(2)}) collective-permute-start(bf16[128,2048]{1,0:T(8,128)(2,1)S(1)} %copy-done.3), channel_id=1, source_target_pairs={{4,8},{5,9},{6,10},{7,11},{8,4},{9,5},{10,6},{11,7},{20,24},{21,25... | collective-permute-start | bytes 1572872 | tf_op jit(solution)/shard_map/Z3O_/ppermute | solution.py:69
  67.8 9.6 %collective-permute-start.17 = (bf16[1,256,512]{2,1,0:T(8,128)(2,1)S(1)}, bf16[1,256,512]{2,1,0:T(8,128)(2,1)S(1)}, u32[]{:S(2)}, u32[]{:S(2)}) collective-permute-start(bf16[1,256,512]{2,1,0:T(8,128)(2,1)S(1)} %get-tuple-element.62), channel_id=1, source_target_pairs={{0,2},{1,3},{2,0},{3,1},{4,6},{5,7},{6,4},{7,5},{8,10},{9,11},{10,... | collective-permute-start | bytes 786440 | tf_op jit(solution)/shard_map/R1_/ppermute | solution.py:57
  77.5 2.3 %collective-permute-start.20 = (bf16[1,256,512]{2,1,0:T(8,128)(2,1)S(1)}, bf16[1,256,512]{2,1,0:T(8,128)(2,1)S(1)}, u32[]{:S(2)}, u32[]{:S(2)}) collective-permute-start(bf16[1,256,512]{2,1,0:T(8,128)(2,1)S(1)} %get-tuple-element.64), channel_id=1, source_target_pairs={{0,1},{1,0},{2,3},{3,2},{4,5},{5,4},{6,7},{7,6},{8,9},{9,8},{10,11... | collective-permute-start | bytes 786440 | tf_op jit(solution)/shard_map/H1_/ppermute | solution.py:57
  78.5 1.5 %collective-permute-start.21 = (bf16[1,256,512]{2,1,0:T(8,128)(2,1)S(1)}, bf16[1,256,512]{2,1,0:T(8,128)(2,1)S(1)}, u32[]{:S(2)}, u32[]{:S(2)}) collective-permute-start(bf16[1,256,512]{2,1,0:T(8,128)(2,1)S(1)} %collective-permute-done.17), channel_id=1, source_target_pairs={{0,1},{1,0},{2,3},{3,2},{4,5},{5,4},{6,7},{7,6},{8,9},{9,8},{10,11... | collective-permute-start | bytes 786440 | tf_op jit(solution)/shard_map/F1_/ppermute | solution.py:57
  78.6 7.5 %collective-permute-start.22 = (bf16[1,256,512]{2,1,0:T(8,128)(2,1)S(1)}, bf16[1,256,512]{2,1,0:T(8,128)(2,1)S(1)}, u32[]{:S(2)}, u32[]{:S(2)}) collective-permute-start(bf16[1,256,512]{2,1,0:T(8,128)(2,1)S(1)} %get-tuple-element.67), channel_id=1, source_target_pairs={{0,2},{1,3},{2,0},{3,1},{4,6},{5,7},{6,4},{7,5},{8,10},{9,11},{10,... | collective-permute-start | bytes 786440 | tf_op jit(solution)/shard_map/R2_/ppermute | solution.py:57
  80.0 1.6 %copy-start.4 = (bf16[2048,512]{1,0:T(8,128)(2,1)S(1)}, bf16[2048,512]{1,0:T(8,128)(2,1)}, u32[]{:S(2)}) copy-start(bf16[2048,512]{1,0:T(8,128)(2,1)} %constant.107.clone.refs_4_) | copy-start | bytes 6291460
  86.1 2.4 %collective-permute-start.25 = (bf16[1,256,512]{2,1,0:T(8,128)(2,1)S(1)}, bf16[1,256,512]{2,1,0:T(8,128)(2,1)S(1)}, u32[]{:S(2)}, u32[]{:S(2)}) collective-permute-start(bf16[1,256,512]{2,1,0:T(8,128)(2,1)S(1)} %get-tuple-element.68), channel_id=1, source_target_pairs={{0,1},{1,0},{2,3},{3,2},{4,5},{5,4},{6,7},{7,6},{8,9},{9,8},{10,11... | collective-permute-start | bytes 786440 | tf_op jit(solution)/shard_map/H2_/ppermute | solution.py:57
  87.3 1.5 %collective-permute-start.26 = (bf16[1,256,512]{2,1,0:T(8,128)(2,1)S(1)}, bf16[1,256,512]{2,1,0:T(8,128)(2,1)S(1)}, u32[]{:S(2)}, u32[]{:S(2)}) collective-permute-start(bf16[1,256,512]{2,1,0:T(8,128)(2,1)S(1)} %collective-permute-done.22), channel_id=1, source_target_pairs={{0,1},{1,0},{2,3},{3,2},{4,5},{5,4},{6,7},{7,6},{8,9},{9,8},{10,11... | collective-permute-start | bytes 786440 | tf_op jit(solution)/shard_map/F2_/ppermute | solution.py:57
  87.3 8.4 %collective-permute-start.27 = (bf16[1,256,512]{2,1,0:T(8,128)(2,1)S(1)}, bf16[1,256,512]{2,1,0:T(8,128)(2,1)S(1)}, u32[]{:S(2)}, u32[]{:S(2)}) collective-permute-start(bf16[1,256,512]{2,1,0:T(8,128)(2,1)S(1)} %cross_stack.8), channel_id=1, source_target_pairs={{0,2},{1,3},{2,0},{3,1},{4,6},{5,7},{6,4},{7,5},{8,10},{9,11},{10,... | collective-permute-start | bytes 786440 | tf_op jit(solution)/shard_map/R3_/ppermute | solution.py:57
  95.2 1.7 %collective-permute-start.28 = (bf16[1,256,512]{2,1,0:T(8,128)(2,1)S(1)}, bf16[1,256,512]{2,1,0:T(8,128)(2,1)S(1)}, u32[]{:S(2)}, u32[]{:S(2)}) collective-permute-start(bf16[1,256,512]{2,1,0:T(8,128)(2,1)S(1)} %cross_stack.9), channel_id=1, source_target_pairs={{0,1},{1,0},{2,3},{3,2},{4,5},{5,4},{6,7},{7,6},{8,9},{9,8},{10,11... | collective-permute-start | bytes 786440 | tf_op jit(solution)/shard_map/H3_/ppermute | solution.py:57
  95.7 1.5 %collective-permute-start.29 = (bf16[1,256,512]{2,1,0:T(8,128)(2,1)S(1)}, bf16[1,256,512]{2,1,0:T(8,128)(2,1)S(1)}, u32[]{:S(2)}, u32[]{:S(2)}) collective-permute-start(bf16[1,256,512]{2,1,0:T(8,128)(2,1)S(1)} %collective-permute-done.27), channel_id=1, source_target_pairs={{0,1},{1,0},{2,3},{3,2},{4,5},{5,4},{6,7},{7,6},{8,9},{9,8},{10,11... | collective-permute-start | bytes 786440 | tf_op jit(solution)/shard_map/F3_/ppermute | solution.py:57

commit v5 on v4

--- a/solution.py
+++ b/solution.py
@@ -179,8 +179,8 @@
 def cross_kernel(sides, chunk, windows, meta, place, filled, *refs):
     count = len(sides)
     blocks, flags, lagmap = refs[:3], refs[3], refs[4]
-    outs = refs[-count - 9 : -9]
-    raw, held, live, near, cross, table, result, sems, out_sems = refs[-9:]
+    outs = refs[-count - 10 : -10]
+    raw, held, live, near, mixed, cross, table, result, sems, out_sems = refs[-10:]
     width = near.shape[-1]
     bins = width // 2
     pairs = place.shape[0] // 2
@@ -213,10 +213,15 @@
         for r in range(QUAD):
             for w in range(windows):
                 flag = live[(i - 1) * QUAD + r, w][:, 0:1]
-                near[(i - 1) * QUAD + r, w] = wide[r, w] * flag
+                value = wide[r, w] * flag
+                near[(i - 1) * QUAD + r, w] = value
+                re, im = value[:, :bins], value[:, bins:]
+                mixed[(i - 1) * QUAD + r, w, :, :bins] = re + im
+                mixed[(i - 1) * QUAD + r, w, :, bins:] = re - im
 
     def one(p):
         a, b = near.at[place[p, 0]], near.at[place[p, 1]]
+        mixed_a, mixed_b = mixed.at[place[p, 0]], mixed.at[place[p, 1]]
         live_a, live_b = live.at[place[p, 0]], live.at[place[p, 1]]
         total = live_a[0] * live_b[0]
         for w in range(1, windows):
@@ -224,13 +229,16 @@
         scale = jnp.where(filled[p] > 0, 1.0, 0.0) * (1.0 / jnp.maximum(total, 1.0))
         res, ims = [], []
         for j in range(0, bins, 128):
-            re = im = None
+            here, there = slice(j, j + 128), slice(bins + j, bins + j + 128)
+            first = second = third = None
             for w in range(windows):
-                ra, ia = a[w, :, j : j + 128], a[w, :, bins + j : bins + j + 128]
-                rb, ib = b[w, :, j : j + 128], b[w, :, bins + j : bins + j + 128]
-                x, y = ra * rb + ia * ib, ra * ib - ia * rb
-                re = x if re is None else re + x
-                im = y if im is None else im + y
+                x = a[w, :, here] * b[w, :, here]
+                y = a[w, :, there] * b[w, :, there]
+                z = mixed_a[w, :, here] * mixed_b[w, :, there]
+                first = x if first is None else first + x
+                second = y if second is None else second + y
+                third = z if third is None else third + z
+            re, im = first + second, first - second - third
             res.append(re * scale)
             ims.append(im * scale)
         return res + ims
@@ -284,6 +292,7 @@
             pltpu.VMEM((3, rows, width), jnp.bfloat16),
             pltpu.VMEM(flags.shape, jnp.bfloat16),
             pltpu.VMEM((3 * QUAD, windows, CHANS, 128), jnp.float32),
+            pltpu.VMEM((3 * QUAD, windows, CHANS, width), jnp.float32),
             pltpu.VMEM((3 * QUAD, windows, CHANS, width), jnp.float32),
             pltpu.VMEM((pairs * CHANS // 16, 16, width), jnp.bfloat16),
             pltpu.VMEM((width, LAGS), jnp.bfloat16),
@@ -372,11 +381,11 @@
     sent = exchange(0, 1, core)
     core = after(core, sent)
     own_peer = to_quad_peer(records, 1, "CA_")
-    live = after((dead[None, :] * glitch).astype(jnp.bfloat16).reshape(-1), sent)
-    notes = jnp.concatenate([swap_quads(live, 0, "NE_"), live, swap_quads(live, 1, "NO_")])
-    notes = jnp.concatenate([notes, pairs.reshape(-1).astype(jnp.bfloat16)])
-    size = notes.shape[0]
-    page = jnp.pad(notes, (0, 16 * width - size)).reshape(16, width)
+    live = after((dead[None, :] * glitch).astype(jnp.bfloat16), sent)
+    columns = [swap_quads(live, 0, "NE_"), live, swap_quads(live, 1, "NO_")]
+    columns.append(jnp.pad(pairs.astype(jnp.bfloat16), ((0, 0), (0, block - 2))))
+    page = jnp.concatenate([jnp.pad(x, ((0, 16 - x.shape[0]), (0, 0))) for x in columns], 1)
+    page = jnp.pad(page, ((0, 0), (0, width - page.shape[1])))
     exchange(1, 1, core, page)
     white, near = [], []
 
@@ -389,15 +398,16 @@
 
     whiten_next(0, 1)
     exchange(2, chunks - 2, after(core, white[0]))
-    notes_peer = to_quad_peer(after(notes, white[0]), 1, "NC_")
+    notes_peer = to_quad_peer(after(page, white[0]), 1, "NC_")
     whiten_next(1, 1, notes_peer)
     whiten_next(2, chunks - 2, white[1])
-    pages = [after(part, white[1])[-16:].reshape(-1)[:size] for part in got[1]]
-    notes = jnp.stack([notes, pages[0], notes_peer, pages[1]])
-    flags = notes[:, : 3 * windows * block].reshape(QUAD, 3, windows, block).swapaxes(0, 1)
-    flags = flags.reshape(-1, block)
-
-    listed = notes[:, 3 * windows * block :].astype(jnp.int32).reshape(2, 2, slots, 2)
+    pages = [after(part, white[1])[-16:] for part in got[1]]
+    notes = jnp.stack([page, pages[0], notes_peer, pages[1]])
+    flags = notes[:, :windows, : 3 * block].reshape(QUAD, windows, 3, block)
+    flags = flags.transpose(2, 0, 1, 3).reshape(-1, block)
+
+    listed = notes[:, :slots, 3 * block : 3 * block + 2].astype(jnp.int32)
+    listed = listed.reshape(2, 2, slots, 2)
     listed = listed.swapaxes(0, 1)[::-1].reshape(-1, 2)
     filled = (listed[..., 0] >= 0) & (listed[..., 1] >= 0)
     inside = (listed % QUAD) ^ mine

time: 99.1 us -> 97 us (0.979)
  Pallas kernels: 51.3 us -> 48.1 us
  other arithmetic: 2.39 us -> 3.77 us
  local copies, waits for them, and re-layouts: 5.63 us -> 4.5 us
    pallas_call x5, Pallas kernels: 32.2 us -> 29.1 us  [cross_stack(): pl.pallas_call(functools.partial(cross_kernel, sides, chunk, windows), ou...]
  transfers between devices with their start and end apart: 30 -> 30, of which waited for: 9 -> 10; matrix products, arithmetic and copies ran while one was open for 8% -> 9% of each run, Pallas kernels for 50% -> 49%
where the time goes in v5:
time: 97 us; the launch traced here: 95.8 us
  Pallas kernels  48.1 us (50%)
  starting transfers between devices  30.7 us (32%)
  waiting for transfers between devices  8.41 us (9%)
  local copies, waits for them, and re-layouts  4.5 us (5%)
  other arithmetic  3.77 us (4%)
    pallas_call x5, Pallas kernels, cross_stack(): pl.pallas_call(functools.partial(cross_kernel, sides, chunk, windows), ou...  29.1 us
    ppermute x10, starting transfers between devices, swap_quads(): return lax.ppermute(value, 'chan', pairs)  16.3 us
    ppermute x20, starting transfers between devices, to_quad_peer(): return lax.ppermute(value, 'chan', [(s, s ^ mask) for s in range(count)])  14.3 us
    pallas_call x3, Pallas kernels, whiten(): pl.pallas_call(functools.partial(whiten_kernel, chunks, first), out_shape...  12.7 us
    ppermute x20, waiting for transfers between devices, to_quad_peer(): return lax.ppermute(value, 'chan', [(s, s ^ mask) for s in range(count)])  8.38 us
    pallas_call x4, Pallas kernels, place_stacks(): pl.pallas_call(place_kernel, out_shape=jax.ShapeDtypeStruct(shape, jnp.fl...  6.35 us
    reshape x2, local copies, waits for them, and re-layouts, cut(): return lax.dynamic_slice(split, start, sizes).reshape(-1, width)  1.97 us
  transfers between devices with their start and end apart: 30, of which 10 were waited for; matrix products, arithmetic and copies ran while one was open for 9% of the time, Pallas kernels for 49%

profile of v5, /device:TPU:11, one launch (start us, length us, event | category | flops | bytes accessed | tf_op | source)
XLA Modules:
  0.0 95.8 jit_solution(2371264920461006613)
XLA Ops:
  0.0 0.7 collective-permute-start.4
  0.7 1.0 %dynamic-slice_bitcast_fusion.2 = (bf16[32,2048]{1,0:T(8,128)(2,1)S(1)}, bf16[32,2048]{1,0:T(8,128)(2,1)S(1)}) fusion(bf16[4,2,4,2,8,2048]{5,4,3,2,1,0:T(8,128)(2,1)} %bitcast.66, s32[]{:T(128)S(6)} %select_n.79, s32[]{:T(128)S(6)} %select_n.81, s32[]{:T(128)S(6)} %select_n.80), kind=kLoop, calls=%fused_computation.4 | loop fusion | bytes 524300 | tf_op jit(solution)/shard_map/reshape | solution.py:368
  1.7 1.3 %collective-permute-start.3 = (bf16[32,2048]{1,0:T(8,128)(2,1)S(1)}, bf16[32,2048]{1,0:T(8,128)(2,1)S(1)}, u32[]{:S(2)}, u32[]{:S(2)}) collective-permute-start(bf16[32,2048]{1,0:T(8,128)(2,1)S(1)} %get-tuple-element.38), channel_id=1, source_target_pairs={{0,2},{1,3},{2,0},{3,1},{4,6},{5,7},{6,4},{7,5},{8,10},{9,11},{10,... | collective-permute-start | bytes 393224 | tf_op jit(solution)/shard_map/Y0A_/ppermute | solution.py:57
  3.0 0.7 multiply_convert_fusion
  3.8 4.3 %collective-permute-start.1 = (bf16[4,128]{1,0:T(4,128)(2,1)S(1)}, bf16[4,128]{1,0:T(4,128)(2,1)S(1)}, u32[]{:S(2)}, u32[]{:S(2)}) collective-permute-start(bf16[4,128]{1,0:T(4,128)(2,1)S(1)} %multiply_convert_fusion), channel_id=1, source_target_pairs={{4,8},{5,9},{6,10},{7,11},{8,4},{9,5},{10,6},{11,7},{20,24},{21,25... | collective-permute-start | bytes 3080 | tf_op jit(solution)/shard_map/NO_/ppermute | solution.py:69
  8.2 1.2 %collective-permute-start.5 = (bf16[32,2048]{1,0:T(8,128)(2,1)S(1)}, bf16[32,2048]{1,0:T(8,128)(2,1)S(1)}, u32[]{:S(2)}, u32[]{:S(2)}) collective-permute-start(bf16[32,2048]{1,0:T(8,128)(2,1)S(1)} %get-tuple-element.42), channel_id=1, source_target_pairs={{0,3},{1,2},{2,1},{3,0},{4,7},{5,6},{6,5},{7,4},{8,11},{9,10},{10,... | collective-permute-start | bytes 393224 | tf_op jit(solution)/shard_map/Y0B_/ppermute | solution.py:57
  9.5 1.0 %dynamic-slice_bitcast_fusion = (bf16[32,2048]{1,0:T(8,128)(2,1)S(1)}, bf16[32,2048]{1,0:T(8,128)(2,1)S(1)}) fusion(bf16[4,2,4,2,8,2048]{5,4,3,2,1,0:T(8,128)(2,1)} %bitcast.67, s32[]{:T(128)S(6)} %select_n.79, s32[]{:T(128)S(6)} %select_n.83, s32[]{:T(128)S(6)} %select_n.82), kind=kLoop, calls=%fused_computation.2 | loop fusion | bytes 524300 | tf_op jit(solution)/shard_map/reshape | solution.py:368
  10.5 0.7 convert_element_type.19
  11.3 0.6 pad_bitcast_fusion
  11.9 0.7 pad_maximum_fusion
  12.6 1.2 %collective-permute-start.2 = (bf16[48,2048]{1,0:T(8,128)(2,1)}, bf16[48,2048]{1,0:T(8,128)(2,1)S(1)}, u32[]{:S(2)}, u32[]{:S(2)}) collective-permute-start(bf16[48,2048]{1,0:T(8,128)(2,1)} %get-tuple-element.41), channel_id=1, source_target_pairs={{0,2},{1,3},{2,0},{3,1},{4,6},{5,7},{6,4},{7,5},{8,10},{9,11},{10,... | collective-permute-start | bytes 589832 | tf_op jit(solution)/shard_map/Y1A_/ppermute | solution.py:57
  14.2 3.7 %whiten.3.refs_1_ = bf16[128,2048]{1,0:T(8,128)(2,1)S(1)} custom-call(s32[2]{0:T(128)S(1)} %pad_add_fusion.1.meta, bf16[4,128,2048]{2,1,0:T(8,128)(2,1)S(1)} %copy-done, bf16[32,2048]{1,0:T(8,128)(2,1)S(1)} %collective-permute-done.3.got, bf16[4,128,2048]{2,1,0:T(8,128)(2,1)} %collective-permute-done.4.own_peer, ...), custom_call_target="tpu_custom_call" | custom-call | flops 2000000000 | bytes 1024 | tf_op jit(solution)/shard_map/whiten/pallas_call | solution.py:156
  18.0 3.2 %collective-permute-start.11 = (bf16[128,2048]{1,0:T(8,128)(2,1)S(1)}, bf16[128,2048]{1,0:T(8,128)(2,1)}, u32[]{:S(2)}, u32[]{:S(2)}) collective-permute-start(bf16[128,2048]{1,0:T(8,128)(2,1)S(1)} %whiten.3.refs_1_), channel_id=1, source_target_pairs={{4,8},{5,9},{6,10},{7,11},{8,4},{9,5},{10,6},{11,7},{20,24},{21,25... | collective-permute-start | bytes 1572872 | tf_op jit(solution)/shard_map/Z0O_/ppermute | solution.py:69
  21.3 0.8 constant_dynamic-slice_fusion
  22.2 0.5 collective-permute-done.6
  22.9 1.6 %collective-permute-start.9 = (bf16[64,2048]{1,0:T(8,128)(2,1)}, bf16[64,2048]{1,0:T(8,128)(2,1)}, u32[]{:S(2)}, u32[]{:S(2)}) collective-permute-start(bf16[64,2048]{1,0:T(8,128)(2,1)} %bitcast.19), channel_id=1, source_target_pairs={{0,3},{1,2},{2,1},{3,0},{4,7},{5,6},{6,5},{7,4},{8,11},{9,10},{10,... | collective-permute-start | bytes 786440 | tf_op jit(solution)/shard_map/Y2B_/ppermute | solution.py:57
  24.5 3.7 %whiten.4.refs_1_ = bf16[128,2048]{1,0:T(8,128)(2,1)S(1)} custom-call(s32[2]{0:T(128)S(1)} %pad_add_fusion.1.meta, bf16[4,128,2048]{2,1,0:T(8,128)(2,1)S(1)} %copy-done, bf16[48,2048]{1,0:T(8,128)(2,1)S(1)} %collective-permute-done.2.got, bf16[4,128,2048]{2,1,0:T(8,128)(2,1)} %collective-permute-done.4.own_peer, ...), custom_call_target="tpu_custom_call" | custom-call | flops 2000000000 | bytes 1024 | tf_op jit(solution)/shard_map/whiten/pallas_call | solution.py:156
  28.2 0.6 slice_bitcast_fusion
  28.9 0.7 maximum_convert_fusion
  29.8 0.8 fusion.25
  31.0 2.6 %collective-permute-start.14 = (bf16[128,2048]{1,0:T(8,128)(2,1)S(1)}, bf16[128,2048]{1,0:T(8,128)(2,1)S(1)}, u32[]{:S(2)}, u32[]{:S(2)}) collective-permute-start(bf16[128,2048]{1,0:T(8,128)(2,1)S(1)} %whiten.4.refs_1_), channel_id=1, source_target_pairs={{4,8},{5,9},{6,10},{7,11},{8,4},{9,5},{10,6},{11,7},{20,24},{21,25... | collective-permute-start | bytes 1572872 | tf_op jit(solution)/shard_map/Z1O_/ppermute | solution.py:69
  33.6 3.2 %collective-permute-done.9.got_peer = bf16[64,2048]{1,0:T(8,128)(2,1)} collective-permute-done((bf16[64,2048]{1,0:T(8,128)(2,1)}, bf16[64,2048]{1,0:T(8,128)(2,1)}, u32[]{:S(2)}, u32[]{:S(2)}) %collective-permute-start.9) | collective-permute-done | bytes 262176 | tf_op jit(solution)/shard_map/Y2B_/ppermute | solution.py:57
  36.8 5.3 %whiten.5 = (bf16[128,2048]{1,0:T(8,128)(2,1)}, bf16[128,2048]{1,0:T(8,128)(2,1)S(1)}) custom-call(s32[2]{0:T(128)S(1)} %pad_add_fusion.1.meta, bf16[4,128,2048]{2,1,0:T(8,128)(2,1)S(1)} %copy-done, bf16[64,2048]{1,0:T(8,128)(2,1)} %collective-permute-done.8.got, bf16[4,128,2048]{2,1,0:T(8,128)(2,1)} %collective-permute-done.4.own_peer, ...), custom_call_target="tpu_custom_call" | custom-call | flops 4000000000 | bytes 1024 | tf_op jit(solution)/shard_map/whiten/pallas_call | solution.py:156
  42.3 2.7 %collective-permute-start.19 = (bf16[128,2048]{1,0:T(8,128)(2,1)}, bf16[128,2048]{1,0:T(8,128)(2,1)}, u32[]{:S(2)}, u32[]{:S(2)}) collective-permute-start(bf16[128,2048]{1,0:T(8,128)(2,1)} %get-tuple-element.52.refs_1_), channel_id=1, source_target_pairs={{4,8},{5,9},{6,10},{7,11},{8,4},{9,5},{10,6},{11,7},{20,24},{21,25... | collective-permute-start | bytes 1572872 | tf_op jit(solution)/shard_map/Z2O_/ppermute | solution.py:69
  45.0 7.0 %cross_stack.5 = (bf16[1,256,512]{2,1,0:T(8,128)(2,1)S(1)}, bf16[1,256,512]{2,1,0:T(8,128)(2,1)S(1)}) custom-call(s32[2]{0:T(128)S(1)} %pad_add_fusion.1.meta, s32[64,2]{1,0:T(8,128)S(1)} %fusion.7.place, s32[64]{0:T(128)S(1)} %get-tuple-element.71.filled, bf16[128,2048]{1,0:T(8,128)(2,1)} %collective-permute-done.10.refs_0_, ...), custom_call_target="tpu_custom_call" | custom-call | flops 6400000000 | bytes 1024 | tf_op jit(solution)/shard_map/cross_stack/pallas_call | solution.py:286
  52.0 0.8 collective-permute-start.12
  52.9 6.3 %cross_stack.6 = (bf16[1,256,512]{2,1,0:T(8,128)(2,1)S(1)}, bf16[1,256,512]{2,1,0:T(8,128)(2,1)S(1)}) custom-call(s32[2]{0:T(128)S(1)} %pad_add_fusion.1.meta, s32[64,2]{1,0:T(8,128)S(1)} %fusion.7.place, s32[64]{0:T(128)S(1)} %get-tuple-element.71.filled, bf16[128,2048]{1,0:T(8,128)(2,1)S(1)} %collective-permute-done.13.refs_0_, ...), custom_call_target="tpu_custom_call" | custom-call | flops 6400000000 | bytes 1024 | tf_op jit(solution)/shard_map/cross_stack/pallas_call | solution.py:286
  59.5 1.3 %collective-permute-start.15 = (bf16[1,256,512]{2,1,0:T(8,128)(2,1)S(1)}, bf16[1,256,512]{2,1,0:T(8,128)(2,1)S(1)}, u32[]{:S(2)}, u32[]{:S(2)}) collective-permute-start(bf16[1,256,512]{2,1,0:T(8,128)(2,1)S(1)} %get-tuple-element.59), channel_id=1, source_target_pairs={{0,1},{1,0},{2,3},{3,2},{4,5},{5,4},{6,7},{7,6},{8,9},{9,8},{10,11... | collective-permute-start | bytes 786440 | tf_op jit(solution)/shard_map/H0_/ppermute | solution.py:57
  60.9 1.1 %collective-permute-done.15 = bf16[1,256,512]{2,1,0:T(8,128)(2,1)S(1)} collective-permute-done((bf16[1,256,512]{2,1,0:T(8,128)(2,1)S(1)}, bf16[1,256,512]{2,1,0:T(8,128)(2,1)S(1)}, u32[]{:S(2)}, u32[]{:S(2)}) %collective-permute-start.15) | collective-permute-done | bytes 262176 | tf_op jit(solution)/shard_map/H0_/ppermute | solution.py:57
  62.0 2.8 %collective-permute-start.24 = (bf16[128,2048]{1,0:T(8,128)(2,1)S(1)}, bf16[128,2048]{1,0:T(8,128)(2,1)S(1)}, u32[]{:S(2)}, u32[]{:S(2)}) collective-permute-start(bf16[128,2048]{1,0:T(8,128)(2,1)S(1)} %copy-done.3), channel_id=1, source_target_pairs={{4,8},{5,9},{6,10},{7,11},{8,4},{9,5},{10,6},{11,7},{20,24},{21,25... | collective-permute-start | bytes 1572872 | tf_op jit(solution)/shard_map/Z3O_/ppermute | solution.py:69
  64.8 1.1 %collective-permute-start.17 = (bf16[1,256,512]{2,1,0:T(8,128)(2,1)S(1)}, bf16[1,256,512]{2,1,0:T(8,128)(2,1)S(1)}, u32[]{:S(2)}, u32[]{:S(2)}) collective-permute-start(bf16[1,256,512]{2,1,0:T(8,128)(2,1)S(1)} %get-tuple-element.62), channel_id=1, source_target_pairs={{0,2},{1,3},{2,0},{3,1},{4,6},{5,7},{6,4},{7,5},{8,10},{9,11},{10,... | collective-permute-start | bytes 786440 | tf_op jit(solution)/shard_map/R1_/ppermute | solution.py:57
  65.9 1.6 %place_stacks.4.refs_0_ = f32[16,2,64,512]{3,2,1,0:T(8,128)} custom-call(s32[4]{0:T(128)S(1)} %pad_add_fusion.slot, bf16[1,2,128,512]{3,2,1,0:T(8,128)(2,1)S(1)} %bitcast.86, bf16[1,2,128,512]{3,2,1,0:T(8,128)(2,1)S(1)} %bitcast.87, bf16[1,2,128,512]{3,2,1,0:T(8,128)(2,1)S(1)} %bitcast.88, bf16[1,2,128,512]{3,2,1,0:T(8,128)(2,1)S(1)} %bitcast.89), custom_call_target="tpu_custom_call" | custom-call | flops 1500000000 | bytes 1024 | tf_op jit(solution)/shard_map/place_stacks/pallas_call | solution.py:329
  67.5 7.0 %cross_stack.7 = (bf16[1,256,512]{2,1,0:T(8,128)(2,1)S(1)}, bf16[1,256,512]{2,1,0:T(8,128)(2,1)S(1)}) custom-call(s32[2]{0:T(128)S(1)} %pad_add_fusion.1.meta, s32[64,2]{1,0:T(8,128)S(1)} %fusion.7.place, s32[64]{0:T(128)S(1)} %get-tuple-element.71.filled, bf16[128,2048]{1,0:T(8,128)(2,1)} %collective-permute-done.18.refs_0_, ...), custom_call_target="tpu_custom_call" | custom-call | flops 6400000000 | bytes 1024 | tf_op jit(solution)/shard_map/cross_stack/pallas_call | solution.py:286
  74.5 1.0 %collective-permute-start.20 = (bf16[1,256,512]{2,1,0:T(8,128)(2,1)S(1)}, bf16[1,256,512]{2,1,0:T(8,128)(2,1)S(1)}, u32[]{:S(2)}, u32[]{:S(2)}) collective-permute-start(bf16[1,256,512]{2,1,0:T(8,128)(2,1)S(1)} %get-tuple-element.64), channel_id=1, source_target_pairs={{0,1},{1,0},{2,3},{3,2},{4,5},{5,4},{6,7},{7,6},{8,9},{9,8},{10,11... | collective-permute-start | bytes 786440 | tf_op jit(solution)/shard_map/H1_/ppermute | solution.py:57
  75.6 0.4 collective-permute-start.22
  76.0 0.6 collective-permute-done.20
  76.7 0.4 collective-permute-done.21
  77.0 1.6 %place_stacks.5.refs_0_ = f32[16,2,64,512]{3,2,1,0:T(8,128)} custom-call(s32[4]{0:T(128)S(1)} %pad_add_fusion.slot, bf16[1,2,128,512]{3,2,1,0:T(8,128)(2,1)S(1)} %bitcast.69, bf16[1,2,128,512]{3,2,1,0:T(8,128)(2,1)S(1)} %bitcast.72, bf16[1,2,128,512]{3,2,1,0:T(8,128)(2,1)S(1)} %bitcast.75, ...), custom_call_target="tpu_custom_call", output_to_operand_aliasing={{}: (5, {})} | custom-call | flops 1500000000 | bytes 1024 | tf_op jit(solution)/shard_map/place_stacks/pallas_call | solution.py:329
  78.6 4.5 %cross_stack.8 = bf16[1,256,512]{2,1,0:T(8,128)(2,1)S(1)} custom-call(s32[2]{0:T(128)S(1)} %pad_add_fusion.1.meta, s32[64,2]{1,0:T(8,128)S(1)} %fusion.7.place, s32[64]{0:T(128)S(1)} %get-tuple-element.71.filled, bf16[128,2048]{1,0:T(8,128)(2,1)S(1)} %collective-permute-done.23.refs_0_, bf16[128,2048]{1,0:T(8,128)(2,1)S(1)} %copy-done.3, ...), custom_call_target="tpu_custom_call" | custom-call | flops 3200000000 | bytes 1024 | tf_op jit(solution)/shard_map/cross_stack/pallas_call | solution.py:286
  83.1 1.2 %collective-permute-start.25 = (bf16[1,256,512]{2,1,0:T(8,128)(2,1)S(1)}, bf16[1,256,512]{2,1,0:T(8,128)(2,1)S(1)}, u32[]{:S(2)}, u32[]{:S(2)}) collective-permute-start(bf16[1,256,512]{2,1,0:T(8,128)(2,1)S(1)} %get-tuple-element.68), channel_id=1, source_target_pairs={{0,1},{1,0},{2,3},{3,2},{4,5},{5,4},{6,7},{7,6},{8,9},{9,8},{10,11... | collective-permute-start | bytes 786440 | tf_op jit(solution)/shard_map/H2_/ppermute | solution.py:57
  84.3 0.4 collective-permute-start.27
  84.8 0.7 collective-permute-done.25
  85.8 1.6 %place_stacks.6.refs_0_ = f32[16,2,64,512]{3,2,1,0:T(8,128)} custom-call(s32[4]{0:T(128)S(1)} %pad_add_fusion.slot, bf16[1,2,128,512]{3,2,1,0:T(8,128)(2,1)S(1)} %bitcast.70, bf16[1,2,128,512]{3,2,1,0:T(8,128)(2,1)S(1)} %bitcast.71, bf16[1,2,128,512]{3,2,1,0:T(8,128)(2,1)S(1)} %bitcast.77, ...), custom_call_target="tpu_custom_call", output_to_operand_aliasing={{}: (5, {})} | custom-call | flops 1500000000 | bytes 1024 | tf_op jit(solution)/shard_map/place_stacks/pallas_call | solution.py:329
  87.4 4.3 %cross_stack.9 = bf16[1,256,512]{2,1,0:T(8,128)(2,1)S(1)} custom-call(s32[2]{0:T(128)S(1)} %pad_add_fusion.1.meta, s32[64,2]{1,0:T(8,128)S(1)} %fusion.7.place, s32[64]{0:T(128)S(1)} %get-tuple-element.71.filled, bf16[128,2048]{1,0:T(8,128)(2,1)S(1)} %collective-permute-done.23.refs_0_, bf16[128,2048]{1,0:T(8,128)(2,1)S(1)} %copy-done.3, ...), custom_call_target="tpu_custom_call" | custom-call | flops 3200000000 | bytes 1024 | tf_op jit(solution)/shard_map/cross_stack/pallas_call | solution.py:286
  91.7 0.4 collective-permute-start.28
  92.2 0.9 collective-permute-start.29
  93.3 0.9 collective-permute-done.29
  94.2 1.6 %place_stacks.7 = f32[16,2,64,512]{3,2,1,0:T(8,128)} custom-call(s32[4]{0:T(128)S(1)} %pad_add_fusion.slot, bf16[1,2,128,512]{3,2,1,0:T(8,128)(2,1)S(1)} %bitcast.74, bf16[1,2,128,512]{3,2,1,0:T(8,128)(2,1)S(1)} %bitcast.73, bf16[1,2,128,512]{3,2,1,0:T(8,128)(2,1)S(1)} %bitcast.76, ...), custom_call_target="tpu_custom_call", output_to_operand_aliasing={{}: (5, {})} | custom-call | flops 1500000000 | bytes 1024 | tf_op jit(solution)/shard_map/place_stacks/pallas_call | solution.py:329
  (58 shorter events, 3.1 us)
Async XLA Ops:
  0.0 14.2 %copy-start.1 = (f32[2,1024]{1,0:T(2,128)S(1)}, f32[2,1024]{1,0:T(2,128)}, u32[]{:S(2)}) copy-start(f32[2,1024]{1,0:T(2,128)} %constant.106.clone.curve) | copy-start | bytes 24580
  0.0 14.2 %copy-start = (bf16[4,128,2048]{2,1,0:T(8,128)(2,1)S(1)}, bf16[4,128,2048]{2,1,0:T(8,128)(2,1)}, u32[]{:S(2)}) copy-start(bf16[4,128,2048]{2,1,0:T(8,128)(2,1)} %own.5) | copy-start | bytes 6291460
  0.0 14.2 %collective-permute-start.4 = (bf16[4,128,2048]{2,1,0:T(8,128)(2,1)}, bf16[4,128,2048]{2,1,0:T(8,128)(2,1)}, u32[]{:S(2)}, u32[]{:S(2)}) collective-permute-start(bf16[4,128,2048]{2,1,0:T(8,128)(2,1)} %own.5), channel_id=1, source_target_pairs={{0,1},{1,0},{2,3},{3,2},{4,5},{5,4},{6,7},{7,6},{8,9},{9,8},{10,11... | collective-permute-start | bytes 6291464 | tf_op jit(solution)/shard_map/CA_/ppermute | solution.py:57
  1.7 12.5 %collective-permute-start.3 = (bf16[32,2048]{1,0:T(8,128)(2,1)S(1)}, bf16[32,2048]{1,0:T(8,128)(2,1)S(1)}, u32[]{:S(2)}, u32[]{:S(2)}) collective-permute-start(bf16[32,2048]{1,0:T(8,128)(2,1)S(1)} %get-tuple-element.38), channel_id=1, source_target_pairs={{0,2},{1,3},{2,0},{3,1},{4,6},{5,7},{6,4},{7,5},{8,10},{9,11},{10,... | collective-permute-start | bytes 393224 | tf_op jit(solution)/shard_map/Y0A_/ppermute | solution.py:57
  3.7 7.6 %collective-permute-start = (bf16[4,128]{1,0:T(4,128)(2,1)S(1)}, bf16[4,128]{1,0:T(4,128)(2,1)S(1)}, u32[]{:S(2)}, u32[]{:S(2)}) collective-permute-start(bf16[4,128]{1,0:T(4,128)(2,1)S(1)} %multiply_convert_fusion), channel_id=1, source_target_pairs={{0,4},{1,5},{2,6},{3,7},{4,0},{5,1},{6,2},{7,3},{8,12},{9,13},{10,... | collective-permute-start | bytes 3080 | tf_op jit(solution)/shard_map/NE_/ppermute | solution.py:69
  3.8 7.4 %collective-permute-start.1 = (bf16[4,128]{1,0:T(4,128)(2,1)S(1)}, bf16[4,128]{1,0:T(4,128)(2,1)S(1)}, u32[]{:S(2)}, u32[]{:S(2)}) collective-permute-start(bf16[4,128]{1,0:T(4,128)(2,1)S(1)} %multiply_convert_fusion), channel_id=1, source_target_pairs={{4,8},{5,9},{6,10},{7,11},{8,4},{9,5},{10,6},{11,7},{20,24},{21,25... | collective-permute-start | bytes 3080 | tf_op jit(solution)/shard_map/NO_/ppermute | solution.py:69
  8.2 6.0 %collective-permute-start.5 = (bf16[32,2048]{1,0:T(8,128)(2,1)S(1)}, bf16[32,2048]{1,0:T(8,128)(2,1)S(1)}, u32[]{:S(2)}, u32[]{:S(2)}) collective-permute-start(bf16[32,2048]{1,0:T(8,128)(2,1)S(1)} %get-tuple-element.42), channel_id=1, source_target_pairs={{0,3},{1,2},{2,1},{3,0},{4,7},{5,6},{6,5},{7,4},{8,11},{9,10},{10,... | collective-permute-start | bytes 393224 | tf_op jit(solution)/shard_map/Y0B_/ppermute | solution.py:57
  12.6 10.3 %collective-permute-start.2 = (bf16[48,2048]{1,0:T(8,128)(2,1)}, bf16[48,2048]{1,0:T(8,128)(2,1)S(1)}, u32[]{:S(2)}, u32[]{:S(2)}) collective-permute-start(bf16[48,2048]{1,0:T(8,128)(2,1)} %get-tuple-element.41), channel_id=1, source_target_pairs={{0,2},{1,3},{2,0},{3,1},{4,6},{5,7},{6,4},{7,5},{8,10},{9,11},{10,... | collective-permute-start | bytes 589832 | tf_op jit(solution)/shard_map/Y1A_/ppermute | solution.py:57
  13.8 10.6 %collective-permute-start.7 = (bf16[48,2048]{1,0:T(8,128)(2,1)S(1)}, bf16[48,2048]{1,0:T(8,128)(2,1)S(1)}, u32[]{:S(2)}, u32[]{:S(2)}) collective-permute-start(bf16[48,2048]{1,0:T(8,128)(2,1)S(1)} %get-tuple-element.45), channel_id=1, source_target_pairs={{0,3},{1,2},{2,1},{3,0},{4,7},{5,6},{6,5},{7,4},{8,11},{9,10},{10,... | collective-permute-start | bytes 589832 | tf_op jit(solution)/shard_map/Y1B_/ppermute | solution.py:57
  17.9 24.3 %collective-permute-start.10 = (bf16[128,2048]{1,0:T(8,128)(2,1)S(1)}, bf16[128,2048]{1,0:T(8,128)(2,1)}, u32[]{:S(2)}, u32[]{:S(2)}) collective-permute-start(bf16[128,2048]{1,0:T(8,128)(2,1)S(1)} %whiten.3.refs_1_), channel_id=1, source_target_pairs={{0,4},{1,5},{2,6},{3,7},{4,0},{5,1},{6,2},{7,3},{8,12},{9,13},{10,... | collective-permute-start | bytes 1572872 | tf_op jit(solution)/shard_map/Z0E_/ppermute | solution.py:69
  18.0 27.0 %collective-permute-start.11 = (bf16[128,2048]{1,0:T(8,128)(2,1)S(1)}, bf16[128,2048]{1,0:T(8,128)(2,1)}, u32[]{:S(2)}, u32[]{:S(2)}) collective-permute-start(bf16[128,2048]{1,0:T(8,128)(2,1)S(1)} %whiten.3.refs_1_), channel_id=1, source_target_pairs={{4,8},{5,9},{6,10},{7,11},{8,4},{9,5},{10,6},{11,7},{20,24},{21,25... | collective-permute-start | bytes 1572872 | tf_op jit(solution)/shard_map/Z0O_/ppermute | solution.py:69
  21.2 1.5 %collective-permute-start.6 = (bf16[16,2048]{1,0:T(8,128)(2,1)S(1)}, bf16[16,2048]{1,0:T(8,128)(2,1)}, u32[]{:S(2)}, u32[]{:S(2)}) collective-permute-start(bf16[16,2048]{1,0:T(8,128)(2,1)S(1)} %get-tuple-element.43), channel_id=1, source_target_pairs={{0,1},{1,0},{2,3},{3,2},{4,5},{5,4},{6,7},{7,6},{8,9},{9,8},{10,11... | collective-permute-start | bytes 196616 | tf_op jit(solution)/shard_map/NC_/ppermute | solution.py:57
  22.2 6.7 %copy-start.5 = (bf16[1,16,2048]{2,1,0:T(8,128)(2,1)S(1)}, bf16[1,16,2048]{2,1,0:T(8,128)(2,1)}, u32[]{:S(2)}) copy-start(bf16[1,16,2048]{2,1,0:T(8,128)(2,1)} %get-tuple-element.81) | copy-start | bytes 196612
  22.7 8.3 %collective-permute-start.8 = (bf16[64,2048]{1,0:T(8,128)(2,1)}, bf16[64,2048]{1,0:T(8,128)(2,1)}, u32[]{:S(2)}, u32[]{:S(2)}) collective-permute-start(bf16[64,2048]{1,0:T(8,128)(2,1)} %bitcast.18), channel_id=1, source_target_pairs={{0,2},{1,3},{2,0},{3,1},{4,6},{5,7},{6,4},{7,5},{8,10},{9,11},{10,... | collective-permute-start | bytes 786440 | tf_op jit(solution)/shard_map/Y2A_/ppermute | solution.py:57
  22.9 13.9 %collective-permute-start.9 = (bf16[64,2048]{1,0:T(8,128)(2,1)}, bf16[64,2048]{1,0:T(8,128)(2,1)}, u32[]{:S(2)}, u32[]{:S(2)}) collective-permute-start(bf16[64,2048]{1,0:T(8,128)(2,1)} %bitcast.19), channel_id=1, source_target_pairs={{0,3},{1,2},{2,1},{3,0},{4,7},{5,6},{6,5},{7,4},{8,11},{9,10},{10,... | collective-permute-start | bytes 786440 | tf_op jit(solution)/shard_map/Y2B_/ppermute | solution.py:57
  30.6 22.3 %collective-permute-start.13 = (bf16[128,2048]{1,0:T(8,128)(2,1)S(1)}, bf16[128,2048]{1,0:T(8,128)(2,1)S(1)}, u32[]{:S(2)}, u32[]{:S(2)}) collective-permute-start(bf16[128,2048]{1,0:T(8,128)(2,1)S(1)} %whiten.4.refs_1_), channel_id=1, source_target_pairs={{0,4},{1,5},{2,6},{3,7},{4,0},{5,1},{6,2},{7,3},{8,12},{9,13},{10,... | collective-permute-start | bytes 1572872 | tf_op jit(solution)/shard_map/Z1E_/ppermute | solution.py:69
  31.0 21.9 %collective-permute-start.14 = (bf16[128,2048]{1,0:T(8,128)(2,1)S(1)}, bf16[128,2048]{1,0:T(8,128)(2,1)S(1)}, u32[]{:S(2)}, u32[]{:S(2)}) collective-permute-start(bf16[128,2048]{1,0:T(8,128)(2,1)S(1)} %whiten.4.refs_1_), channel_id=1, source_target_pairs={{4,8},{5,9},{6,10},{7,11},{8,4},{9,5},{10,6},{11,7},{20,24},{21,25... | collective-permute-start | bytes 1572872 | tf_op jit(solution)/shard_map/Z1O_/ppermute | solution.py:69
  42.1 9.9 %copy-start.2 = (bf16[128,2048]{1,0:T(8,128)(2,1)}, bf16[128,2048]{1,0:T(8,128)(2,1)S(1)}, u32[]{:S(2)}) copy-start(bf16[128,2048]{1,0:T(8,128)(2,1)S(1)} %get-tuple-element.53.refs_1_) | copy-start | bytes 1572868
  42.1 25.4 %collective-permute-start.18 = (bf16[128,2048]{1,0:T(8,128)(2,1)}, bf16[128,2048]{1,0:T(8,128)(2,1)}, u32[]{:S(2)}, u32[]{:S(2)}) collective-permute-start(bf16[128,2048]{1,0:T(8,128)(2,1)} %get-tuple-element.52.refs_1_), channel_id=1, source_target_pairs={{0,4},{1,5},{2,6},{3,7},{4,0},{5,1},{6,2},{7,3},{8,12},{9,13},{10,... | collective-permute-start | bytes 1572872 | tf_op jit(solution)/shard_map/Z2E_/ppermute | solution.py:69
  42.3 25.2 %collective-permute-start.19 = (bf16[128,2048]{1,0:T(8,128)(2,1)}, bf16[128,2048]{1,0:T(8,128)(2,1)}, u32[]{:S(2)}, u32[]{:S(2)}) collective-permute-start(bf16[128,2048]{1,0:T(8,128)(2,1)} %get-tuple-element.52.refs_1_), channel_id=1, source_target_pairs={{4,8},{5,9},{6,10},{7,11},{8,4},{9,5},{10,6},{11,7},{20,24},{21,25... | collective-permute-start | bytes 1572872 | tf_op jit(solution)/shard_map/Z2O_/ppermute | solution.py:69
  52.0 8.9 %copy-start.3 = (bf16[128,2048]{1,0:T(8,128)(2,1)S(1)}, bf16[128,2048]{1,0:T(8,128)(2,1)}, u32[]{:S(2)}) copy-start(bf16[128,2048]{1,0:T(8,128)(2,1)} %copy-done.2) | copy-start | bytes 1572868
  52.0 7.4 %collective-permute-start.12 = (bf16[1,256,512]{2,1,0:T(8,128)(2,1)S(1)}, bf16[1,256,512]{2,1,0:T(8,128)(2,1)S(1)}, u32[]{:S(2)}, u32[]{:S(2)}) collective-permute-start(bf16[1,256,512]{2,1,0:T(8,128)(2,1)S(1)} %get-tuple-element.57), channel_id=1, source_target_pairs={{0,2},{1,3},{2,0},{3,1},{4,6},{5,7},{6,4},{7,5},{8,10},{9,11},{10,... | collective-permute-start | bytes 786440 | tf_op jit(solution)/shard_map/R0_/ppermute | solution.py:57
  59.5 2.5 %collective-permute-start.15 = (bf16[1,256,512]{2,1,0:T(8,128)(2,1)S(1)}, bf16[1,256,512]{2,1,0:T(8,128)(2,1)S(1)}, u32[]{:S(2)}, u32[]{:S(2)}) collective-permute-start(bf16[1,256,512]{2,1,0:T(8,128)(2,1)S(1)} %get-tuple-element.59), channel_id=1, source_target_pairs={{0,1},{1,0},{2,3},{3,2},{4,5},{5,4},{6,7},{7,6},{8,9},{9,8},{10,11... | collective-permute-start | bytes 786440 | tf_op jit(solution)/shard_map/H0_/ppermute | solution.py:57
  60.8 4.0 %collective-permute-start.16 = (bf16[1,256,512]{2,1,0:T(8,128)(2,1)S(1)}, bf16[1,256,512]{2,1,0:T(8,128)(2,1)S(1)}, u32[]{:S(2)}, u32[]{:S(2)}) collective-permute-start(bf16[1,256,512]{2,1,0:T(8,128)(2,1)S(1)} %collective-permute-done.12), channel_id=1, source_target_pairs={{0,1},{1,0},{2,3},{3,2},{4,5},{5,4},{6,7},{7,6},{8,9},{9,8},{10,11... | collective-permute-start | bytes 786440 | tf_op jit(solution)/shard_map/F0_/ppermute | solution.py:57
  60.9 17.7 %collective-permute-start.23 = (bf16[128,2048]{1,0:T(8,128)(2,1)S(1)}, bf16[128,2048]{1,0:T(8,128)(2,1)S(1)}, u32[]{:S(2)}, u32[]{:S(2)}) collective-permute-start(bf16[128,2048]{1,0:T(8,128)(2,1)S(1)} %copy-done.3), channel_id=1, source_target_pairs={{0,4},{1,5},{2,6},{3,7},{4,0},{5,1},{6,2},{7,3},{8,12},{9,13},{10,... | collective-permute-start | bytes 1572872 | tf_op jit(solution)/shard_map/Z3E_/ppermute | solution.py:69
  62.0 16.6 %collective-permute-start.24 = (bf16[128,2048]{1,0:T(8,128)(2,1)S(1)}, bf16[128,2048]{1,0:T(8,128)(2,1)S(1)}, u32[]{:S(2)}, u32[]{:S(2)}) collective-permute-start(bf16[128,2048]{1,0:T(8,128)(2,1)S(1)} %copy-done.3), channel_id=1, source_target_pairs={{4,8},{5,9},{6,10},{7,11},{8,4},{9,5},{10,6},{11,7},{20,24},{21,25... | collective-permute-start | bytes 1572872 | tf_op jit(solution)/shard_map/Z3O_/ppermute | solution.py:69
  64.8 9.7 %collective-permute-start.17 = (bf16[1,256,512]{2,1,0:T(8,128)(2,1)S(1)}, bf16[1,256,512]{2,1,0:T(8,128)(2,1)S(1)}, u32[]{:S(2)}, u32[]{:S(2)}) collective-permute-start(bf16[1,256,512]{2,1,0:T(8,128)(2,1)S(1)} %get-tuple-element.62), channel_id=1, source_target_pairs={{0,2},{1,3},{2,0},{3,1},{4,6},{5,7},{6,4},{7,5},{8,10},{9,11},{10,... | collective-permute-start | bytes 786440 | tf_op jit(solution)/shard_map/R1_/ppermute | solution.py:57
  74.5 2.2 %collective-permute-start.20 = (bf16[1,256,512]{2,1,0:T(8,128)(2,1)S(1)}, bf16[1,256,512]{2,1,0:T(8,128)(2,1)S(1)}, u32[]{:S(2)}, u32[]{:S(2)}) collective-permute-start(bf16[1,256,512]{2,1,0:T(8,128)(2,1)S(1)} %get-tuple-element.64), channel_id=1, source_target_pairs={{0,1},{1,0},{2,3},{3,2},{4,5},{5,4},{6,7},{7,6},{8,9},{9,8},{10,11... | collective-permute-start | bytes 786440 | tf_op jit(solution)/shard_map/H1_/ppermute | solution.py:57
  75.5 1.5 %collective-permute-start.21 = (bf16[1,256,512]{2,1,0:T(8,128)(2,1)S(1)}, bf16[1,256,512]{2,1,0:T(8,128)(2,1)S(1)}, u32[]{:S(2)}, u32[]{:S(2)}) collective-permute-start(bf16[1,256,512]{2,1,0:T(8,128)(2,1)S(1)} %collective-permute-done.17), channel_id=1, source_target_pairs={{0,1},{1,0},{2,3},{3,2},{4,5},{5,4},{6,7},{7,6},{8,9},{9,8},{10,11... | collective-permute-start | bytes 786440 | tf_op jit(solution)/shard_map/F1_/ppermute | solution.py:57
  75.6 7.5 %collective-permute-start.22 = (bf16[1,256,512]{2,1,0:T(8,128)(2,1)S(1)}, bf16[1,256,512]{2,1,0:T(8,128)(2,1)S(1)}, u32[]{:S(2)}, u32[]{:S(2)}) collective-permute-start(bf16[1,256,512]{2,1,0:T(8,128)(2,1)S(1)} %get-tuple-element.67), channel_id=1, source_target_pairs={{0,2},{1,3},{2,0},{3,1},{4,6},{5,7},{6,4},{7,5},{8,10},{9,11},{10,... | collective-permute-start | bytes 786440 | tf_op jit(solution)/shard_map/R2_/ppermute | solution.py:57
  77.0 1.6 %copy-start.4 = (bf16[2048,512]{1,0:T(8,128)(2,1)S(1)}, bf16[2048,512]{1,0:T(8,128)(2,1)}, u32[]{:S(2)}) copy-start(bf16[2048,512]{1,0:T(8,128)(2,1)} %constant.107.clone.refs_4_) | copy-start | bytes 6291460
  83.1 2.3 %collective-permute-start.25 = (bf16[1,256,512]{2,1,0:T(8,128)(2,1)S(1)}, bf16[1,256,512]{2,1,0:T(8,128)(2,1)S(1)}, u32[]{:S(2)}, u32[]{:S(2)}) collective-permute-start(bf16[1,256,512]{2,1,0:T(8,128)(2,1)S(1)} %get-tuple-element.68), channel_id=1, source_target_pairs={{0,1},{1,0},{2,3},{3,2},{4,5},{5,4},{6,7},{7,6},{8,9},{9,8},{10,11... | collective-permute-start | bytes 786440 | tf_op jit(solution)/shard_map/H2_/ppermute | solution.py:57
  84.3 1.5 %collective-permute-start.26 = (bf16[1,256,512]{2,1,0:T(8,128)(2,1)S(1)}, bf16[1,256,512]{2,1,0:T(8,128)(2,1)S(1)}, u32[]{:S(2)}, u32[]{:S(2)}) collective-permute-start(bf16[1,256,512]{2,1,0:T(8,128)(2,1)S(1)} %collective-permute-done.22), channel_id=1, source_target_pairs={{0,1},{1,0},{2,3},{3,2},{4,5},{5,4},{6,7},{7,6},{8,9},{9,8},{10,11... | collective-permute-start | bytes 786440 | tf_op jit(solution)/shard_map/F2_/ppermute | solution.py:57
  84.3 7.9 %collective-permute-start.27 = (bf16[1,256,512]{2,1,0:T(8,128)(2,1)S(1)}, bf16[1,256,512]{2,1,0:T(8,128)(2,1)S(1)}, u32[]{:S(2)}, u32[]{:S(2)}) collective-permute-start(bf16[1,256,512]{2,1,0:T(8,128)(2,1)S(1)} %cross_stack.8), channel_id=1, source_target_pairs={{0,2},{1,3},{2,0},{3,1},{4,6},{5,7},{6,4},{7,5},{8,10},{9,11},{10,... | collective-permute-start | bytes 786440 | tf_op jit(solution)/shard_map/R3_/ppermute | solution.py:57
  91.7 1.6 %collective-permute-start.28 = (bf16[1,256,512]{2,1,0:T(8,128)(2,1)S(1)}, bf16[1,256,512]{2,1,0:T(8,128)(2,1)S(1)}, u32[]{:S(2)}, u32[]{:S(2)}) collective-permute-start(bf16[1,256,512]{2,1,0:T(8,128)(2,1)S(1)} %cross_stack.9), channel_id=1, source_target_pairs={{0,1},{1,0},{2,3},{3,2},{4,5},{5,4},{6,7},{7,6},{8,9},{9,8},{10,11... | collective-permute-start | bytes 786440 | tf_op jit(solution)/shard_map/H3_/ppermute | solution.py:57
  92.2 2.0 %collective-permute-start.29 = (bf16[1,256,512]{2,1,0:T(8,128)(2,1)S(1)}, bf16[1,256,512]{2,1,0:T(8,128)(2,1)S(1)}, u32[]{:S(2)}, u32[]{:S(2)}) collective-permute-start(bf16[1,256,512]{2,1,0:T(8,128)(2,1)S(1)} %collective-permute-done.27), channel_id=1, source_target_pairs={{0,1},{1,0},{2,3},{3,2},{4,5},{5,4},{6,7},{7,6},{8,9},{9,8},{10,11... | collective-permute-start | bytes 786440 | tf_op jit(solution)/shard_map/F3_/ppermute | solution.py:57
